TPU v7x, 128 devices: a whole 4x4x4 slice. The times are simulated.
128 devices in a mesh: seq: 8 (over x, core), chan: 16 (over y, z).
Axes of the slice: x: 4, y: 4, z: 4, core: 2. Of those that a mesh axis runs over, the one named last changes fastest.
Arguments:
- query_proj: bfloat16 [16384, 8192], P('seq', 'chan'), may hold values from -6 to 6
- key_proj: bfloat16 [16384, 8192], P('seq', 'chan'), may hold values from -6 to 6
- value_proj: bfloat16 [16384, 8192], P('seq', 'chan'), may hold values from -6 to 6
- pole_rate: float32 [16, 8192], P(None, 'chan'), may hold values from 1.2207031e-05 to 0.0333333333
- pole_residue: float32 [16, 8192], P(None, 'chan'), may hold values from -0.3 to 0.3
- skip_gain: float32 [8192], P('chan'), may hold values from 0.5 to 1.5
- out_weight: bfloat16 [8192, 8192], P('chan'), may hold values from -0.0625 to 0.0625
Outputs:
- layer_out: bfloat16 [16384, 8192], P(('seq', 'chan'))
All inputs are finite; a program needn't handle non-finite values.
Results may differ from a plain program's by a relative error of at most 0.02.
Values may be sent and summed in bfloat16 or wider, within the bound.
No kernel may reach another device: no remote copies, remote signals or barrier semaphores. Data moves between devices by JAX's collectives and lax.ppermute only.
A program may use at most 192 MiB of HBM per device.

v0:
```python
import math

import jax
import jax.numpy as jnp
from jax import lax
from jax.sharding import PartitionSpec as P


def for_sending(value):

    def short(part):
        return part.astype(jnp.bfloat16) if part.dtype == jnp.float32 else part

    return jax.tree.map(short, value)


def from_behind(value, axis, by):
    devices = lax.axis_size(axis)
    pairs = [(i, i + by) for i in range(devices) if 0 <= i + by < devices]
    return lax.ppermute(value, axis, pairs)


def local(query_proj, key_proj, value_proj, pole_rate, pole_residue, skip_gain, out_weight):
    highest = lax.Precision.HIGHEST
    rows, width = key_proj.shape
    block = math.gcd(rows, 128)
    nblocks = rows // block
    drive = key_proj.astype(jnp.float32) * value_proj.astype(jnp.float32)
    offsets = jnp.arange(block, dtype=jnp.float32)
    decay = jnp.exp(-pole_rate[None] * offsets[:, None, None])
    impulse = jnp.sum(pole_residue[None] * decay, axis=1)
    lag = jnp.arange(block)[:, None] - jnp.arange(block)[None, :]
    toeplitz = jnp.where((lag >= 0)[:, :, None], impulse[jnp.maximum(lag, 0)], 0.0)
    blocked = drive.reshape(nblocks, block, width)
    inner = jnp.einsum("tsc,bsc->btc", toeplitz, blocked, precision=highest)
    tail_decay = jnp.exp(-pole_rate[None] * (block - 1.0 - offsets)[:, None, None])
    block_state = jnp.einsum("src,bsc->brc", tail_decay, blocked, precision=highest)
    block_index = jnp.arange(nblocks, dtype=jnp.float32)
    block_gap = block_index[:, None] - 1.0 - block_index[None, :]
    mix_weight = jnp.where(
        (block_gap >= 0)[:, :, None, None],
        jnp.exp(-pole_rate[None, None] * block * jnp.maximum(block_gap, 0.0)[:, :, None, None]),
        0.0,
    )
    within = jnp.sum(mix_weight * block_state[None], axis=1)
    span_state = jnp.sum(
        jnp.exp(-pole_rate[None] * block * (nblocks - 1.0 - block_index)[:, None, None])
        * block_state,
        axis=0,
    )
    whole_decay = jnp.exp(-pole_rate * rows)
    incoming = jnp.zeros_like(span_state)
    for turn in range(lax.axis_size("seq") - 1):
        incoming = from_behind(for_sending(whole_decay * incoming + span_state), "seq", 1)
    carried = (
        within + jnp.exp(-pole_rate[None] * block * block_index[:, None, None]) * incoming[None]
    )
    lead = pole_residue[None] * jnp.exp(-pole_rate[None] * (offsets + 1.0)[:, None, None])
    outer = jnp.einsum("trc,brc->btc", lead, carried, precision=highest)
    conv = (inner + outer).reshape(rows, width)
    mixed = (query_proj.astype(jnp.float32) * (conv + skip_gain[None, :] * drive)).astype(
        jnp.bfloat16
    )
    return lax.psum_scatter(
        jnp.dot(mixed, out_weight, preferred_element_type=jnp.float32).astype(jnp.bfloat16),
        "chan",
        scatter_dimension=0,
        tiled=True,
    )


def solution(mesh):
    in_specs = (
        P("seq", "chan"),
        P("seq", "chan"),
        P("seq", "chan"),
        P(None, "chan"),
        P(None, "chan"),
        P("chan"),
        P("chan", None),
    )
    out_specs = P(("seq", "chan"), None)
    return jax.shard_map(local, mesh=mesh, in_specs=in_specs, out_specs=out_specs, check_vma=False)
```

profile of v0, /device:TPU:1, one launch (start us, length us, event | category | flops | bytes accessed | tf_op | source)
XLA Modules:
  0.0 475.3 jit_solution(5932715720665761258)
XLA Ops:
  6.6 4.8 %convert_multiply_fusion = f32[2048,512]{1,0:T(8,128)} fusion(bf16[2048,512]{1,0:T(8,128)(2,1)} %param.9, bf16[2048,512]{1,0:T(8,128)(2,1)} %param.8), kind=kLoop, calls=%fused_computation.25 | loop fusion | flops 3145728 | bytes 8388608 | tf_op jit(solution)/shard_map/mul | solution.py:28
  11.3 5.4 %copy.49 = f32[16,128,512]{1,0,2:T(8,128)} copy(f32[16,128,512]{2,1,0:T(8,128)} %bitcast.20) | data formatting | bytes 8388608 | tf_op jit(solution)/shard_map/reshape | solution.py:34
  16.8 0.1 copy.46
  16.9 0.1 copy.52
  17.1 11.6 %multiply_reduce_fusion.1 = (f32[16,512]{0,1:T(8,128)S(1)}, f32[16,16,512]{1,0,2:T(8,128)}) fusion(f32[16]{0:T(128)S(1)} %iota_subtract_fusion.1, f32[16,512]{0,1:T(8,128)S(1)} %copy.52, f32[16,128,512]{1,0,2:T(8,128)} %copy.49, f32[128]{0:T(128)S(1)} %iota_subtract_fusion.2, f32[16,512]{0,1:T(8,128)S(1)} %copy.46), kind=kOutput, calls=%fused_computation.17 | convolution fusion | flops 202760192 | bytes 4817472 | tf_op jit(solution)/shard_map/src,bsc->brc/dot_general | solution.py:37
  28.6 0.1 copy.53
  28.8 4.5 collective-permute-start
  33.3 0.1 copy.45
  33.4 6.0 %multiply_reduce_fusion.2 = f32[128,512]{0,1:T(8,128)S(1)} fusion(f32[16,512]{0,1:T(8,128)S(1)} %copy.46, f32[16,512]{0,1:T(8,128)S(1)} %copy.45), kind=kLoop, calls=%fused_computation.24 | loop fusion | flops 3080192 | bytes 327680 | tf_op jit(solution)/shard_map/reduce_sum | solution.py:31
  39.4 0.1 copy.47
  39.6 64.3 %gather_fusion = f32[16384,512]{1,0:T(8,128)} fusion(f32[128,512]{1,0:T(8,128)S(1)} %copy.47, s32[16384]{0:T(1024)S(1)} %bitcast_clamp_fusion), kind=kCustom, calls=%fused_computation | custom fusion | bytes 67174400 | tf_op jit(solution)/shard_map/gather | solution.py:33
  103.9 35.6 %copy.48 = f32[128,128,512]{1,0,2:T(8,128)} copy(f32[128,128,512]{2,1,0:T(8,128)} %bitcast.19) | data formatting | bytes 67108864 | tf_op jit(solution)/shard_map/gather | solution.py:33
  139.5 2.1 collective-permute-start.1
  141.6 57.1 %fusion = f32[512,16,128]{2,1,0:T(8,128)} fusion(f32[16,128,512]{1,0,2:T(8,128)} %copy.49, f32[128,128,512]{1,0,2:T(8,128)} %copy.48, pred[128,128]{1,0:T(8,128)(4,1)S(1)} %subtract_compare_fusion), kind=kOutput, calls=%fused_computation.1 | convolution fusion | flops 1619001344 | bytes 41959424 | tf_op jit(solution)/shard_map/tsc,bsc->btc/dot_general | solution.py:35
  198.7 3.5 collective-permute-start.2
  202.2 0.8 collective-permute-done.2
  203.1 4.2 collective-permute-start.3
  207.3 0.1 fusion.32
  207.3 0.8 collective-permute-done.3
  208.1 4.2 collective-permute-start.4
  212.3 0.1 fusion.33
  212.4 2.8 copy.51
  215.3 2.2 collective-permute-start.5
  217.4 2.1 multiply_reduce_fusion
  219.6 3.2 collective-permute-start.6
  222.8 3.6 copy.61
  226.4 0.1 copy.60
  226.5 9.4 %add_bitcast_fusion = f32[16,128,512]{1,0,2:T(8,128)} fusion(f32[512,16,128]{2,1,0:T(8,128)} %fusion, f32[128]{0:T(128)S(1)} %iota_add_fusion, f32[16,16,512]{1,0,2:T(8,128)} %copy.61, f32[16,512]{0,1:T(8,128)S(1)} %copy.60, f32[16,512]{0,1:T(8,128)S(1)} %copy.52, f32[16,512]{0,1:T(8,128)S(1)} %copy.46, f32[16,512]{0,1:T(8,128)S(1)} %copy.45), kind=kOutput, calls=%fused_computation.10 | convolution fusion | flops 204865536 | bytes 9044480 | tf_op jit(solution)/shard_map/trc,brc->btc/dot_general | solution.py:59
  236.0 5.5 %copy.63 = f32[16,128,512]{2,1,0:T(8,128)} copy(f32[16,128,512]{1,0,2:T(8,128)} %add_bitcast_fusion) | data formatting | bytes 8388608 | tf_op jit(solution)/shard_map/reshape | solution.py:60
  241.5 6.0 %fusion.5 = bf16[2048,512]{1,0:T(8,128)(2,1)} fusion(f32[16,128,512]{2,1,0:T(8,128)} %copy.63, bf16[2048,512]{1,0:T(8,128)(2,1)} %param.7, f32[512]{0:T(512)S(1)} %copy-done.3, bf16[2048,512]{1,0:T(8,128)(2,1)S(1)} %copy-done, bf16[2048,512]{1,0:T(8,128)(2,1)} %param.8), kind=kLoop, calls=%fused_computation.9 | loop fusion | flops 8388608 | bytes 12584960 | tf_op jit(solution)/shard_map/convert_element_type | solution.py:61
  247.4 25.7 %convolution_convert_fusion = bf16[2048,8192]{1,0:T(8,128)(2,1)} fusion(bf16[2048,512]{1,0:T(8,128)(2,1)} %fusion.5, bf16[512,8192]{1,0:T(8,128)(2,1)} %param.13), kind=kOutput, calls=%fused_computation.3 | convolution fusion | flops 17196646400 | bytes 44040192 | tf_op jit(solution)/shard_map/dot_general | solution.py:65
  273.1 195.3 %reduce-scatter.2.cloned.1.call-done = bf16[128,8192]{1,0:T(8,128)(2,1)} async-done(((bf16[2048,8192]{1,0:T(8,128)(2,1)}), bf16[128,8192]{1,0:T(8,128)(2,1)}) %reduce-scatter.2.cloned.1.call-update) | async-done | bytes 2097168 | tf_op jit(solution)/shard_map/reduce_scatter | solution.py:64
  (29 shorter events, 0.2 us)
Async XLA Ops:
  6.5 461.9 %reduce-scatter.2.cloned.1.call-start = ((), (), s32[]{:S(2)}) async-start(), calls=%async_computation.1 | async-start | bytes 35651584 | tf_op jit(solution)/shard_map/reduce_scatter | solution.py:64
  11.3 5.4 %copy-start.1 = (f32[16,512]{1,0:T(8,128)S(1)}, f32[16,512]{1,0:T(8,128)}, u32[]{:S(2)}) copy-start(f32[16,512]{1,0:T(8,128)} %param.10) | copy-start | bytes 98308
  17.1 16.2 %copy-start.2 = (f32[16,512]{1,0:T(8,128)S(1)}, f32[16,512]{1,0:T(8,128)}, u32[]{:S(2)}) copy-start(f32[16,512]{1,0:T(8,128)} %param.11) | copy-start | bytes 98308
  28.8 110.7 %collective-permute-start = (bf16[16,512]{1,0:T(8,128)(2,1)S(1)}, bf16[16,512]{1,0:T(8,128)(2,1)S(1)}, u32[]{:S(2)}, u32[]{:S(2)}) collective-permute-start(bf16[16,512]{1,0:T(8,128)(2,1)S(1)} %add_convert_fusion.6), channel_id=1, source_target_pairs={{0,16},{16,32},{32,48},{48,64},{64,80},{80,96},{96,112},{1,17},{17... | collective-permute-start | bytes 49160 | tf_op jit(solution)/shard_map/ppermute | solution.py:20
  139.5 59.2 %collective-permute-start.1 = (bf16[16,512]{1,0:T(8,128)(2,1)S(1)}, bf16[16,512]{1,0:T(8,128)(2,1)S(1)}, u32[]{:S(2)}, u32[]{:S(2)}) collective-permute-start(bf16[16,512]{1,0:T(8,128)(2,1)S(1)} %add_convert_fusion.5), channel_id=1, source_target_pairs={{0,16},{16,32},{32,48},{48,64},{64,80},{80,96},{96,112},{1,17},{17... | collective-permute-start | bytes 49160 | tf_op jit(solution)/shard_map/ppermute | solution.py:20
  198.7 4.4 collective-permute-start.2
  203.1 5.1 %collective-permute-start.3 = (bf16[16,512]{1,0:T(8,128)(2,1)S(1)}, bf16[16,512]{1,0:T(8,128)(2,1)S(1)}, u32[]{:S(2)}, u32[]{:S(2)}) collective-permute-start(bf16[16,512]{1,0:T(8,128)(2,1)S(1)} %add_convert_fusion.3), channel_id=1, source_target_pairs={{0,16},{16,32},{32,48},{48,64},{64,80},{80,96},{96,112},{1,17},{17... | collective-permute-start | bytes 49160 | tf_op jit(solution)/shard_map/ppermute | solution.py:20
  208.1 7.1 %collective-permute-start.4 = (bf16[16,512]{1,0:T(8,128)(2,1)S(1)}, bf16[16,512]{1,0:T(8,128)(2,1)S(1)}, u32[]{:S(2)}, u32[]{:S(2)}) collective-permute-start(bf16[16,512]{1,0:T(8,128)(2,1)S(1)} %add_convert_fusion.2), channel_id=1, source_target_pairs={{0,16},{16,32},{32,48},{48,64},{64,80},{80,96},{96,112},{1,17},{17... | collective-permute-start | bytes 49160 | tf_op jit(solution)/shard_map/ppermute | solution.py:20
  215.3 4.3 collective-permute-start.5
  219.6 6.8 %collective-permute-start.6 = (bf16[16,512]{1,0:T(8,128)(2,1)S(1)}, bf16[16,512]{1,0:T(8,128)(2,1)S(1)}, u32[]{:S(2)}, u32[]{:S(2)}) collective-permute-start(bf16[16,512]{1,0:T(8,128)(2,1)S(1)} %add_convert_fusion), channel_id=1, source_target_pairs={{0,16},{16,32},{32,48},{48,64},{64,80},{80,96},{96,112},{1,17},{17... | collective-permute-start | bytes 49160 | tf_op jit(solution)/shard_map/ppermute | solution.py:20
  236.0 5.5 %copy-start = (bf16[2048,512]{1,0:T(8,128)(2,1)S(1)}, bf16[2048,512]{1,0:T(8,128)(2,1)}, u32[]{:S(2)}) copy-start(bf16[2048,512]{1,0:T(8,128)(2,1)} %param.9) | copy-start | bytes 6291460
  236.0 5.5 %copy-start.3 = (f32[512]{0:T(512)S(1)}, f32[512]{0:T(512)}, u32[]{:S(2)}) copy-start(f32[512]{0:T(512)} %param.12) | copy-start | bytes 6148
Sparse Core Ops, SparseCore 0:
  273.3 195.1 reduce-scatter.1
where the time goes:
time: 476 us; the launch traced here: 475 us
  waiting for transfers between devices  197 us (41%)
  local copies, waits for them, and re-layouts  118 us (25%)
  matrix products  104 us (22%)
  starting transfers between devices  23.9 us (5%)
  other arithmetic  19.2 us (4%)
  between operations  13.6 us (3%)
    reduce_scatter x1, waiting for transfers between devices, local(): lax.psum_scatter(jnp.dot(mixed, out_weight, preferred_element_type=jnp.fl...  195 us
    gather x2, local copies, waits for them, and re-layouts, local(): impulse[jnp.maximum(lag, 0)]  99.9 us
    dot_general x1, matrix products, local(): inner = jnp.einsum('tsc,bsc->btc', toeplitz, blocked, precision=highest)  57.1 us
    dot_general x1, matrix products, local(): jnp.dot(mixed, out_weight, preferred_element_type=jnp.float32)  25.7 us
    ppermute x7, starting transfers between devices, from_behind(): return lax.ppermute(value, axis, pairs)  23.9 us
    dot_general x1, matrix products, local(): jnp.einsum('src,bsc->brc', tail_decay, blocked, precision=highest)  11.6 us
  transfers between devices with their start and end apart: 8, of which 3 were waited for; matrix products, arithmetic and copies ran while one was open for 36% of the time, Pallas kernels for 0%

commit v1 on v0

v1 whole, which is shorter than its diff:
```python
import functools
import jax, jax.numpy as jnp
from jax import lax
from jax.experimental import pallas as pl
from jax.experimental.pallas import tpu as pltpu
from jax.sharding import PartitionSpec as P
POLES=16

def state_kernel(k_ref, v_ref, rate_ref, excl_ref, span_ref, drive, fb, *, T, unroll):
    W = k_ref.shape[-1]
    nO = k_ref.shape[0]
    drive[...] = (k_ref[...].astype(jnp.float32) * v_ref[...].astype(jnp.float32)).reshape(nO*T, W)
    rate = rate_ref[...]
    f = jnp.exp(-rate)
    for r in range(POLES):
        fb[r] = jnp.broadcast_to(f[r:r+1], (8, W))
    oid = lax.broadcasted_iota(jnp.int32, (8, W), 0)
    prev = None
    fT = jnp.exp(-rate * T)
    finals = []
    for p in range(nO//8):
        def body(i, s):
            s = list(s)
            for j in range(unroll):
                u = drive[pl.ds(p*8*T + i*unroll + j, 8, stride=T), :]
                for r in range(POLES):
                    s[r] = fb[r]*s[r] + u
            return tuple(s)
        s = lax.fori_loop(0, T//unroll, body, tuple(jnp.zeros((8,W),jnp.float32) for _ in range(POLES)))
        finals.append(s)
    spans=[]
    for r in range(POLES):
        carry = jnp.zeros((1,W),jnp.float32)
        g = fT[r:r+1]
        g2 = g*g; g4 = g2*g2; g8 = g4*g4
        pw = jnp.ones((8,W),jnp.float32)
        pw = jnp.where((oid & 1)!=0, pw*g, pw)
        pw = jnp.where((oid & 2)!=0, pw*g2, pw)
        pw = jnp.where((oid & 4)!=0, pw*g4, pw)
        for p in range(nO//8):
            s = finals[p][r]
            for d, gd in ((1,g),(2,g2),(4,g4)):
                s = s + jnp.where(oid>=d, pltpu.roll(s, d, 0), 0.0)*gd
            ex = jnp.where(oid>=1, pltpu.roll(s,1,0), 0.0) + pw*carry
            excl_ref[r, pl.ds(p*8,8), :] = ex
            carry = s[7:8] + g8*carry
        spans.append(carry)
    span_ref[...] = jnp.concatenate(spans, axis=0)

def states(k3, v3, rate, unroll=4):
    nO,T,C = k3.shape
    W=128
    return pl.pallas_call(
        functools.partial(state_kernel, T=T, unroll=unroll),
        grid=(C//W,),
        in_specs=[pl.BlockSpec((nO,T,W), lambda c:(0,0,c)), pl.BlockSpec((nO,T,W), lambda c:(0,0,c)),
                  pl.BlockSpec((POLES,W), lambda c:(0,c))],
        out_specs=[pl.BlockSpec((POLES,nO,W), lambda c:(0,0,c)), pl.BlockSpec((POLES,W), lambda c:(0,c))],
        out_shape=[jax.ShapeDtypeStruct((POLES,nO,C), jnp.float32), jax.ShapeDtypeStruct((POLES,C), jnp.float32)],
        scratch_shapes=[pltpu.VMEM((nO*T,W), jnp.float32), pltpu.VMEM((POLES,8,W), jnp.float32)],
        name="states",
    )(k3, v3, rate)

def conv_kernel(q_ref, k_ref, v_ref, rate_ref, res_ref, skip_ref, init_ref, out_ref, state_ref, drive, y, fb, rb, *, unroll):
    nO, T, W = k_ref.shape
    drive[...] = (k_ref[...].astype(jnp.float32) * v_ref[...].astype(jnp.float32)).reshape(nO*T, W)
    f = jnp.exp(-rate_ref[...])
    for r in range(POLES):
        fb[r] = jnp.broadcast_to(f[r:r+1], (8, W))
        rb[r] = jnp.broadcast_to(res_ref[r:r+1], (8, W))
    rb[POLES] = jnp.broadcast_to(skip_ref[...], (8, W))
    for p in range(nO//8):
        def body(i, s):
            s = list(s)
            for j in range(unroll):
                t = i*unroll + j
                u = drive[pl.ds(p*8*T + t, 8, stride=T), :]
                acc = [rb[POLES]*u, None, None, None]
                for r in range(POLES):
                    s[r] = fb[r]*s[r] + u
                    m = rb[r]*s[r]
                    acc[r%4] = m if acc[r%4] is None else acc[r%4] + m
                y[pl.ds(p*8*T + t, 8, stride=T), :] = (acc[0]+acc[1])+(acc[2]+acc[3])
            return tuple(s)
        s = lax.fori_loop(0, T//unroll, body, tuple(init_ref[r, pl.ds(p*8,8), :] for r in range(POLES)))
        for r in range(POLES):
            state_ref[r, pl.ds(p*8,8), :] = s[r]
    out_ref[...] = (q_ref[...].astype(jnp.float32) * y[...].reshape(nO,T,W)).astype(jnp.bfloat16)

def conv_chunk(q3,k3,v3,rate,res,skip,init,i,tc,unroll=4):
    nO,T,C = k3.shape
    W=128
    row = pl.BlockSpec((nO,tc,W), lambda c:(0,i,c))
    par = pl.BlockSpec((POLES,W), lambda c:(0,c))
    st = pl.BlockSpec((POLES,nO,W), lambda c:(0,0,c))
    return pl.pallas_call(
        functools.partial(conv_kernel, unroll=unroll),
        grid=(C//W,),
        in_specs=[row,row,row,par,par,pl.BlockSpec((1,W), lambda c:(0,c)),st],
        out_specs=[pl.BlockSpec((nO,tc,W), lambda c:(0,0,c)), st],
        out_shape=[jax.ShapeDtypeStruct((nO,tc,C), jnp.bfloat16), jax.ShapeDtypeStruct((POLES,nO,C), jnp.float32)],
        scratch_shapes=[pltpu.VMEM((nO*tc,W), jnp.float32), pltpu.VMEM((nO*tc,W), jnp.float32), pltpu.VMEM((POLES,8,W), jnp.float32), pltpu.VMEM((POLES+1,8,W), jnp.float32)],
        name="conv",
    )(q3,k3,v3,rate,res,skip.reshape(1,-1),init)


def incoming_state(span, rate, rows):
    devices = lax.axis_size("seq")
    me = lax.axis_index("seq")
    spans = lax.all_gather(span, "seq", axis=0)
    gap = (me - 1 - jnp.arange(devices)).astype(jnp.float32)[:, None, None]
    weight = jnp.where(gap >= 0, jnp.exp(-rate[None] * rows * jnp.maximum(gap, 0.0)), 0.0)
    return jnp.sum(weight * spans, axis=0)


def local(query_proj, key_proj, value_proj, pole_rate, pole_residue, skip_gain, out_weight):
    rows, width = key_proj.shape
    owners = lax.axis_size("chan")
    per = rows // owners
    q3, k3, v3 = [x.reshape(owners, per, width) for x in (query_proj, key_proj, value_proj)]
    excl, span = states(k3, v3, pole_rate)
    incoming = incoming_state(span, pole_rate, rows)
    index = jnp.arange(owners, dtype=jnp.float32)[None, :, None]
    init = excl + jnp.exp(-pole_rate[:, None, :] * per * index) * incoming[:, None, :]
    mixed, _ = conv_chunk(q3, k3, v3, pole_rate, pole_residue, skip_gain, init, 0, per)
    mixed = mixed.reshape(rows, width)
    parts = []
    chunks = 4
    cols = out_weight.shape[1] // chunks
    for j in range(chunks):
        weight = lax.slice_in_dim(out_weight, j * cols, (j + 1) * cols, axis=1)
        partial = jnp.dot(mixed, weight, preferred_element_type=jnp.float32).astype(jnp.bfloat16)
        parts.append(lax.psum_scatter(partial, "chan", scatter_dimension=0, tiled=True))
    return jnp.concatenate(parts, axis=1)


def solution(mesh):
    in_specs = (
        P("seq", "chan"),
        P("seq", "chan"),
        P("seq", "chan"),
        P(None, "chan"),
        P(None, "chan"),
        P("chan"),
        P("chan", None),
    )
    out_specs = P(("seq", "chan"), None)
    return jax.shard_map(local, mesh=mesh, in_specs=in_specs, out_specs=out_specs, check_vma=False)
```

time: 476 us -> 421 us (0.88)
  waiting for transfers between devices: 197 us -> 322 us
  local copies, waits for them, and re-layouts: 118 us -> 1.52 us
  matrix products: 104 us -> 35.1 us
  Pallas kernels: 0 us -> 28 us
  starting transfers between devices: 23.9 us -> 0.13 us
  blocking collectives: 0 us -> 14.7 us
  other arithmetic: 19.2 us -> 5.84 us
    reduce_scatter x1 -> x4, waiting for transfers between devices: 195 us -> 321 us  [local(): lax.psum_scatter(partial, 'chan', scatter_dimension=0, tiled=True)]
    gather x2 -> x0, local copies, waits for them, and re-layouts: 99.9 us -> none  [local(): impulse[jnp.maximum(lag, 0)]]
    dot_general x4, matrix products: 104 us -> 35.1 us  [local(): jnp.dot(mixed, weight, preferred_element_type=jnp.float32)]
    pallas_call x0 -> x2, Pallas kernels: none -> 28 us  [the longest x1 17.2 us: conv_chunk(): pl.pallas_call(functools.partial(conv_kernel, unroll=unroll), grid=(C //...]
    ppermute x7 -> x0, starting transfers between devices: 23.9 us -> none  [from_behind(): return lax.ppermute(value, axis, pairs)]
    all_gather x0 -> x1, blocking collectives: none -> 14.7 us  [incoming_state(): spans = lax.all_gather(span, 'seq', axis=0)]
    reshape x2 -> x0, local copies, waits for them, and re-layouts: 10.9 us -> none  [the longest x1 5.46 us: local(): conv = (inner + outer).reshape(rows, width)]
    reduce_sum x2 -> x1, other arithmetic: 8.1 us -> 0.12 us  [incoming_state(): return jnp.sum(weight * spans, axis=0)]
  transfers between devices with their start and end apart: 8 -> 4, of which waited for: 3 -> 4; matrix products, arithmetic and copies ran while one was open for 36% -> 6% of each run, Pallas kernels for 0% -> 0%
where the time goes in v1:
time: 421 us; the launch traced here: 420 us
  waiting for transfers between devices  322 us (76%)
  matrix products  35.1 us (8%)
  Pallas kernels  28 us (7%)
  blocking collectives  14.7 us (3%)
  between operations  13.1 us (3%)
  other arithmetic  5.84 us (1%)
    reduce_scatter x4, waiting for transfers between devices, local(): lax.psum_scatter(partial, 'chan', scatter_dimension=0, tiled=True)  321 us
    dot_general x4, matrix products, local(): jnp.dot(mixed, weight, preferred_element_type=jnp.float32)  35.1 us
    pallas_call x1, Pallas kernels, conv_chunk(): pl.pallas_call(functools.partial(conv_kernel, unroll=unroll), grid=(C //...  17.2 us
    all_gather x1, blocking collectives, incoming_state(): spans = lax.all_gather(span, 'seq', axis=0)  14.7 us
    pallas_call x1, Pallas kernels, states(): pl.pallas_call(functools.partial(state_kernel, T=T, unroll=unroll), grid=...  10.8 us
  transfers between devices with their start and end apart: 4, of which 4 were waited for; matrix products, arithmetic and copies ran while one was open for 6% of the time, Pallas kernels for 0%

profile of v1, /device:TPU:1, one launch (start us, length us, event | category | flops | bytes accessed | tf_op | source)
XLA Modules:
  0.0 419.9 jit_solution(2864116845985918592)
XLA Ops:
  6.5 0.0 reduce-scatter.11.cloned.1.call-start
  6.6 0.8 negate_multiply_fusion.1
  7.3 10.8 %states.1 = (f32[16,16,512]{2,1,0:T(8,128)}, f32[16,512]{1,0:T(8,128)}) custom-call(bf16[16,128,512]{2,1,0:T(8,128)(2,1)} %bitcast.10, bf16[16,128,512]{2,1,0:T(8,128)(2,1)} %bitcast.12, f32[16,512]{1,0:T(8,128)} %rate_ref.3), custom_call_target="tpu_custom_call" | custom-call | tf_op jit(solution)/shard_map/states/pallas_call | solution.py:53
  18.1 14.7 %all-gather = f32[128,512]{1,0:T(8,128)S(1)} all-gather(f32[16,512]{1,0:T(8,128)} %get-tuple-element.9), channel_id=2, replica_groups=mesh['seq'=8,'chan'=16] {'seq'}, dimensions={0}, use_global_device_ids=true | all-gather | bytes 294912 | tf_op jit(solution)/shard_map/all_gather | solution.py:110
  32.8 0.1 multiply_reduce_fusion
  33.0 1.9 multiply_add_fusion.init_ref
  34.9 17.2 %conv.1 = (bf16[16,128,512]{2,1,0:T(8,128)(2,1)}, f32[16,16,512]{2,1,0:T(8,128)}) custom-call(bf16[16,128,512]{2,1,0:T(8,128)(2,1)} %bitcast.14, bf16[16,128,512]{2,1,0:T(8,128)(2,1)} %bitcast.11, bf16[16,128,512]{2,1,0:T(8,128)(2,1)} %bitcast.13, f32[16,512]{1,0:T(8,128)} %rate_ref.3, f32[16,512]{1,0:T(8,128)} %res_ref.1, f32[1,512]{1,0:T(1,128)} %bitcast.16, ...), custom_call_target="tpu_custom_call" | custom-call | tf_op jit(solution)/shard_map/conv/pallas_call | solution.py:96
  52.0 10.0 %convolution_convert_fusion = bf16[2048,2048]{1,0:T(8,128)(2,1)} fusion(bf16[2048,512]{1,0:T(8,128)(2,1)} %bitcast.17, bf16[512,8192]{1,0:T(8,128)(2,1)} %param.13), kind=kOutput, calls=%fused_computation | convolution fusion | flops 4299161600 | bytes 12582912 | tf_op jit(solution)/shard_map/dot_general | solution.py:132
  62.0 0.0 copy-start
  62.0 0.0 reduce-scatter.11.cloned.1.call-update
  62.0 0.0 reduce-scatter.9.cloned.1.call-start
  62.1 1.5 copy-done
  63.6 8.2 %convolution_convert_fusion.1 = bf16[2048,2048]{1,0:T(8,128)(2,1)} fusion(bf16[2048,512]{1,0:T(8,128)(2,1)S(1)} %bitcast.18, bf16[512,8192]{1,0:T(8,128)(2,1)} %param.13), kind=kOutput, calls=%fused_computation.1 | convolution fusion | flops 4299161600 | bytes 12582912 | tf_op jit(solution)/shard_map/dot_general | solution.py:132
  71.8 0.0 reduce-scatter.9.cloned.1.call-update
  71.8 0.0 reduce-scatter.7.cloned.1.call-start
  71.9 8.6 %convolution_convert_fusion.2 = bf16[2048,2048]{1,0:T(8,128)(2,1)} fusion(bf16[2048,512]{1,0:T(8,128)(2,1)S(1)} %bitcast.19, bf16[512,8192]{1,0:T(8,128)(2,1)} %param.13), kind=kOutput, calls=%fused_computation.2 | convolution fusion | flops 4299161600 | bytes 12582912 | tf_op jit(solution)/shard_map/dot_general | solution.py:132
  80.5 0.0 reduce-scatter.7.cloned.1.call-update
  80.5 0.0 reduce-scatter.5.cloned.1.call-start
  80.6 8.3 %convolution_convert_fusion.3 = bf16[2048,2048]{1,0:T(8,128)(2,1)} fusion(bf16[2048,512]{1,0:T(8,128)(2,1)S(1)} %bitcast.20, bf16[512,8192]{1,0:T(8,128)(2,1)} %param.13), kind=kOutput, calls=%fused_computation.3 | convolution fusion | flops 4299161600 | bytes 12582912 | tf_op jit(solution)/shard_map/dot_general | solution.py:132
  88.8 0.0 reduce-scatter.5.cloned.1.call-update
  88.9 58.6 %reduce-scatter.11.cloned.1.call-done = bf16[128,2048]{1,0:T(8,128)(2,1)} async-done(((bf16[2048,2048]{1,0:T(8,128)(2,1)}), bf16[128,2048]{1,0:T(8,128)(2,1)}) %reduce-scatter.11.cloned.1.call-update) | async-done | bytes 524304 | tf_op jit(solution)/shard_map/reduce_scatter | solution.py:133
  147.4 87.6 %reduce-scatter.9.cloned.1.call-done = bf16[128,2048]{1,0:T(8,128)(2,1)} async-done(((bf16[2048,2048]{1,0:T(8,128)(2,1)}), bf16[128,2048]{1,0:T(8,128)(2,1)}) %reduce-scatter.9.cloned.1.call-update) | async-done | bytes 524304 | tf_op jit(solution)/shard_map/reduce_scatter | solution.py:133
  235.1 87.9 %reduce-scatter.7.cloned.1.call-done = bf16[128,2048]{1,0:T(8,128)(2,1)} async-done(((bf16[2048,2048]{1,0:T(8,128)(2,1)}), bf16[128,2048]{1,0:T(8,128)(2,1)}) %reduce-scatter.7.cloned.1.call-update) | async-done | bytes 524304 | tf_op jit(solution)/shard_map/reduce_scatter | solution.py:133
  322.9 87.4 %reduce-scatter.5.cloned.1.call-done = bf16[128,2048]{1,0:T(8,128)(2,1)} async-done(((bf16[2048,2048]{1,0:T(8,128)(2,1)}), bf16[128,2048]{1,0:T(8,128)(2,1)}) %reduce-scatter.5.cloned.1.call-update) | async-done | bytes 524304 | tf_op jit(solution)/shard_map/reduce_scatter | solution.py:133
  410.4 3.0 pad_maximum_fusion
  (2 shorter events, 0.0 us)
Async XLA Ops:
  6.5 140.9 %reduce-scatter.11.cloned.1.call-start = ((), (), s32[]{:S(2)}) async-start(), calls=%async_computation.7 | async-start | bytes 8912896 | tf_op jit(solution)/shard_map/reduce_scatter | solution.py:133
  62.0 1.6 copy-start
  62.0 173.0 %reduce-scatter.9.cloned.1.call-start = ((), (), s32[]{:S(2)}) async-start(), calls=%async_computation.6 | async-start | bytes 8912896 | tf_op jit(solution)/shard_map/reduce_scatter | solution.py:133
  71.8 251.1 %reduce-scatter.7.cloned.1.call-start = ((), (), s32[]{:S(2)}) async-start(), calls=%async_computation.5 | async-start | bytes 8912896 | tf_op jit(solution)/shard_map/reduce_scatter | solution.py:133
  80.5 329.8 %reduce-scatter.5.cloned.1.call-start = ((), (), s32[]{:S(2)}) async-start(), calls=%async_computation.4 | async-start | bytes 8912896 | tf_op jit(solution)/shard_map/reduce_scatter | solution.py:133
Sparse Core Ops, SparseCore 0:
  62.1 85.2 reduce-scatter.10
  150.8 84.1 reduce-scatter.8
  238.5 84.4 reduce-scatter.6
  326.2 84.1 reduce-scatter.4

commit v2 on v1

v2 whole, which is shorter than its diff:
```python
import functools

import jax
import jax.numpy as jnp
from jax import lax
from jax.experimental import pallas as pl
from jax.experimental.pallas import tpu as pltpu
from jax.sharding import PartitionSpec as P

POLES = 16
LANES = 128
NX, NCORE, NY, NZ = 4, 2, 4, 4
STEPS = (1, -1, 2)
ROW_PARTS = (2, 2, 4)
COL_PARTS = (2, 2, 4)
TILES = (((0,), (0,)), ((1,), (0,)), ((0, 1), (1,)), ((2,), (0, 1)), ((0, 1), (2,)), ((2,), (2,)))
ANY = pl.BlockSpec(memory_space=pl.ANY)
SMEM = pl.BlockSpec(memory_space=pltpu.SMEM)
VMEM = pl.BlockSpec(memory_space=pltpu.VMEM)
LIMIT = pltpu.CompilerParams(vmem_limit_bytes=48 * 1024 * 1024)


def over_y(value, step):
    return lax.ppermute(value, "chan", [(y * NZ + z, (y + step) % NY * NZ + z) for y in range(NY) for z in range(NZ)])


def over_z(value, step):
    return lax.ppermute(value, "chan", [(y * NZ + z, y * NZ + (z + step) % NZ) for y in range(NY) for z in range(NZ)])


def with_partner(value):
    return lax.ppermute(value, "chan", [(y * NZ + z, (y ^ 1) * NZ + z) for y in range(NY) for z in range(NZ)])


def other_core(value):
    return lax.ppermute(value, "seq", [(s, s ^ 1) for s in range(NX * NCORE)])


def from_chip_behind(value, step):
    pairs = [(x * NCORE + c, (x + step) * NCORE + c) for x in range(NX - step) for c in range(NCORE)]
    return lax.ppermute(value, "seq", pairs)


def state_kernel(k_ref, v_ref, rate_ref, excl_ref, span_ref, drive, fb, *, T, unroll):
    W = k_ref.shape[-1]
    nO = k_ref.shape[0]
    drive[...] = (k_ref[...].astype(jnp.float32) * v_ref[...].astype(jnp.float32)).reshape(nO*T, W)
    rate = rate_ref[...]
    f = jnp.exp(-rate)
    for r in range(POLES):
        fb[r] = jnp.broadcast_to(f[r:r+1], (8, W))
    oid = lax.broadcasted_iota(jnp.int32, (8, W), 0)
    prev = None
    fT = jnp.exp(-rate * T)
    finals = []
    G = nO//8
    fr = [fb[r] for r in range(POLES)]
    def body(i, s):
        s = [list(x) for x in s]
        for j in range(unroll):
            for p in range(G):
                u = drive[pl.ds(p*8*T + i*unroll + j, 8, stride=T), :]
                for r in range(POLES):
                    s[p][r] = fr[r]*s[p][r] + u
        return tuple(tuple(x) for x in s)
    finals = lax.fori_loop(0, T//unroll, body, tuple(tuple(jnp.zeros((8,W),jnp.float32) for _ in range(POLES)) for p in range(G)))
    spans=[]
    for r in range(POLES):
        carry = jnp.zeros((1,W),jnp.float32)
        g = fT[r:r+1]
        g2 = g*g; g4 = g2*g2; g8 = g4*g4
        pw = jnp.ones((8,W),jnp.float32)
        pw = jnp.where((oid & 1)!=0, pw*g, pw)
        pw = jnp.where((oid & 2)!=0, pw*g2, pw)
        pw = jnp.where((oid & 4)!=0, pw*g4, pw)
        for p in range(nO//8):
            s = finals[p][r]
            for d, gd in ((1,g),(2,g2),(4,g4)):
                s = s + jnp.where(oid>=d, pltpu.roll(s, d, 0), 0.0)*gd
            ex = jnp.where(oid>=1, pltpu.roll(s,1,0), 0.0) + pw*carry
            excl_ref[r, pl.ds(p*8,8), :] = ex
            carry = s[7:8] + g8*carry
        spans.append(carry)
    span_ref[...] = jnp.concatenate(spans, axis=0)

def states(k3, v3, rate, unroll=4):
    nO,T,C = k3.shape
    W=128
    return pl.pallas_call(
        functools.partial(state_kernel, T=T, unroll=unroll),
        grid=(C//W,),
        in_specs=[pl.BlockSpec((nO,T,W), lambda c:(0,0,c)), pl.BlockSpec((nO,T,W), lambda c:(0,0,c)),
                  pl.BlockSpec((POLES,W), lambda c:(0,c))],
        out_specs=[pl.BlockSpec((POLES,nO,W), lambda c:(0,0,c)), pl.BlockSpec((POLES,W), lambda c:(0,c))],
        out_shape=[jax.ShapeDtypeStruct((POLES,nO,C), jnp.float32), jax.ShapeDtypeStruct((POLES,C), jnp.float32)],
        scratch_shapes=[pltpu.VMEM((nO*T,W), jnp.float32), pltpu.VMEM((POLES,8,W), jnp.float32)],
        name="states",
    )(k3, v3, rate)


def conv_kernel(pos_ref, q_ref, k_ref, v_ref, rate_ref, res_ref, skip_ref, init_ref, *rest, unroll, per, first, last):
    rest = list(rest)
    inc_ref = rest.pop(0) if first else None
    outs = rest[:4]
    state_ref = None if last else rest[4]
    drive, y, fb, rb, mixed = rest[4 if last else 5:]
    nO, T, W = k_ref.shape
    drive[...] = (k_ref[...].astype(jnp.float32) * v_ref[...].astype(jnp.float32)).reshape(nO * T, W)
    rate = rate_ref[...]
    f = jnp.exp(-rate)
    for r in range(POLES):
        fb[r] = jnp.broadcast_to(f[r:r + 1], (8, W))
        rb[r] = jnp.broadcast_to(res_ref[r:r + 1], (8, W))
    rb[POLES] = jnp.broadcast_to(skip_ref[...], (8, W))
    fr = [fb[r] for r in range(POLES)]
    G = nO // 8

    def begin(p, r):
        s = init_ref[r, pl.ds(p * 8, 8), :]
        if first:
            owner = (lax.broadcasted_iota(jnp.int32, (8, W), 0) + p * 8).astype(jnp.float32)
            s = s + jnp.exp(-(rate[r:r + 1] * float(per)) * owner) * inc_ref[r:r + 1]
        return s

    def body(i, s):
        s = [list(x) for x in s]
        for j in range(unroll):
            t = i * unroll + j
            us = [drive[pl.ds(p * 8 * T + t, 8, stride=T), :] for p in range(G)]
            acc = [[rb[POLES] * us[p], None] for p in range(G)]
            for r in range(POLES):
                rr = rb[r]
                for p in range(G):
                    s[p][r] = fr[r] * s[p][r] + us[p]
                    m = rr * s[p][r]
                    acc[p][r % 2] = m if acc[p][r % 2] is None else acc[p][r % 2] + m
            for p in range(G):
                y[pl.ds(p * 8 * T + t, 8, stride=T), :] = acc[p][0] + acc[p][1]
        return tuple(tuple(x) for x in s)

    s = lax.fori_loop(0, T // unroll, body, tuple(tuple(begin(p, r) for r in range(POLES)) for p in range(G)))
    if not last:
        for p in range(G):
            for r in range(POLES):
                state_ref[r, pl.ds(p * 8, 8), :] = s[p][r]
    mixed[...] = (q_ref[...].astype(jnp.float32) * y[...].reshape(nO, T, W)).astype(jnp.bfloat16)
    my_y, my_z = pos_ref[0], pos_ref[1]
    for out_ref, step in zip(outs, (0,) + STEPS):
        half = lax.rem(my_y + step + NY, NY) // 2
        for zr in range(NZ):
            z = lax.rem(my_z + zr, NZ)
            for yl in range(2):
                out_ref[zr, yl] = mixed[half * 8 + yl * NZ + z]


def conv_chunk(pos, q3, k3, v3, rate, res, skip, init, inc, index, tc, last):
    nO, T, C = k3.shape
    W = LANES
    first = inc is not None
    row = pl.BlockSpec((nO, tc, W), lambda c: (0, index, c))
    par = pl.BlockSpec((POLES, W), lambda c: (0, c))
    st = pl.BlockSpec((POLES, nO, W), lambda c: (0, 0, c))
    ops = [pos, q3, k3, v3, rate, res, skip.reshape(1, -1), init]
    specs = [SMEM, row, row, row, par, par, pl.BlockSpec((1, W), lambda c: (0, c)), st]
    if first:
        ops.append(inc)
        specs.append(par)
    out = jax.ShapeDtypeStruct((NZ, 2, tc, C), jnp.bfloat16)
    out_shape = [out] * 4
    out_specs = [pl.BlockSpec((NZ, 2, tc, W), lambda c: (0, 0, 0, c))] * 4
    if not last:
        out_shape = out_shape + [jax.ShapeDtypeStruct((POLES, nO, C), jnp.float32)]
        out_specs = out_specs + [st]
    res = pl.pallas_call(
        functools.partial(conv_kernel, unroll=4, per=T, first=first, last=last),
        grid=(C // W,),
        in_specs=specs,
        out_specs=out_specs,
        out_shape=out_shape,
        scratch_shapes=[
            pltpu.VMEM((nO * tc, W), jnp.float32),
            pltpu.VMEM((nO * tc, W), jnp.float32),
            pltpu.VMEM((POLES, 8, W), jnp.float32),
            pltpu.VMEM((POLES + 1, 8, W), jnp.float32),
            pltpu.VMEM((nO, tc, W), jnp.bfloat16),
        ],
        compiler_params=LIMIT,
        cost_estimate=pl.CostEstimate(flops=nO * tc * C * POLES * 4, bytes_accessed=nO * tc * C * 10, transcendentals=0),
        name="conv",
    )(*ops)
    return res[:4], (None if last else res[4])


def share_kernel(pos_ref, w_ref, *refs, widths, offsets, half_cols):
    n = len(widths) * len(STEPS)
    outs, sems = refs[:n], refs[n]
    copies = []
    for g, (width, offset) in enumerate(zip(widths, offsets)):
        for i, step in enumerate(STEPS):
            half = lax.rem(lax.rem(pos_ref[0] + step + NY, NY), 2)
            col = pl.multiple_of(half * half_cols + offset + pos_ref[2] * width, LANES)
            k = g * len(STEPS) + i
            copies.append(pltpu.make_async_copy(w_ref.at[:, pl.ds(col, width)], outs[k], sems.at[k]))
    for c in copies:
        c.start()
    for c in copies:
        c.wait()


def weight_shares(pos, weight, widths, offsets, half_cols):
    k = weight.shape[0]
    n = len(widths) * len(STEPS)
    out = pl.pallas_call(
        functools.partial(share_kernel, widths=widths, offsets=offsets, half_cols=half_cols),
        in_specs=[SMEM, ANY],
        out_specs=[ANY] * n,
        out_shape=[jax.ShapeDtypeStruct((k, w), weight.dtype) for w in widths for _ in STEPS],
        scratch_shapes=[pltpu.SemaphoreType.DMA((n,))],
        name="weight_shares",
    )(pos, weight)
    return [out[g * len(STEPS):(g + 1) * len(STEPS)] for g in range(len(widths))]


def tile_kernel(pos_ref, w_ref, *refs, row_sizes, cols, offsets, half_cols, block):
    nr, nc = len(row_sizes), len(cols)
    a_refs, b_refs = refs[:4 * nr], refs[4 * nr:4 * nr + nc]
    outs = refs[4 * nr + nc:4 * nr + nc + NZ]
    a_v, b_v, sem_a, sem_b, sem_w = refs[4 * nr + nc + NZ:]
    width = w_ref.shape[0]
    total = sum(row_sizes)
    a_copies = []
    start = 0
    for i, tc in enumerate(row_sizes):
        for d in range(4):
            dst = a_v.at[:, :, pl.ds(start, tc), pl.ds(d * width, width)]
            a_copies.append(pltpu.make_async_copy(a_refs[4 * i + d], dst, sem_a.at[4 * i + d]))
        start += tc
    for c in a_copies:
        c.start()
    waits = []
    base = 0
    n = 0
    for g, (size, offset) in enumerate(zip(cols, offsets)):
        piece = size // (NX * NCORE)
        for start in range(0, size, block):
            here = []
            col = pl.multiple_of(lax.rem(pos_ref[0], 2) * half_cols + offset + start, LANES)
            nb = (base + start) // block
            here.append(pltpu.make_async_copy(
                w_ref.at[:, pl.ds(col, block)], b_v.at[pl.ds(0, width), pl.ds(base + start, block)], sem_w.at[nb]))
            for s in range(start // piece, (start + block) // piece):
                here.append(pltpu.make_async_copy(
                    b_refs[g].at[s], b_v.at[pl.ds(width, 3 * width), pl.ds(base + s * piece, piece)], sem_b.at[n]))
                n += 1
            for c in here:
                c.start()
            waits.append(here)
        base += size
    for c in a_copies:
        c.wait()
    a = a_v[...].reshape(NZ * 2 * total, 4 * width)
    for nb, here in enumerate(waits):
        for c in here:
            c.wait()
        at = pl.ds(nb * block, block)
        part = jnp.dot(a, b_v[:, at], preferred_element_type=jnp.float32).astype(jnp.bfloat16)
        part = part.reshape(NZ, 2, total, block)
        for zr in range(NZ):
            outs[zr][:, :, at] = part[zr]


def tile(pos, weight, a_parts, b_parts, cols, offsets, half_cols):
    width = weight.shape[0]
    row_sizes = tuple(a[0].shape[2] for a in a_parts)
    total, n = sum(row_sizes), sum(cols)
    block = 512
    flat = [piece for a in a_parts for piece in a]
    return pl.pallas_call(
        functools.partial(tile_kernel, row_sizes=row_sizes, cols=cols, offsets=offsets, half_cols=half_cols, block=block),
        in_specs=[SMEM, ANY] + [ANY] * (len(flat) + len(b_parts)),
        out_specs=[VMEM] * NZ,
        out_shape=[jax.ShapeDtypeStruct((2, total, n), jnp.bfloat16)] * NZ,
        scratch_shapes=[
            pltpu.VMEM((NZ, 2, total, 4 * width), jnp.bfloat16),
            pltpu.VMEM((4 * width, n), jnp.bfloat16),
            pltpu.SemaphoreType.DMA((len(flat),)),
            pltpu.SemaphoreType.DMA((NX * NCORE * len(cols),)),
            pltpu.SemaphoreType.DMA((n // block,)),
        ],
        compiler_params=LIMIT,
        cost_estimate=pl.CostEstimate(
            flops=2 * NZ * 2 * total * 4 * width * n, bytes_accessed=4 * width * n * 2 + NZ * 2 * total * n * 4, transcendentals=0),
        name="tile",
    )(pos, weight, *flat, *b_parts)


def place_kernel(pos_ref, *refs, places, half_cols):
    n = len(places)
    ins, out, sems = refs[:n], refs[n], refs[n + 1]
    copies = []
    for i, (other, row, rows, col, cols) in enumerate(places):
        half = lax.rem(pos_ref[0] + other, 2)
        at = pl.multiple_of(half * half_cols + col, LANES)
        copies.append(pltpu.make_async_copy(ins[i], out.at[pl.ds(row, rows), pl.ds(at, cols)], sems.at[i]))
    for c in copies:
        c.start()
    for c in copies:
        c.wait()


def local(query_proj, key_proj, value_proj, pole_rate, pole_residue, skip_gain, out_weight):
    rows, width = key_proj.shape
    owners = NY * NZ
    per = rows // owners
    total_cols = out_weight.shape[1]
    half_cols = total_cols // 2
    seq, chan = lax.axis_index("seq"), lax.axis_index("chan")
    my_y, my_z, core = chan // NZ, chan % NZ, seq % NCORE
    pos = jnp.stack([my_y, my_z, seq]).astype(jnp.int32)
    unit = per // sum(ROW_PARTS)
    tcs = [unit * n for n in ROW_PARTS]
    unit = half_cols // sum(COL_PARTS)
    cols = [unit * n for n in COL_PARTS]
    offsets = [sum(cols[:g]) for g in range(len(cols))]

    shares = weight_shares(pos, out_weight, [c // (NX * NCORE) for c in cols], offsets, half_cols)
    weights = []
    for group in shares:
        got = jnp.concatenate([over_y(piece, step) for piece, step in zip(group, STEPS)], axis=0)
        weights.append(lax.all_gather(got, "seq", axis=0))

    q3, k3, v3 = [x.reshape(owners, per, width) for x in (query_proj, key_proj, value_proj)]
    excl, span = states(k3, v3, pole_rate)
    across = jnp.exp(-pole_rate * rows)
    across2 = jnp.exp(-pole_rate * (2.0 * rows))
    across4 = jnp.exp(-pole_rate * (4.0 * rows))
    theirs = other_core(span)
    chip = jnp.where(core == 0, across * span + theirs, across * theirs + span)
    behind = from_chip_behind(chip, 1) + across2 * from_chip_behind(chip, 2) + across4 * from_chip_behind(chip, 3)
    incoming = jnp.where(core == 0, behind, across * behind + theirs)

    mixed = []
    state, start = excl, 0
    for i, tc in enumerate(tcs):
        sent, state = conv_chunk(
            pos, q3, k3, v3, pole_rate, pole_residue, skip_gain, state, incoming if i == 0 else None,
            start // tc, tc, i == len(tcs) - 1)
        mixed.append([sent[0]] + [over_y(piece, step) for piece, step in zip(sent[1:], STEPS)])
        start += tc

    pieces, places = [], []
    parity = my_y % 2
    for row_set, col_set in TILES:
        part = tile(
            pos, out_weight, [mixed[i] for i in row_set], [weights[g] for g in col_set],
            tuple(cols[g] for g in col_set), tuple(offsets[g] for g in col_set), half_cols)
        arrived = [part[0]] + [over_z(part[step % NZ], step) for step in STEPS]
        summed = sum(p.astype(jnp.float32) for p in arrived).astype(jnp.bfloat16)
        keep = lax.dynamic_index_in_dim(summed, parity, 0, keepdims=False)
        send = lax.dynamic_index_in_dim(summed, 1 - parity, 0, keepdims=False)
        row = sum(tcs[:row_set[0]])
        size = sum(tcs[i] for i in row_set)
        col = offsets[col_set[0]]
        n = sum(cols[g] for g in col_set)
        pieces += [keep, with_partner(send)]
        places += [(0, row, size, col, n), (1, row, size, col, n)]
    return pl.pallas_call(
        functools.partial(place_kernel, places=tuple(places), half_cols=half_cols),
        in_specs=[SMEM] + [ANY] * len(pieces),
        out_specs=ANY,
        out_shape=jax.ShapeDtypeStruct((per, total_cols), jnp.bfloat16),
        scratch_shapes=[pltpu.SemaphoreType.DMA((len(pieces),))],
        name="place",
    )(pos, *pieces)


def solution(mesh):
    in_specs = (
        P("seq", "chan"),
        P("seq", "chan"),
        P("seq", "chan"),
        P(None, "chan"),
        P(None, "chan"),
        P("chan"),
        P("chan", None),
    )
    out_specs = P(("seq", "chan"), None)
    return jax.shard_map(local, mesh=mesh, in_specs=in_specs, out_specs=out_specs, check_vma=False)
```

time: 421 us -> 379 us (0.900)
  waiting for transfers between devices: 322 us -> 86.6 us
  Pallas kernels: 28 us -> 186 us
  starting transfers between devices: 0.13 us -> 61.3 us
  matrix products: 35.1 us -> 0 us
  local copies, waits for them, and re-layouts: 1.52 us -> 22.7 us
  blocking collectives: 14.7 us -> 0 us
    reduce_scatter x4 -> x0, waiting for transfers between devices: 321 us -> none  [local(): lax.psum_scatter(partial, 'chan', scatter_dimension=0, tiled=True)]
    pallas_call x1 -> x11, Pallas kernels: 17.2 us -> 175 us  [the longest x1 65.4 us: local(): pl.pallas_call(functools.partial(place_kernel, places=tuple(places), half...]
    ppermute x0 -> x46, waiting for transfers between devices: none -> 86.5 us  [the longest x18 54.1 us: over_z(): lax.ppermute(value, 'chan', [(y * NZ + z, y * NZ + (z + step) % NZ) for y...]
    ppermute x0 -> x46, starting transfers between devices: none -> 61.2 us  [the longest x18 24.8 us: over_z(): lax.ppermute(value, 'chan', [(y * NZ + z, y * NZ + (z + step) % NZ) for y...]
    dot_general x4 -> x0, matrix products: 35.1 us -> none  [local(): jnp.dot(mixed, weight, preferred_element_type=jnp.float32)]
    unnamed x2 -> x100, local copies, waits for them, and re-layouts: 1.52 us -> 18.4 us
    all_gather x1 -> x0, blocking collectives: 14.7 us -> none  [incoming_state(): spans = lax.all_gather(span, 'seq', axis=0)]
    squeeze x0 -> x6, local copies, waits for them, and re-layouts: none -> 4.23 us  [local(): send = lax.dynamic_index_in_dim(summed, 1 - parity, 0, keepdims=False)]
  transfers between devices with their start and end apart: 4 -> 49, of which waited for: 4 -> 20; matrix products, arithmetic and copies ran while one was open for 6% -> 3% of each run, Pallas kernels for 0% -> 19%
where the time goes in v2:
time: 379 us; the launch traced here: 377 us
  Pallas kernels  186 us (49%)
  waiting for transfers between devices  86.6 us (23%)
  starting transfers between devices  61.3 us (16%)
  local copies, waits for them, and re-layouts  22.7 us (6%)
  between operations  13.7 us (4%)
  other arithmetic  6.85 us (2%)
    pallas_call x1, Pallas kernels, local(): pl.pallas_call(functools.partial(place_kernel, places=tuple(places), half...  65.4 us
    ppermute x18, waiting for transfers between devices, over_z(): lax.ppermute(value, 'chan', [(y * NZ + z, y * NZ + (z + step) % NZ) for y...  54.1 us
    pallas_call x1, Pallas kernels, weight_shares(): pl.pallas_call(functools.partial(share_kernel, widths=widths, offsets=off...  49.5 us
    pallas_call x6, Pallas kernels, tile(): pl.pallas_call(functools.partial(tile_kernel, row_sizes=row_sizes, cols=c...  39.3 us
    ppermute x18, starting transfers between devices, over_z(): lax.ppermute(value, 'chan', [(y * NZ + z, y * NZ + (z + step) % NZ) for y...  24.8 us
    ppermute x18, starting transfers between devices, over_y(): lax.ppermute(value, 'chan', [(y * NZ + z, (y + step) % NY * NZ + z) for y...  24.6 us
    ppermute x18, waiting for transfers between devices, over_y(): lax.ppermute(value, 'chan', [(y * NZ + z, (y + step) % NY * NZ + z) for y...  22 us
    pallas_call x3, Pallas kernels, conv_chunk(): pl.pallas_call(functools.partial(conv_kernel, unroll=4, per=T, first=firs...  20.9 us
  transfers between devices with their start and end apart: 49, of which 20 were waited for; matrix products, arithmetic and copies ran while one was open for 3% of the time, Pallas kernels for 19%

profile of v2, /device:TPU:1, one launch (start us, length us, event | category | flops | bytes accessed | tf_op | source)
XLA Modules:
  0.0 376.9 jit_solution(11005730713085681382)
XLA Ops:
  7.2 49.5 %weight_shares.1 = (bf16[512,128]{1,0:T(8,128)(2,1)}, bf16[512,128]{1,0:T(8,128)(2,1)}, bf16[512,128]{1,0:T(8,128)(2,1)}, bf16[512,128]{1,0:T(8,128)(2,1)}, bf16...) custom-call(s32[3]{0:T(128)} %pad_add_fusion.pos_ref, ...), custom_call_target="tpu_custom_call" | custom-call | tf_op jit(solution)/shard_map/weight_shares/pallas_call | solution.py:213
  56.7 3.8 %collective-permute-start.9 = (bf16[512,128]{1,0:T(8,128)(2,1)}, bf16[512,128]{1,0:T(8,128)(2,1)S(1)}, u32[]{:S(2)}, u32[]{:S(2)}) collective-permute-start(bf16[512,128]{1,0:T(8,128)(2,1)} %get-tuple-element.62), channel_id=1, source_target_pairs={{0,8},{1,9},{2,10},{3,11},{4,12},{5,13},{6,14},{7,15},{8,0},{9,1},... | collective-permute-start | bytes 393224 | tf_op jit(solution)/shard_map/ppermute | solution.py:24
  63.7 3.2 collective-permute-done.8
  67.7 3.3 collective-permute-start.23
  73.6 4.1 %collective-permute-done.22 = bf16[512,128]{1,0:T(8,128)(2,1)S(1)} collective-permute-done((bf16[512,128]{1,0:T(8,128)(2,1)}, bf16[512,128]{1,0:T(8,128)(2,1)S(1)}, u32[]{:S(2)}, u32[]{:S(2)}) %collective-permute-start.22) | collective-permute-done | bytes 131104 | tf_op jit(solution)/shard_map/ppermute | solution.py:24
  83.0 4.1 %collective-permute-done.37 = bf16[512,256]{1,0:T(8,128)(2,1)S(1)} collective-permute-done((bf16[512,256]{1,0:T(8,128)(2,1)S(1)}, bf16[512,256]{1,0:T(8,128)(2,1)S(1)}, u32[]{:S(2)}, u32[]{:S(2)}) %collective-permute-start.37) | collective-permute-done | bytes 262176 | tf_op jit(solution)/shard_map/ppermute | solution.py:24
  87.1 7.0 %collective-permute-done.36 = bf16[512,256]{1,0:T(8,128)(2,1)S(1)} collective-permute-done((bf16[512,256]{1,0:T(8,128)(2,1)S(1)}, bf16[512,256]{1,0:T(8,128)(2,1)S(1)}, u32[]{:S(2)}, u32[]{:S(2)}) %collective-permute-start.36) | collective-permute-done | bytes 262176 | tf_op jit(solution)/shard_map/ppermute | solution.py:24
  95.2 10.6 %states.1 = (f32[16,16,512]{2,1,0:T(8,128)}, f32[16,512]{1,0:T(8,128)}) custom-call(bf16[16,128,512]{2,1,0:T(8,128)(2,1)} %bitcast.43, bf16[16,128,512]{2,1,0:T(8,128)(2,1)} %bitcast.47, f32[16,512]{1,0:T(8,128)} %rate_ref.7), custom_call_target="tpu_custom_call" | custom-call | tf_op jit(solution)/shard_map/states/pallas_call | solution.py:89
  108.9 4.4 %collective-permute-start.3 = (f32[16,512]{1,0:T(8,128)S(1)}, f32[16,512]{1,0:T(8,128)S(1)}, u32[]{:S(2)}, u32[]{:S(2)}) collective-permute-start(f32[16,512]{1,0:T(8,128)S(1)} %add_select_fusion.1), channel_id=1, source_target_pairs={{0,96},{16,112},{1,97},{17,113},{2,98},{18,114},{3,99},{19,115},{4... | collective-permute-start | bytes 98312 | tf_op jit(solution)/shard_map/ppermute | solution.py:41
  114.6 3.1 collective-permute-start.2
  119.8 5.3 %conv.3 = (bf16[4,2,32,512]{3,2,1,0:T(8,128)(2,1)S(1)}, bf16[4,2,32,512]{3,2,1,0:T(8,128)(2,1)S(1)}, bf16[4,2,32,512]{3,2,1,0:T(8,128)(2,1)S(1)}, bf16[4,2,32,512]{3,2,1,0:T(8,128)(2,1)S(1)}, f32[16,16,512]{2,1,0:T(8,128)S(1)}) custom-call(s32[3]{0:T(128)S(1)} %copy-done.30, bf16[16,128,512]{2,1,0:T(8,128)(2,1)S(1)} %bitcast.37, ...), custom_call_target="tpu_custom_call" | custom-call | flops 16777216 | bytes 2621440 | tf_op jit(solution)/shard_map/conv/pallas_call | solution.py:174
  128.8 5.9 %conv.4 = (bf16[4,2,32,512]{3,2,1,0:T(8,128)(2,1)S(1)}, bf16[4,2,32,512]{3,2,1,0:T(8,128)(2,1)S(1)}, bf16[4,2,32,512]{3,2,1,0:T(8,128)(2,1)}, bf16[4,2,32,512]{3,2,1,0:T(8,128)(2,1)}, f32[16,16,512]{2,1,0:T(8,128)S(1)}) custom-call(s32[3]{0:T(128)S(1)} %copy-done.30, bf16[16,128,512]{2,1,0:T(8,128)(2,1)S(1)} %bitcast.38, bf16[16,128,512]{2,1,0:T(8,128)(2,1)} %bitcast.45, ...), custom_call_target="tpu_custom_call" | custom-call | flops 16777216 | bytes 2621440 | tf_op jit(solution)/shard_map/conv/pallas_call | solution.py:174
  139.0 9.7 %conv.5 = (bf16[4,2,64,512]{3,2,1,0:T(8,128)(2,1)S(1)}, bf16[4,2,64,512]{3,2,1,0:T(8,128)(2,1)}, bf16[4,2,64,512]{3,2,1,0:T(8,128)(2,1)}, bf16[4,2,64,512]{3,2,1,0:T(8,128)(2,1)}) custom-call(s32[3]{0:T(128)S(1)} %copy-done.30, bf16[16,128,512]{2,1,0:T(8,128)(2,1)S(1)} %bitcast.39, bf16[16,128,512]{2,1,0:T(8,128)(2,1)} %bitcast.46, ...), custom_call_target="tpu_custom_call" | custom-call | flops 33554432 | bytes 5242880 | tf_op jit(solution)/shard_map/conv/pallas_call | solution.py:174
  150.9 2.7 collective-permute-start.29
  160.0 4.2 %tile.6 = (bf16[2,32,1024]{2,1,0:T(8,128)(2,1)S(1)}, bf16[2,32,1024]{2,1,0:T(8,128)(2,1)S(1)}, bf16[2,32,1024]{2,1,0:T(8,128)(2,1)}, bf16[2,32,1024]{2,1,0:T(8,128)(2,1)}) custom-call(s32[3]{0:T(128)S(1)} %copy-done.30, bf16[512,8192]{1,0:T(8,128)(2,1)} %w_ref.13, bf16[4,2,32,512]{3,2,1,0:T(8,128)(2,1)S(1)} %get-tuple-element.56.refs_0_, ...), custom_call_target="tpu_custom_call" | custom-call | flops 1073741824 | bytes 5242880 | tf_op jit(solution)/shard_map/tile/pallas_call | solution.py:278
  165.6 4.1 %collective-permute-start.12 = (bf16[2,32,1024]{2,1,0:T(8,128)(2,1)}, bf16[2,32,1024]{2,1,0:T(8,128)(2,1)}, u32[]{:S(2)}, u32[]{:S(2)}) collective-permute-start(bf16[2,32,1024]{2,1,0:T(8,128)(2,1)} %get-tuple-element.66), channel_id=1, source_target_pairs={{0,2},{1,3},{2,0},{3,1},{4,6},{5,7},{6,4},{7,5},{8,10},{9,11},{10,... | collective-permute-start | bytes 393224 | tf_op jit(solution)/shard_map/ppermute | solution.py:28
  170.1 3.3 tile.7
  180.2 5.0 %tile.8 = (bf16[2,64,1024]{2,1,0:T(8,128)(2,1)S(1)}, bf16[2,64,1024]{2,1,0:T(8,128)(2,1)S(1)}, bf16[2,64,1024]{2,1,0:T(8,128)(2,1)S(1)}, bf16[2,64,1024]{2,1,0:T(8,128)(2,1)S(1)}) custom-call(s32[3]{0:T(128)S(1)} %copy-done.30, bf16[512,8192]{1,0:T(8,128)(2,1)} %w_ref.13, bf16[4,2,32,512]{3,2,1,0:T(8,128)(2,1)S(1)} %get-tuple-element.56.refs_0_, ...), custom_call_target="tpu_custom_call" | custom-call | flops 2147483648 | bytes 6291456 | tf_op jit(solution)/shard_map/tile/pallas_call | solution.py:278
  189.3 9.7 %tile.9 = (bf16[2,64,2048]{2,1,0:T(8,128)(2,1)S(1)}, bf16[2,64,2048]{2,1,0:T(8,128)(2,1)S(1)}, bf16[2,64,2048]{2,1,0:T(8,128)(2,1)S(1)}, bf16[2,64,2048]{2,1,0:T(8,128)(2,1)S(1)}) custom-call(s32[3]{0:T(128)S(1)} %copy-done.30, bf16[512,8192]{1,0:T(8,128)(2,1)} %w_ref.13, bf16[4,2,64,512]{3,2,1,0:T(8,128)(2,1)S(1)} %copy-done.24, ...), custom_call_target="tpu_custom_call" | custom-call | flops 4294967296 | bytes 12582912 | tf_op jit(solution)/shard_map/tile/pallas_call | solution.py:278
  209.6 5.1 %collective-permute-done.24 = bf16[2,64,1024]{2,1,0:T(8,128)(2,1)S(1)} collective-permute-done((bf16[2,64,1024]{2,1,0:T(8,128)(2,1)S(1)}, bf16[2,64,1024]{2,1,0:T(8,128)(2,1)S(1)}, u32[]{:S(2)}, u32[]{:S(2)}) %collective-permute-start.24) | collective-permute-done | bytes 262176 | tf_op jit(solution)/shard_map/ppermute | solution.py:28
  214.8 5.7 %collective-permute-done.33 = bf16[2,64,2048]{2,1,0:T(8,128)(2,1)S(1)} collective-permute-done((bf16[2,64,2048]{2,1,0:T(8,128)(2,1)S(1)}, bf16[2,64,2048]{2,1,0:T(8,128)(2,1)S(1)}, u32[]{:S(2)}, u32[]{:S(2)}) %collective-permute-start.33) | collective-permute-done | bytes 524320 | tf_op jit(solution)/shard_map/ppermute | solution.py:28
  220.6 9.8 %collective-permute-done.32 = bf16[2,64,2048]{2,1,0:T(8,128)(2,1)S(1)} collective-permute-done((bf16[2,64,2048]{2,1,0:T(8,128)(2,1)S(1)}, bf16[2,64,2048]{2,1,0:T(8,128)(2,1)S(1)}, u32[]{:S(2)}, u32[]{:S(2)}) %collective-permute-start.32) | collective-permute-done | bytes 524320 | tf_op jit(solution)/shard_map/ppermute | solution.py:28
  230.4 4.1 %collective-permute-done.31 = bf16[2,64,2048]{2,1,0:T(8,128)(2,1)S(1)} collective-permute-done((bf16[2,64,2048]{2,1,0:T(8,128)(2,1)S(1)}, bf16[2,64,2048]{2,1,0:T(8,128)(2,1)S(1)}, u32[]{:S(2)}, u32[]{:S(2)}) %collective-permute-start.31) | collective-permute-done | bytes 524320 | tf_op jit(solution)/shard_map/ppermute | solution.py:28
  234.9 7.5 %tile.10 = (bf16[2,64,2048]{2,1,0:T(8,128)(2,1)S(1)}, bf16[2,64,2048]{2,1,0:T(8,128)(2,1)S(1)}, bf16[2,64,2048]{2,1,0:T(8,128)(2,1)S(1)}, bf16[2,64,2048]{2,1,0:T(8,128)(2,1)S(1)}) custom-call(s32[3]{0:T(128)S(1)} %copy-done.30, bf16[512,8192]{1,0:T(8,128)(2,1)} %w_ref.13, bf16[4,2,32,512]{3,2,1,0:T(8,128)(2,1)S(1)} %get-tuple-element.56.refs_0_, ...), custom_call_target="tpu_custom_call" | custom-call | flops 4294967296 | bytes 12582912 | tf_op jit(solution)/shard_map/tile/pallas_call | solution.py:278
  244.8 9.5 %tile.11 = (bf16[2,64,2048]{2,1,0:T(8,128)(2,1)S(1)}, bf16[2,64,2048]{2,1,0:T(8,128)(2,1)S(1)}, bf16[2,64,2048]{2,1,0:T(8,128)(2,1)S(1)}, bf16[2,64,2048]{2,1,0:T(8,128)(2,1)S(1)}) custom-call(s32[3]{0:T(128)S(1)} %copy-done.30, bf16[512,8192]{1,0:T(8,128)(2,1)} %w_ref.13, bf16[4,2,64,512]{3,2,1,0:T(8,128)(2,1)S(1)} %copy-done.24, ...), custom_call_target="tpu_custom_call" | custom-call | flops 4294967296 | bytes 12582912 | tf_op jit(solution)/shard_map/tile/pallas_call | solution.py:278
  254.4 3.0 collective-permute-start.44
  257.3 11.4 %collective-permute-done.39 = bf16[2,64,2048]{2,1,0:T(8,128)(2,1)S(1)} collective-permute-done((bf16[2,64,2048]{2,1,0:T(8,128)(2,1)S(1)}, bf16[2,64,2048]{2,1,0:T(8,128)(2,1)S(1)}, u32[]{:S(2)}, u32[]{:S(2)}) %collective-permute-start.39) | collective-permute-done | bytes 524320 | tf_op jit(solution)/shard_map/ppermute | solution.py:28
  268.7 3.9 %collective-permute-start.43 = (bf16[2,64,2048]{2,1,0:T(8,128)(2,1)S(1)}, bf16[2,64,2048]{2,1,0:T(8,128)(2,1)S(1)}, u32[]{:S(2)}, u32[]{:S(2)}) collective-permute-start(bf16[2,64,2048]{2,1,0:T(8,128)(2,1)S(1)} %get-tuple-element.101), channel_id=1, source_target_pairs={{0,3},{1,0},{2,1},{3,2},{4,7},{5,4},{6,5},{7,6},{8,11},{9,8},{10,9... | collective-permute-start | bytes 1572872 | tf_op jit(solution)/shard_map/ppermute | solution.py:28
  276.1 11.5 %collective-permute-done.43 = bf16[2,64,2048]{2,1,0:T(8,128)(2,1)S(1)} collective-permute-done((bf16[2,64,2048]{2,1,0:T(8,128)(2,1)S(1)}, bf16[2,64,2048]{2,1,0:T(8,128)(2,1)S(1)}, u32[]{:S(2)}, u32[]{:S(2)}) %collective-permute-start.43) | collective-permute-done | bytes 524320 | tf_op jit(solution)/shard_map/ppermute | solution.py:28
  287.6 4.1 %collective-permute-done.42 = bf16[2,64,2048]{2,1,0:T(8,128)(2,1)S(1)} collective-permute-done((bf16[2,64,2048]{2,1,0:T(8,128)(2,1)S(1)}, bf16[2,64,2048]{2,1,0:T(8,128)(2,1)S(1)}, u32[]{:S(2)}, u32[]{:S(2)}) %collective-permute-start.42) | collective-permute-done | bytes 524320 | tf_op jit(solution)/shard_map/ppermute | solution.py:28
  295.6 8.3 %collective-permute-done.20.refs_3_ = bf16[32,1024]{1,0:T(8,128)(2,1)S(1)} collective-permute-done((bf16[32,1024]{1,0:T(8,128)(2,1)S(1)}, bf16[32,1024]{1,0:T(8,128)(2,1)S(1)}, u32[]{:S(2)}, u32[]{:S(2)}) %collective-permute-start.20) | collective-permute-done | bytes 65568 | tf_op jit(solution)/shard_map/ppermute | solution.py:32
  304.9 65.4 %place.1 = bf16[128,8192]{1,0:T(8,128)(2,1)} custom-call(s32[3]{0:T(128)} %pad_add_fusion.pos_ref, bf16[32,1024]{1,0:T(8,128)(2,1)} %get-tuple-element.114.refs_0_, bf16[32,1024]{1,0:T(8,128)(2,1)} %copy-done.45, bf16[32,1024]{1,0:T(8,128)(2,1)} %get-tuple-element.112.refs_2_, bf16[32,1024]{1,0:T(8,128)(2,1)} %copy-done.46, ...), custom_call_target="tpu_custom_call" | custom-call | tf_op jit(solution)/shard_map/place/pallas_call | solution.py:367
  (199 shorter events, 70.8 us)
Async XLA Ops:
  6.5 148.6 %all-gather.7.cloned.1.call-start = ((), (), s32[]{:S(2)}) async-start(), calls=%async_computation | async-start | bytes 3538944 | tf_op jit(solution)/shard_map/all_gather | solution.py:330
  67.7 107.7 %all-gather.9.cloned.1.call-start = ((), (), s32[]{:S(2)}) async-start(), calls=%async_computation.1 | async-start | bytes 3538944 | tf_op jit(solution)/shard_map/all_gather | solution.py:330
  79.3 155.6 %all-gather.11.cloned.1.call-start = ((), (), s32[]{:S(2)}) async-start(), calls=%async_computation.2 | async-start | bytes 7077888 | tf_op jit(solution)/shard_map/all_gather | solution.py:330
  81.5 12.6 %collective-permute-start.36 = (bf16[512,256]{1,0:T(8,128)(2,1)S(1)}, bf16[512,256]{1,0:T(8,128)(2,1)S(1)}, u32[]{:S(2)}, u32[]{:S(2)}) collective-permute-start(bf16[512,256]{1,0:T(8,128)(2,1)S(1)} %copy-done.48), channel_id=1, source_target_pairs={{0,12},{1,13},{2,14},{3,15},{4,0},{5,1},{6,2},{7,3},{8,4},{9,5},{1... | collective-permute-start | bytes 786440 | tf_op jit(solution)/shard_map/ppermute | solution.py:24
  83.0 11.2 %collective-permute-start.35 = (bf16[512,256]{1,0:T(8,128)(2,1)S(1)}, bf16[512,256]{1,0:T(8,128)(2,1)S(1)}, u32[]{:S(2)}, u32[]{:S(2)}) collective-permute-start(bf16[512,256]{1,0:T(8,128)(2,1)S(1)} %copy-done.47), channel_id=1, source_target_pairs={{0,4},{1,5},{2,6},{3,7},{4,8},{5,9},{6,10},{7,11},{8,12},{9,13},{1... | collective-permute-start | bytes 786440 | tf_op jit(solution)/shard_map/ppermute | solution.py:24
  125.2 12.9 %collective-permute-start.4 = (bf16[4,2,32,512]{3,2,1,0:T(8,128)(2,1)S(1)}, bf16[4,2,32,512]{3,2,1,0:T(8,128)(2,1)S(1)}, u32[]{:S(2)}, u32[]{:S(2)}) collective-permute-start(bf16[4,2,32,512]{3,2,1,0:T(8,128)(2,1)S(1)} %get-tuple-element.57), channel_id=1, source_target_pairs={{0,4},{1,5},{2,6},{3,7},{4,8},{5,9},{6,10},{7,11},{8,12},{9,13},{1... | collective-permute-start | bytes 786440 | tf_op jit(solution)/shard_map/ppermute | solution.py:24
  126.3 23.1 %collective-permute-start.5 = (bf16[4,2,32,512]{3,2,1,0:T(8,128)(2,1)S(1)}, bf16[4,2,32,512]{3,2,1,0:T(8,128)(2,1)S(1)}, u32[]{:S(2)}, u32[]{:S(2)}) collective-permute-start(bf16[4,2,32,512]{3,2,1,0:T(8,128)(2,1)S(1)} %get-tuple-element.58), channel_id=1, source_target_pairs={{0,12},{1,13},{2,14},{3,15},{4,0},{5,1},{6,2},{7,3},{8,4},{9,5},{1... | collective-permute-start | bytes 786440 | tf_op jit(solution)/shard_map/ppermute | solution.py:24
  127.9 22.2 %collective-permute-start.6 = (bf16[4,2,32,512]{3,2,1,0:T(8,128)(2,1)S(1)}, bf16[4,2,32,512]{3,2,1,0:T(8,128)(2,1)S(1)}, u32[]{:S(2)}, u32[]{:S(2)}) collective-permute-start(bf16[4,2,32,512]{3,2,1,0:T(8,128)(2,1)S(1)} %get-tuple-element.59), channel_id=1, source_target_pairs={{0,8},{1,9},{2,10},{3,11},{4,12},{5,13},{6,14},{7,15},{8,0},{9,1},... | collective-permute-start | bytes 786440 | tf_op jit(solution)/shard_map/ppermute | solution.py:24
  135.4 18.1 %collective-permute-start.14 = (bf16[4,2,32,512]{3,2,1,0:T(8,128)(2,1)S(1)}, bf16[4,2,32,512]{3,2,1,0:T(8,128)(2,1)S(1)}, u32[]{:S(2)}, u32[]{:S(2)}) collective-permute-start(bf16[4,2,32,512]{3,2,1,0:T(8,128)(2,1)S(1)} %get-tuple-element.69), channel_id=1, source_target_pairs={{0,4},{1,5},{2,6},{3,7},{4,8},{5,9},{6,10},{7,11},{8,12},{9,13},{1... | collective-permute-start | bytes 786440 | tf_op jit(solution)/shard_map/ppermute | solution.py:24
  136.3 29.3 %collective-permute-start.15 = (bf16[4,2,32,512]{3,2,1,0:T(8,128)(2,1)}, bf16[4,2,32,512]{3,2,1,0:T(8,128)(2,1)}, u32[]{:S(2)}, u32[]{:S(2)}) collective-permute-start(bf16[4,2,32,512]{3,2,1,0:T(8,128)(2,1)} %get-tuple-element.70), channel_id=1, source_target_pairs={{0,12},{1,13},{2,14},{3,15},{4,0},{5,1},{6,2},{7,3},{8,4},{9,5},{1... | collective-permute-start | bytes 786440 | tf_op jit(solution)/shard_map/ppermute | solution.py:24
  138.1 31.5 %collective-permute-start.16 = (bf16[4,2,32,512]{3,2,1,0:T(8,128)(2,1)}, bf16[4,2,32,512]{3,2,1,0:T(8,128)(2,1)}, u32[]{:S(2)}, u32[]{:S(2)}) collective-permute-start(bf16[4,2,32,512]{3,2,1,0:T(8,128)(2,1)} %get-tuple-element.71), channel_id=1, source_target_pairs={{0,8},{1,9},{2,10},{3,11},{4,12},{5,13},{6,14},{7,15},{8,0},{9,1},... | collective-permute-start | bytes 786440 | tf_op jit(solution)/shard_map/ppermute | solution.py:24
  150.2 35.0 %collective-permute-start.28 = (bf16[4,2,64,512]{3,2,1,0:T(8,128)(2,1)}, bf16[4,2,64,512]{3,2,1,0:T(8,128)(2,1)}, u32[]{:S(2)}, u32[]{:S(2)}) collective-permute-start(bf16[4,2,64,512]{3,2,1,0:T(8,128)(2,1)} %get-tuple-element.85), channel_id=1, source_target_pairs={{0,4},{1,5},{2,6},{3,7},{4,8},{5,9},{6,10},{7,11},{8,12},{9,13},{1... | collective-permute-start | bytes 1572872 | tf_op jit(solution)/shard_map/ppermute | solution.py:24
  150.9 35.4 %collective-permute-start.29 = (bf16[4,2,64,512]{3,2,1,0:T(8,128)(2,1)}, bf16[4,2,64,512]{3,2,1,0:T(8,128)(2,1)}, u32[]{:S(2)}, u32[]{:S(2)}) collective-permute-start(bf16[4,2,64,512]{3,2,1,0:T(8,128)(2,1)} %get-tuple-element.86), channel_id=1, source_target_pairs={{0,12},{1,13},{2,14},{3,15},{4,0},{5,1},{6,2},{7,3},{8,4},{9,5},{1... | collective-permute-start | bytes 1572872 | tf_op jit(solution)/shard_map/ppermute | solution.py:24
  154.3 33.3 %collective-permute-start.30 = (bf16[4,2,64,512]{3,2,1,0:T(8,128)(2,1)}, bf16[4,2,64,512]{3,2,1,0:T(8,128)(2,1)}, u32[]{:S(2)}, u32[]{:S(2)}) collective-permute-start(bf16[4,2,64,512]{3,2,1,0:T(8,128)(2,1)} %get-tuple-element.87), channel_id=1, source_target_pairs={{0,8},{1,9},{2,10},{3,11},{4,12},{5,13},{6,14},{7,15},{8,0},{9,1},... | collective-permute-start | bytes 1572872 | tf_op jit(solution)/shard_map/ppermute | solution.py:24
  165.6 33.4 %collective-permute-start.12 = (bf16[2,32,1024]{2,1,0:T(8,128)(2,1)}, bf16[2,32,1024]{2,1,0:T(8,128)(2,1)}, u32[]{:S(2)}, u32[]{:S(2)}) collective-permute-start(bf16[2,32,1024]{2,1,0:T(8,128)(2,1)} %get-tuple-element.66), channel_id=1, source_target_pairs={{0,2},{1,3},{2,0},{3,1},{4,6},{5,7},{6,4},{7,5},{8,10},{9,11},{10,... | collective-permute-start | bytes 393224 | tf_op jit(solution)/shard_map/ppermute | solution.py:28
  169.7 31.1 %collective-permute-start.11 = (bf16[2,32,1024]{2,1,0:T(8,128)(2,1)}, bf16[2,32,1024]{2,1,0:T(8,128)(2,1)}, u32[]{:S(2)}, u32[]{:S(2)}) collective-permute-start(bf16[2,32,1024]{2,1,0:T(8,128)(2,1)} %get-tuple-element.65), channel_id=1, source_target_pairs={{0,3},{1,0},{2,1},{3,2},{4,7},{5,4},{6,5},{7,6},{8,11},{9,8},{10,9... | collective-permute-start | bytes 393224 | tf_op jit(solution)/shard_map/ppermute | solution.py:28
  185.2 15.6 %collective-permute-start.10 = (bf16[2,32,1024]{2,1,0:T(8,128)(2,1)S(1)}, bf16[2,32,1024]{2,1,0:T(8,128)(2,1)S(1)}, u32[]{:S(2)}, u32[]{:S(2)}) collective-permute-start(bf16[2,32,1024]{2,1,0:T(8,128)(2,1)S(1)} %copy-done.37), channel_id=1, source_target_pairs={{0,1},{1,2},{2,3},{3,0},{4,5},{5,6},{6,7},{7,4},{8,9},{9,10},{10,1... | collective-permute-start | bytes 393224 | tf_op jit(solution)/shard_map/ppermute | solution.py:28
  186.3 18.2 %collective-permute-start.19 = (bf16[2,32,1024]{2,1,0:T(8,128)(2,1)S(1)}, bf16[2,32,1024]{2,1,0:T(8,128)(2,1)S(1)}, u32[]{:S(2)}, u32[]{:S(2)}) collective-permute-start(bf16[2,32,1024]{2,1,0:T(8,128)(2,1)S(1)} %copy-done.39), channel_id=1, source_target_pairs={{0,2},{1,3},{2,0},{3,1},{4,6},{5,7},{6,4},{7,5},{8,10},{9,11},{10,... | collective-permute-start | bytes 393224 | tf_op jit(solution)/shard_map/ppermute | solution.py:28
  187.5 19.8 %collective-permute-start.26 = (bf16[2,64,1024]{2,1,0:T(8,128)(2,1)S(1)}, bf16[2,64,1024]{2,1,0:T(8,128)(2,1)S(1)}, u32[]{:S(2)}, u32[]{:S(2)}) collective-permute-start(bf16[2,64,1024]{2,1,0:T(8,128)(2,1)S(1)} %get-tuple-element.82), channel_id=1, source_target_pairs={{0,2},{1,3},{2,0},{3,1},{4,6},{5,7},{6,4},{7,5},{8,10},{9,11},{10,... | collective-permute-start | bytes 786440 | tf_op jit(solution)/shard_map/ppermute | solution.py:28
  204.6 16.0 %collective-permute-start.33 = (bf16[2,64,2048]{2,1,0:T(8,128)(2,1)S(1)}, bf16[2,64,2048]{2,1,0:T(8,128)(2,1)S(1)}, u32[]{:S(2)}, u32[]{:S(2)}) collective-permute-start(bf16[2,64,2048]{2,1,0:T(8,128)(2,1)S(1)} %get-tuple-element.91), channel_id=1, source_target_pairs={{0,2},{1,3},{2,0},{3,1},{4,6},{5,7},{6,4},{7,5},{8,10},{9,11},{10,... | collective-permute-start | bytes 1572872 | tf_op jit(solution)/shard_map/ppermute | solution.py:28
  205.8 24.6 %collective-permute-start.32 = (bf16[2,64,2048]{2,1,0:T(8,128)(2,1)S(1)}, bf16[2,64,2048]{2,1,0:T(8,128)(2,1)S(1)}, u32[]{:S(2)}, u32[]{:S(2)}) collective-permute-start(bf16[2,64,2048]{2,1,0:T(8,128)(2,1)S(1)} %get-tuple-element.90), channel_id=1, source_target_pairs={{0,3},{1,0},{2,1},{3,2},{4,7},{5,4},{6,5},{7,6},{8,11},{9,8},{10,9... | collective-permute-start | bytes 1572872 | tf_op jit(solution)/shard_map/ppermute | solution.py:28
  207.3 27.1 %collective-permute-start.31 = (bf16[2,64,2048]{2,1,0:T(8,128)(2,1)S(1)}, bf16[2,64,2048]{2,1,0:T(8,128)(2,1)S(1)}, u32[]{:S(2)}, u32[]{:S(2)}) collective-permute-start(bf16[2,64,2048]{2,1,0:T(8,128)(2,1)S(1)} %get-tuple-element.89), channel_id=1, source_target_pairs={{0,1},{1,2},{2,3},{3,0},{4,5},{5,6},{6,7},{7,4},{8,9},{9,10},{10,1... | collective-permute-start | bytes 1572872 | tf_op jit(solution)/shard_map/ppermute | solution.py:28
  209.3 86.3 %collective-permute-start.13 = (bf16[32,1024]{1,0:T(8,128)(2,1)}, bf16[32,1024]{1,0:T(8,128)(2,1)S(1)}, u32[]{:S(2)}, u32[]{:S(2)}) collective-permute-start(bf16[32,1024]{1,0:T(8,128)(2,1)} %get-tuple-element.113), channel_id=1, source_target_pairs={{0,4},{1,5},{2,6},{3,7},{4,0},{5,1},{6,2},{7,3},{8,12},{9,13},{10,... | collective-permute-start | bytes 196616 | tf_op jit(solution)/shard_map/ppermute | solution.py:32
  242.4 11.9 %collective-permute-start.40 = (bf16[2,64,2048]{2,1,0:T(8,128)(2,1)S(1)}, bf16[2,64,2048]{2,1,0:T(8,128)(2,1)S(1)}, u32[]{:S(2)}, u32[]{:S(2)}) collective-permute-start(bf16[2,64,2048]{2,1,0:T(8,128)(2,1)S(1)} %get-tuple-element.98), channel_id=1, source_target_pairs={{0,2},{1,3},{2,0},{3,1},{4,6},{5,7},{6,4},{7,5},{8,10},{9,11},{10,... | collective-permute-start | bytes 1572872 | tf_op jit(solution)/shard_map/ppermute | solution.py:28
  242.5 26.2 %collective-permute-start.39 = (bf16[2,64,2048]{2,1,0:T(8,128)(2,1)S(1)}, bf16[2,64,2048]{2,1,0:T(8,128)(2,1)S(1)}, u32[]{:S(2)}, u32[]{:S(2)}) collective-permute-start(bf16[2,64,2048]{2,1,0:T(8,128)(2,1)S(1)} %get-tuple-element.97), channel_id=1, source_target_pairs={{0,3},{1,0},{2,1},{3,2},{4,7},{5,4},{6,5},{7,6},{8,11},{9,8},{10,9... | collective-permute-start | bytes 1572872 | tf_op jit(solution)/shard_map/ppermute | solution.py:28
  242.6 30.7 %collective-permute-start.38 = (bf16[2,64,2048]{2,1,0:T(8,128)(2,1)S(1)}, bf16[2,64,2048]{2,1,0:T(8,128)(2,1)S(1)}, u32[]{:S(2)}, u32[]{:S(2)}) collective-permute-start(bf16[2,64,2048]{2,1,0:T(8,128)(2,1)S(1)} %get-tuple-element.96), channel_id=1, source_target_pairs={{0,1},{1,2},{2,3},{3,0},{4,5},{5,6},{6,7},{7,4},{8,9},{9,10},{10,1... | collective-permute-start | bytes 1572872 | tf_op jit(solution)/shard_map/ppermute | solution.py:28
  244.8 59.1 %collective-permute-start.34 = (bf16[64,2048]{1,0:T(8,128)(2,1)S(1)}, bf16[64,2048]{1,0:T(8,128)(2,1)S(1)}, u32[]{:S(2)}, u32[]{:S(2)}) collective-permute-start(bf16[64,2048]{1,0:T(8,128)(2,1)S(1)} %get-tuple-element.107), channel_id=1, source_target_pairs={{0,4},{1,5},{2,6},{3,7},{4,0},{5,1},{6,2},{7,3},{8,12},{9,13},{10,... | collective-permute-start | bytes 786440 | tf_op jit(solution)/shard_map/ppermute | solution.py:32
  254.4 21.7 %collective-permute-start.44 = (bf16[2,64,2048]{2,1,0:T(8,128)(2,1)S(1)}, bf16[2,64,2048]{2,1,0:T(8,128)(2,1)S(1)}, u32[]{:S(2)}, u32[]{:S(2)}) collective-permute-start(bf16[2,64,2048]{2,1,0:T(8,128)(2,1)S(1)} %get-tuple-element.102), channel_id=1, source_target_pairs={{0,2},{1,3},{2,0},{3,1},{4,6},{5,7},{6,4},{7,5},{8,10},{9,11},{10,... | collective-permute-start | bytes 1572872 | tf_op jit(solution)/shard_map/ppermute | solution.py:28
  268.7 18.9 %collective-permute-start.43 = (bf16[2,64,2048]{2,1,0:T(8,128)(2,1)S(1)}, bf16[2,64,2048]{2,1,0:T(8,128)(2,1)S(1)}, u32[]{:S(2)}, u32[]{:S(2)}) collective-permute-start(bf16[2,64,2048]{2,1,0:T(8,128)(2,1)S(1)} %get-tuple-element.101), channel_id=1, source_target_pairs={{0,3},{1,0},{2,1},{3,2},{4,7},{5,4},{6,5},{7,6},{8,11},{9,8},{10,9... | collective-permute-start | bytes 1572872 | tf_op jit(solution)/shard_map/ppermute | solution.py:28
  273.3 18.4 %collective-permute-start.42 = (bf16[2,64,2048]{2,1,0:T(8,128)(2,1)S(1)}, bf16[2,64,2048]{2,1,0:T(8,128)(2,1)S(1)}, u32[]{:S(2)}, u32[]{:S(2)}) collective-permute-start(bf16[2,64,2048]{2,1,0:T(8,128)(2,1)S(1)} %get-tuple-element.100), channel_id=1, source_target_pairs={{0,1},{1,2},{2,3},{3,0},{4,5},{5,6},{6,7},{7,4},{8,9},{9,10},{10,1... | collective-permute-start | bytes 1572872 | tf_op jit(solution)/shard_map/ppermute | solution.py:28
  276.1 27.9 %collective-permute-start.41 = (bf16[64,2048]{1,0:T(8,128)(2,1)S(1)}, bf16[64,2048]{1,0:T(8,128)(2,1)S(1)}, u32[]{:S(2)}, u32[]{:S(2)}) collective-permute-start(bf16[64,2048]{1,0:T(8,128)(2,1)S(1)} %get-tuple-element.105), channel_id=1, source_target_pairs={{0,4},{1,5},{2,6},{3,7},{4,0},{5,1},{6,2},{7,3},{8,12},{9,13},{10,... | collective-permute-start | bytes 786440 | tf_op jit(solution)/shard_map/ppermute | solution.py:32
  292.9 11.1 %collective-permute-start.45 = (bf16[64,2048]{1,0:T(8,128)(2,1)S(1)}, bf16[64,2048]{1,0:T(8,128)(2,1)S(1)}, u32[]{:S(2)}, u32[]{:S(2)}) collective-permute-start(bf16[64,2048]{1,0:T(8,128)(2,1)S(1)} %get-tuple-element.103), channel_id=1, source_target_pairs={{0,4},{1,5},{2,6},{3,7},{4,0},{5,1},{6,2},{7,3},{8,12},{9,13},{10,... | collective-permute-start | bytes 786440 | tf_op jit(solution)/shard_map/ppermute | solution.py:32
  (67 other events, 551.6 us)
Sparse Core Ops, SparseCore 0:
  67.8 31.0 all-gather.6
  100.5 27.7 all-gather.8
  130.0 41.5 all-gather.10

commit v3 on v2

--- a/solution.py
+++ b/solution.py
@@ -11,10 +11,10 @@
 LANES = 128
 NX, NCORE, NY, NZ = 4, 2, 4, 4
 STEPS = (1, -1, 2)
-ROW_PARTS = (2, 2, 4)
-COL_PARTS = (2, 2, 4)
-TILES = (((0,), (0,)), ((1,), (0,)), ((0, 1), (1,)), ((2,), (0, 1)), ((0, 1), (2,)), ((2,), (2,)))
-ANY = pl.BlockSpec(memory_space=pl.ANY)
+ROW_PARTS = (1, 1)
+COL_PARTS = (1, 1)
+TILES = (((0,), (0,)), ((1,), (0,)), ((0,), (1,)), ((1,), (1,)))
+HBM = pl.BlockSpec(memory_space=pltpu.HBM)
 SMEM = pl.BlockSpec(memory_space=pltpu.SMEM)
 VMEM = pl.BlockSpec(memory_space=pltpu.VMEM)
 LIMIT = pltpu.CompilerParams(vmem_limit_bytes=48 * 1024 * 1024)
@@ -165,7 +165,7 @@
     if first:
         ops.append(inc)
         specs.append(par)
-    out = jax.ShapeDtypeStruct((NZ, 2, tc, C), jnp.bfloat16)
+    out = pltpu.HBM((NZ, 2, tc, C), jnp.bfloat16)
     out_shape = [out] * 4
     out_specs = [pl.BlockSpec((NZ, 2, tc, W), lambda c: (0, 0, 0, c))] * 4
     if not last:
@@ -212,10 +212,11 @@
     n = len(widths) * len(STEPS)
     out = pl.pallas_call(
         functools.partial(share_kernel, widths=widths, offsets=offsets, half_cols=half_cols),
-        in_specs=[SMEM, ANY],
-        out_specs=[ANY] * n,
-        out_shape=[jax.ShapeDtypeStruct((k, w), weight.dtype) for w in widths for _ in STEPS],
+        in_specs=[SMEM, HBM],
+        out_specs=[VMEM] * n,
+        out_shape=[pltpu.HBM((k, w), weight.dtype) for w in widths for _ in STEPS],
         scratch_shapes=[pltpu.SemaphoreType.DMA((n,))],
+        compiler_params=LIMIT,
         name="weight_shares",
     )(pos, weight)
     return [out[g * len(STEPS):(g + 1) * len(STEPS)] for g in range(len(widths))]
@@ -277,9 +278,9 @@
     flat = [piece for a in a_parts for piece in a]
     return pl.pallas_call(
         functools.partial(tile_kernel, row_sizes=row_sizes, cols=cols, offsets=offsets, half_cols=half_cols, block=block),
-        in_specs=[SMEM, ANY] + [ANY] * (len(flat) + len(b_parts)),
+        in_specs=[SMEM, HBM] + [HBM] * (len(flat) + len(b_parts)),
         out_specs=[VMEM] * NZ,
-        out_shape=[jax.ShapeDtypeStruct((2, total, n), jnp.bfloat16)] * NZ,
+        out_shape=[pltpu.HBM((2, total, n), jnp.bfloat16)] * NZ,
         scratch_shapes=[
             pltpu.VMEM((NZ, 2, total, 4 * width), jnp.bfloat16),
             pltpu.VMEM((4 * width, n), jnp.bfloat16),
@@ -324,13 +325,16 @@
     offsets = [sum(cols[:g]) for g in range(len(cols))]
 
     shares = weight_shares(pos, out_weight, [c // (NX * NCORE) for c in cols], offsets, half_cols)
-    weights = []
-    for group in shares:
-        got = jnp.concatenate([over_y(piece, step) for piece, step in zip(group, STEPS)], axis=0)
-        weights.append(lax.all_gather(got, "seq", axis=0))
+    fetched = [[over_y(piece, step) for piece, step in zip(group, STEPS)] for group in shares]
 
     q3, k3, v3 = [x.reshape(owners, per, width) for x in (query_proj, key_proj, value_proj)]
     excl, span = states(k3, v3, pole_rate)
+
+    def gathered(group, after):
+        _, *pieces = lax.optimization_barrier((after, *group))
+        return lax.all_gather(jnp.concatenate(pieces, axis=0), "seq", axis=0)
+
+    weights = [gathered(fetched[0], span)]
     across = jnp.exp(-pole_rate * rows)
     across2 = jnp.exp(-pole_rate * (2.0 * rows))
     across4 = jnp.exp(-pole_rate * (4.0 * rows))
@@ -345,6 +349,8 @@
         sent, state = conv_chunk(
             pos, q3, k3, v3, pole_rate, pole_residue, skip_gain, state, incoming if i == 0 else None,
             start // tc, tc, i == len(tcs) - 1)
+        if i + 1 < len(fetched):
+            weights.append(gathered(fetched[i + 1], sent[0]))
         mixed.append([sent[0]] + [over_y(piece, step) for piece, step in zip(sent[1:], STEPS)])
         start += tc
 
@@ -366,10 +372,11 @@
         places += [(0, row, size, col, n), (1, row, size, col, n)]
     return pl.pallas_call(
         functools.partial(place_kernel, places=tuple(places), half_cols=half_cols),
-        in_specs=[SMEM] + [ANY] * len(pieces),
-        out_specs=ANY,
+        in_specs=[SMEM] + [HBM] * len(pieces),
+        out_specs=VMEM,
         out_shape=jax.ShapeDtypeStruct((per, total_cols), jnp.bfloat16),
         scratch_shapes=[pltpu.SemaphoreType.DMA((len(pieces),))],
+        compiler_params=LIMIT,
         name="place",
     )(pos, *pieces)
 

time: 379 us -> 205 us (0.54)
  Pallas kernels: 186 us -> 75.3 us
  waiting for transfers between devices: 86.6 us -> 54 us
  local copies, waits for them, and re-layouts: 22.7 us -> 4.5 us
  starting transfers between devices: 61.3 us -> 48.3 us
    pallas_call x1, Pallas kernels: 65.4 us -> 2.1 us  [local(): pl.pallas_call(functools.partial(place_kernel, places=tuple(places), half...]
    pallas_call x1, Pallas kernels: 49.5 us -> 3.2 us  [weight_shares(): pl.pallas_call(functools.partial(share_kernel, widths=widths, offsets=off...]
    ppermute x18 -> x12, waiting for transfers between devices: 54.1 us -> 35.8 us  [over_z(): lax.ppermute(value, 'chan', [(y * NZ + z, y * NZ + (z + step) % NZ) for y...]
    unnamed x100 -> x44, local copies, waits for them, and re-layouts: 18.4 us -> 4.31 us
    ppermute x18 -> x12, waiting for transfers between devices: 22 us -> 11 us  [over_y(): lax.ppermute(value, 'chan', [(y * NZ + z, (y + step) % NY * NZ + z) for y...]
    ppermute x18 -> x12, starting transfers between devices: 24.6 us -> 15.4 us  [over_y(): lax.ppermute(value, 'chan', [(y * NZ + z, (y + step) % NY * NZ + z) for y...]
    ppermute x18 -> x12, starting transfers between devices: 24.8 us -> 19.5 us  [over_z(): lax.ppermute(value, 'chan', [(y * NZ + z, y * NZ + (z + step) % NZ) for y...]
    squeeze x6 -> x4, local copies, waits for them, and re-layouts: 4.23 us -> 0.19 us  [local(): send = lax.dynamic_index_in_dim(summed, 1 - parity, 0, keepdims=False)]
  transfers between devices with their start and end apart: 49 -> 34, of which waited for: 20 -> 12; matrix products, arithmetic and copies ran while one was open for 3% -> 3% of each run, Pallas kernels for 19% -> 35%
where the time goes in v3:
time: 205 us; the launch traced here: 203 us
  Pallas kernels  75.3 us (37%)
  waiting for transfers between devices  54 us (26%)
  starting transfers between devices  48.3 us (24%)
  between operations  13.8 us (7%)
  other arithmetic  6.76 us (3%)
  local copies, waits for them, and re-layouts  4.5 us (2%)
    pallas_call x4, Pallas kernels, tile(): pl.pallas_call(functools.partial(tile_kernel, row_sizes=row_sizes, cols=c...  39.7 us
    ppermute x12, waiting for transfers between devices, over_z(): lax.ppermute(value, 'chan', [(y * NZ + z, y * NZ + (z + step) % NZ) for y...  35.8 us
    pallas_call x2, Pallas kernels, conv_chunk(): pl.pallas_call(functools.partial(conv_kernel, unroll=4, per=T, first=firs...  19.8 us
    ppermute x12, starting transfers between devices, over_z(): lax.ppermute(value, 'chan', [(y * NZ + z, y * NZ + (z + step) % NZ) for y...  19.5 us
    ppermute x12, starting transfers between devices, over_y(): lax.ppermute(value, 'chan', [(y * NZ + z, (y + step) % NY * NZ + z) for y...  15.4 us
    ppermute x12, waiting for transfers between devices, over_y(): lax.ppermute(value, 'chan', [(y * NZ + z, (y + step) % NY * NZ + z) for y...  11 us
    pallas_call x1, Pallas kernels, states(): pl.pallas_call(functools.partial(state_kernel, T=T, unroll=unroll), grid=...  10.5 us
    ppermute x3, starting transfers between devices, from_chip_behind(): return lax.ppermute(value, 'seq', pairs)  8.69 us
  transfers between devices with their start and end apart: 34, of which 12 were waited for; matrix products, arithmetic and copies ran while one was open for 3% of the time, Pallas kernels for 35%

profile of v3, /device:TPU:1, one launch (start us, length us, event | category | flops | bytes accessed | tf_op | source)
XLA Modules:
  0.0 202.7 jit_solution(6006254934439415561)
XLA Ops:
  6.6 3.2 %weight_shares.1 = (bf16[512,256]{1,0:T(8,128)(2,1)}, bf16[512,256]{1,0:T(8,128)(2,1)}, bf16[512,256]{1,0:T(8,128)(2,1)}, bf16[512,256]{1,0:T(8,128)(2,1)}, bf16...) custom-call(s32[3]{0:T(128)S(1)} %pad_add_fusion.pos_ref, bf16[512,8192]{1,0:T(8,128)(2,1)} %w_ref.9), custom_call_target="tpu_custom_call" | custom-call | tf_op jit(solution)/shard_map/weight_shares/pallas_call | solution.py:213
  9.8 2.2 %collective-permute-start.7 = (bf16[512,256]{1,0:T(8,128)(2,1)}, bf16[512,256]{1,0:T(8,128)(2,1)S(1)}, u32[]{:S(2)}, u32[]{:S(2)}) collective-permute-start(bf16[512,256]{1,0:T(8,128)(2,1)} %get-tuple-element.50), channel_id=1, source_target_pairs={{0,4},{1,5},{2,6},{3,7},{4,8},{5,9},{6,10},{7,11},{8,12},{9,13},{1... | collective-permute-start | bytes 786440 | tf_op jit(solution)/shard_map/ppermute | solution.py:24
  15.1 10.5 %states.1 = (f32[16,16,512]{2,1,0:T(8,128)}, f32[16,512]{1,0:T(8,128)}) custom-call(bf16[16,128,512]{2,1,0:T(8,128)(2,1)} %bitcast.25, bf16[16,128,512]{2,1,0:T(8,128)(2,1)} %bitcast.36, f32[16,512]{1,0:T(8,128)} %rate_ref.5), custom_call_target="tpu_custom_call" | custom-call | tf_op jit(solution)/shard_map/states/pallas_call | solution.py:89
  30.7 4.3 %collective-permute-start.3 = (f32[16,512]{1,0:T(8,128)S(1)}, f32[16,512]{1,0:T(8,128)S(1)}, u32[]{:S(2)}, u32[]{:S(2)}) collective-permute-start(f32[16,512]{1,0:T(8,128)S(1)} %add_select_fusion.1), channel_id=1, source_target_pairs={{0,96},{16,112},{1,97},{17,113},{2,98},{18,114},{3,99},{19,115},{4... | collective-permute-start | bytes 98312 | tf_op jit(solution)/shard_map/ppermute | solution.py:41
  36.3 3.1 %collective-permute-start.2 = (f32[16,512]{1,0:T(8,128)S(1)}, f32[16,512]{1,0:T(8,128)S(1)}, u32[]{:S(2)}, u32[]{:S(2)}) collective-permute-start(f32[16,512]{1,0:T(8,128)S(1)} %add_select_fusion.1), channel_id=1, source_target_pairs={{0,64},{16,80},{32,96},{48,112},{1,65},{17,81},{33,97},{49,113},{2... | collective-permute-start | bytes 98312 | tf_op jit(solution)/shard_map/ppermute | solution.py:41
  40.3 1.8 collective-permute-start.22
  42.3 1.6 copy-done.1
  43.9 10.0 %conv.2 = (bf16[4,2,64,512]{3,2,1,0:T(8,128)(2,1)}, bf16[4,2,64,512]{3,2,1,0:T(8,128)(2,1)}, bf16[4,2,64,512]{3,2,1,0:T(8,128)(2,1)}, bf16[4,2,64,512]{3,2,1,0:T(8,128)(2,1)}, f32[16,16,512]{2,1,0:T(8,128)S(1)}) custom-call(s32[3]{0:T(128)S(1)} %pad_add_fusion.pos_ref, bf16[16,128,512]{2,1,0:T(8,128)(2,1)S(1)} %bitcast.28, ...), custom_call_target="tpu_custom_call" | custom-call | flops 33554432 | bytes 5242880 | tf_op jit(solution)/shard_map/conv/pallas_call | solution.py:174
  55.9 1.8 collective-permute-start.5
  57.7 1.7 collective-permute-start.6
  59.4 1.6 copy-done.2
  62.1 9.7 %conv.3 = (bf16[4,2,64,512]{3,2,1,0:T(8,128)(2,1)}, bf16[4,2,64,512]{3,2,1,0:T(8,128)(2,1)}, bf16[4,2,64,512]{3,2,1,0:T(8,128)(2,1)}, bf16[4,2,64,512]{3,2,1,0:T(8,128)(2,1)}) custom-call(s32[3]{0:T(128)S(1)} %pad_add_fusion.pos_ref, bf16[16,128,512]{2,1,0:T(8,128)(2,1)S(1)} %bitcast.29, bf16[16,128,512]{2,1,0:T(8,128)(2,1)S(1)} %bitcast.27, ...), custom_call_target="tpu_custom_call" | custom-call | flops 33554432 | bytes 5242880 | tf_op jit(solution)/shard_map/conv/pallas_call | solution.py:174
  71.8 2.7 %collective-permute-start.15 = (bf16[4,2,64,512]{3,2,1,0:T(8,128)(2,1)}, bf16[4,2,64,512]{3,2,1,0:T(8,128)(2,1)S(1)}, u32[]{:S(2)}, u32[]{:S(2)}) collective-permute-start(bf16[4,2,64,512]{3,2,1,0:T(8,128)(2,1)} %get-tuple-element.63), channel_id=1, source_target_pairs={{0,12},{1,13},{2,14},{3,15},{4,0},{5,1},{6,2},{7,3},{8,4},{9,5},{1... | collective-permute-start | bytes 1572872 | tf_op jit(solution)/shard_map/ppermute | solution.py:24
  74.7 5.1 %collective-permute-done.6.refs_3_ = bf16[4,2,64,512]{3,2,1,0:T(8,128)(2,1)} collective-permute-done((bf16[4,2,64,512]{3,2,1,0:T(8,128)(2,1)}, bf16[4,2,64,512]{3,2,1,0:T(8,128)(2,1)}, u32[]{:S(2)}, u32[]{:S(2)}) %collective-permute-start.6) | collective-permute-done | bytes 524320 | tf_op jit(solution)/shard_map/ppermute | solution.py:24
  79.8 11.5 %tile.4 = (bf16[2,64,2048]{2,1,0:T(8,128)(2,1)}, bf16[2,64,2048]{2,1,0:T(8,128)(2,1)}, bf16[2,64,2048]{2,1,0:T(8,128)(2,1)}, bf16[2,64,2048]{2,1,0:T(8,128)(2,1)}) custom-call(s32[3]{0:T(128)S(1)} %pad_add_fusion.pos_ref, bf16[512,8192]{1,0:T(8,128)(2,1)} %w_ref.9, bf16[4,2,64,512]{3,2,1,0:T(8,128)(2,1)S(1)} %copy-done.3, ...), custom_call_target="tpu_custom_call" | custom-call | flops 4294967296 | bytes 12582912 | tf_op jit(solution)/shard_map/tile/pallas_call | solution.py:279
  91.3 3.6 %collective-permute-start.12 = (bf16[2,64,2048]{2,1,0:T(8,128)(2,1)}, bf16[2,64,2048]{2,1,0:T(8,128)(2,1)}, u32[]{:S(2)}, u32[]{:S(2)}) collective-permute-start(bf16[2,64,2048]{2,1,0:T(8,128)(2,1)} %get-tuple-element.59), channel_id=1, source_target_pairs={{0,2},{1,3},{2,0},{3,1},{4,6},{5,7},{6,4},{7,5},{8,10},{9,11},{10,... | collective-permute-start | bytes 1572872 | tf_op jit(solution)/shard_map/ppermute | solution.py:28
  95.7 1.6 collective-permute-start.10
  97.3 5.0 %collective-permute-done.16.refs_3_ = bf16[4,2,64,512]{3,2,1,0:T(8,128)(2,1)S(1)} collective-permute-done((bf16[4,2,64,512]{3,2,1,0:T(8,128)(2,1)}, bf16[4,2,64,512]{3,2,1,0:T(8,128)(2,1)S(1)}, u32[]{:S(2)}, u32[]{:S(2)}) %collective-permute-start.16) | collective-permute-done | bytes 524320 | tf_op jit(solution)/shard_map/ppermute | solution.py:24
  102.3 8.8 %tile.5 = (bf16[2,64,2048]{2,1,0:T(8,128)(2,1)}, bf16[2,64,2048]{2,1,0:T(8,128)(2,1)}, bf16[2,64,2048]{2,1,0:T(8,128)(2,1)}, bf16[2,64,2048]{2,1,0:T(8,128)(2,1)}) custom-call(s32[3]{0:T(128)S(1)} %pad_add_fusion.pos_ref, bf16[512,8192]{1,0:T(8,128)(2,1)} %w_ref.9, bf16[4,2,64,512]{3,2,1,0:T(8,128)(2,1)S(1)} %copy-done.4, ...), custom_call_target="tpu_custom_call" | custom-call | flops 4294967296 | bytes 12582912 | tf_op jit(solution)/shard_map/tile/pallas_call | solution.py:279
  111.1 3.5 %collective-permute-start.19 = (bf16[2,64,2048]{2,1,0:T(8,128)(2,1)}, bf16[2,64,2048]{2,1,0:T(8,128)(2,1)}, u32[]{:S(2)}, u32[]{:S(2)}) collective-permute-start(bf16[2,64,2048]{2,1,0:T(8,128)(2,1)} %get-tuple-element.68), channel_id=1, source_target_pairs={{0,2},{1,3},{2,0},{3,1},{4,6},{5,7},{6,4},{7,5},{8,10},{9,11},{10,... | collective-permute-start | bytes 1572872 | tf_op jit(solution)/shard_map/ppermute | solution.py:28
  115.1 10.7 %tile.6 = (bf16[2,64,2048]{2,1,0:T(8,128)(2,1)}, bf16[2,64,2048]{2,1,0:T(8,128)(2,1)}, bf16[2,64,2048]{2,1,0:T(8,128)(2,1)}, bf16[2,64,2048]{2,1,0:T(8,128)(2,1)}) custom-call(s32[3]{0:T(128)S(1)} %pad_add_fusion.pos_ref, bf16[512,8192]{1,0:T(8,128)(2,1)} %w_ref.9, bf16[4,2,64,512]{3,2,1,0:T(8,128)(2,1)S(1)} %copy-done.3, ...), custom_call_target="tpu_custom_call" | custom-call | flops 4294967296 | bytes 12582912 | tf_op jit(solution)/shard_map/tile/pallas_call | solution.py:279
  126.9 8.8 %tile.7 = (bf16[2,64,2048]{2,1,0:T(8,128)(2,1)}, bf16[2,64,2048]{2,1,0:T(8,128)(2,1)}, bf16[2,64,2048]{2,1,0:T(8,128)(2,1)}, bf16[2,64,2048]{2,1,0:T(8,128)(2,1)}) custom-call(s32[3]{0:T(128)S(1)} %pad_add_fusion.pos_ref, bf16[512,8192]{1,0:T(8,128)(2,1)} %w_ref.9, bf16[4,2,64,512]{3,2,1,0:T(8,128)(2,1)S(1)} %copy-done.4, ...), custom_call_target="tpu_custom_call" | custom-call | flops 4294967296 | bytes 12582912 | tf_op jit(solution)/shard_map/tile/pallas_call | solution.py:279
  137.0 2.1 %collective-permute-start.25 = (bf16[2,64,2048]{2,1,0:T(8,128)(2,1)S(1)}, bf16[2,64,2048]{2,1,0:T(8,128)(2,1)S(1)}, u32[]{:S(2)}, u32[]{:S(2)}) collective-permute-start(bf16[2,64,2048]{2,1,0:T(8,128)(2,1)S(1)} %copy-done.19), channel_id=1, source_target_pairs={{0,3},{1,0},{2,1},{3,2},{4,7},{5,4},{6,5},{7,6},{8,11},{9,8},{10,9... | collective-permute-start | bytes 1572872 | tf_op jit(solution)/shard_map/ppermute | solution.py:28
  139.0 1.7 add_convert_fusion.3
  140.8 2.0 collective-permute-done.18
  142.8 4.0 %collective-permute-start.29 = (bf16[2,64,2048]{2,1,0:T(8,128)(2,1)S(1)}, bf16[2,64,2048]{2,1,0:T(8,128)(2,1)S(1)}, u32[]{:S(2)}, u32[]{:S(2)}) collective-permute-start(bf16[2,64,2048]{2,1,0:T(8,128)(2,1)S(1)} %copy-done.16), channel_id=1, source_target_pairs={{0,3},{1,0},{2,1},{3,2},{4,7},{5,4},{6,5},{7,6},{8,11},{9,8},{10,9... | collective-permute-start | bytes 1572872 | tf_op jit(solution)/shard_map/ppermute | solution.py:28
  146.8 1.6 add_convert_fusion.2
  151.3 13.5 %collective-permute-done.25 = bf16[2,64,2048]{2,1,0:T(8,128)(2,1)S(1)} collective-permute-done((bf16[2,64,2048]{2,1,0:T(8,128)(2,1)S(1)}, bf16[2,64,2048]{2,1,0:T(8,128)(2,1)S(1)}, u32[]{:S(2)}, u32[]{:S(2)}) %collective-permute-start.25) | collective-permute-done | bytes 524320 | tf_op jit(solution)/shard_map/ppermute | solution.py:28
  165.7 6.8 %collective-permute-done.24 = bf16[2,64,2048]{2,1,0:T(8,128)(2,1)S(1)} collective-permute-done((bf16[2,64,2048]{2,1,0:T(8,128)(2,1)S(1)}, bf16[2,64,2048]{2,1,0:T(8,128)(2,1)S(1)}, u32[]{:S(2)}, u32[]{:S(2)}) %collective-permute-start.24) | collective-permute-done | bytes 524320 | tf_op jit(solution)/shard_map/ppermute | solution.py:28
  174.4 11.2 %collective-permute-done.29 = bf16[2,64,2048]{2,1,0:T(8,128)(2,1)S(1)} collective-permute-done((bf16[2,64,2048]{2,1,0:T(8,128)(2,1)S(1)}, bf16[2,64,2048]{2,1,0:T(8,128)(2,1)S(1)}, u32[]{:S(2)}, u32[]{:S(2)}) %collective-permute-start.29) | collective-permute-done | bytes 524320 | tf_op jit(solution)/shard_map/ppermute | solution.py:28
  187.6 6.1 %collective-permute-done.31.refs_7_ = bf16[64,2048]{1,0:T(8,128)(2,1)S(1)} collective-permute-done((bf16[64,2048]{1,0:T(8,128)(2,1)S(1)}, bf16[64,2048]{1,0:T(8,128)(2,1)S(1)}, u32[]{:S(2)}, u32[]{:S(2)}) %collective-permute-start.31) | collective-permute-done | bytes 262176 | tf_op jit(solution)/shard_map/ppermute | solution.py:32
  193.7 2.1 %place.1 = bf16[128,8192]{1,0:T(8,128)(2,1)} custom-call(s32[3]{0:T(128)S(1)} %pad_add_fusion.pos_ref, bf16[64,2048]{1,0:T(8,128)(2,1)S(1)} %get-tuple-element.90.refs_0_, bf16[64,2048]{1,0:T(8,128)(2,1)S(1)} %collective-permute-done.13.refs_1_, bf16[64,2048]{1,0:T(8,128)(2,1)S(1)} %get-tuple-element.88.refs_2_, ...), custom_call_target="tpu_custom_call" | custom-call | tf_op jit(solution)/shard_map/place/pallas_call | solution.py:373
  (104 shorter events, 25.1 us)
Async XLA Ops:
  6.5 73.3 %all-gather.5.cloned.1.call-start = ((), (), s32[]{:S(2)}) async-start(), calls=%async_computation | async-start | bytes 7077888 | tf_op jit(solution)/shard_map/all_gather | solution.py:335
  9.8 15.8 %collective-permute-start.7 = (bf16[512,256]{1,0:T(8,128)(2,1)}, bf16[512,256]{1,0:T(8,128)(2,1)S(1)}, u32[]{:S(2)}, u32[]{:S(2)}) collective-permute-start(bf16[512,256]{1,0:T(8,128)(2,1)} %get-tuple-element.50), channel_id=1, source_target_pairs={{0,4},{1,5},{2,6},{3,7},{4,8},{5,9},{6,10},{7,11},{8,12},{9,13},{1... | collective-permute-start | bytes 786440 | tf_op jit(solution)/shard_map/ppermute | solution.py:24
  12.0 13.6 %collective-permute-start.8 = (bf16[512,256]{1,0:T(8,128)(2,1)}, bf16[512,256]{1,0:T(8,128)(2,1)S(1)}, u32[]{:S(2)}, u32[]{:S(2)}) collective-permute-start(bf16[512,256]{1,0:T(8,128)(2,1)} %get-tuple-element.51), channel_id=1, source_target_pairs={{0,12},{1,13},{2,14},{3,15},{4,0},{5,1},{6,2},{7,3},{8,4},{9,5},{1... | collective-permute-start | bytes 786440 | tf_op jit(solution)/shard_map/ppermute | solution.py:24
  13.5 12.8 %collective-permute-start.9 = (bf16[512,256]{1,0:T(8,128)(2,1)}, bf16[512,256]{1,0:T(8,128)(2,1)S(1)}, u32[]{:S(2)}, u32[]{:S(2)}) collective-permute-start(bf16[512,256]{1,0:T(8,128)(2,1)} %get-tuple-element.52), channel_id=1, source_target_pairs={{0,8},{1,9},{2,10},{3,11},{4,12},{5,13},{6,14},{7,15},{8,0},{9,1},... | collective-permute-start | bytes 786440 | tf_op jit(solution)/shard_map/ppermute | solution.py:24
  27.3 87.8 %all-gather.7.cloned.1.call-start = ((), (), s32[]{:S(2)}) async-start(), calls=%async_computation.1 | async-start | bytes 7077888 | tf_op jit(solution)/shard_map/all_gather | solution.py:335
  30.7 11.5 %collective-permute-start.3 = (f32[16,512]{1,0:T(8,128)S(1)}, f32[16,512]{1,0:T(8,128)S(1)}, u32[]{:S(2)}, u32[]{:S(2)}) collective-permute-start(f32[16,512]{1,0:T(8,128)S(1)} %add_select_fusion.1), channel_id=1, source_target_pairs={{0,96},{16,112},{1,97},{17,113},{2,98},{18,114},{3,99},{19,115},{4... | collective-permute-start | bytes 98312 | tf_op jit(solution)/shard_map/ppermute | solution.py:41
  35.0 7.2 %collective-permute-start.1 = (f32[16,512]{1,0:T(8,128)S(1)}, f32[16,512]{1,0:T(8,128)S(1)}, u32[]{:S(2)}, u32[]{:S(2)}) collective-permute-start(f32[16,512]{1,0:T(8,128)S(1)} %add_select_fusion.1), channel_id=1, source_target_pairs={{0,32},{16,48},{32,64},{48,80},{64,96},{80,112},{1,33},{17,49},{33... | collective-permute-start | bytes 98312 | tf_op jit(solution)/shard_map/ppermute | solution.py:41
  39.4 14.5 %collective-permute-start.21 = (bf16[512,256]{1,0:T(8,128)(2,1)}, bf16[512,256]{1,0:T(8,128)(2,1)S(1)}, u32[]{:S(2)}, u32[]{:S(2)}) collective-permute-start(bf16[512,256]{1,0:T(8,128)(2,1)} %get-tuple-element.69), channel_id=1, source_target_pairs={{0,4},{1,5},{2,6},{3,7},{4,8},{5,9},{6,10},{7,11},{8,12},{9,13},{1... | collective-permute-start | bytes 786440 | tf_op jit(solution)/shard_map/ppermute | solution.py:24
  40.3 13.6 %collective-permute-start.22 = (bf16[512,256]{1,0:T(8,128)(2,1)}, bf16[512,256]{1,0:T(8,128)(2,1)S(1)}, u32[]{:S(2)}, u32[]{:S(2)}) collective-permute-start(bf16[512,256]{1,0:T(8,128)(2,1)} %get-tuple-element.70), channel_id=1, source_target_pairs={{0,12},{1,13},{2,14},{3,15},{4,0},{5,1},{6,2},{7,3},{8,4},{9,5},{1... | collective-permute-start | bytes 786440 | tf_op jit(solution)/shard_map/ppermute | solution.py:24
  42.1 11.8 %collective-permute-start.23 = (bf16[512,256]{1,0:T(8,128)(2,1)}, bf16[512,256]{1,0:T(8,128)(2,1)S(1)}, u32[]{:S(2)}, u32[]{:S(2)}) collective-permute-start(bf16[512,256]{1,0:T(8,128)(2,1)} %get-tuple-element.71), channel_id=1, source_target_pairs={{0,8},{1,9},{2,10},{3,11},{4,12},{5,13},{6,14},{7,15},{8,0},{9,1},... | collective-permute-start | bytes 786440 | tf_op jit(solution)/shard_map/ppermute | solution.py:24
  55.0 19.5 %collective-permute-start.4 = (bf16[4,2,64,512]{3,2,1,0:T(8,128)(2,1)}, bf16[4,2,64,512]{3,2,1,0:T(8,128)(2,1)S(1)}, u32[]{:S(2)}, u32[]{:S(2)}) collective-permute-start(bf16[4,2,64,512]{3,2,1,0:T(8,128)(2,1)} %get-tuple-element.47), channel_id=1, source_target_pairs={{0,4},{1,5},{2,6},{3,7},{4,8},{5,9},{6,10},{7,11},{8,12},{9,13},{1... | collective-permute-start | bytes 1572872 | tf_op jit(solution)/shard_map/ppermute | solution.py:24
  55.9 18.8 %collective-permute-start.5 = (bf16[4,2,64,512]{3,2,1,0:T(8,128)(2,1)}, bf16[4,2,64,512]{3,2,1,0:T(8,128)(2,1)}, u32[]{:S(2)}, u32[]{:S(2)}) collective-permute-start(bf16[4,2,64,512]{3,2,1,0:T(8,128)(2,1)} %get-tuple-element.48), channel_id=1, source_target_pairs={{0,12},{1,13},{2,14},{3,15},{4,0},{5,1},{6,2},{7,3},{8,4},{9,5},{1... | collective-permute-start | bytes 1572872 | tf_op jit(solution)/shard_map/ppermute | solution.py:24
  57.7 22.1 %collective-permute-start.6 = (bf16[4,2,64,512]{3,2,1,0:T(8,128)(2,1)}, bf16[4,2,64,512]{3,2,1,0:T(8,128)(2,1)}, u32[]{:S(2)}, u32[]{:S(2)}) collective-permute-start(bf16[4,2,64,512]{3,2,1,0:T(8,128)(2,1)} %get-tuple-element.49), channel_id=1, source_target_pairs={{0,8},{1,9},{2,10},{3,11},{4,12},{5,13},{6,14},{7,15},{8,0},{9,1},... | collective-permute-start | bytes 1572872 | tf_op jit(solution)/shard_map/ppermute | solution.py:24
  71.8 23.9 %collective-permute-start.14 = (bf16[4,2,64,512]{3,2,1,0:T(8,128)(2,1)}, bf16[4,2,64,512]{3,2,1,0:T(8,128)(2,1)S(1)}, u32[]{:S(2)}, u32[]{:S(2)}) collective-permute-start(bf16[4,2,64,512]{3,2,1,0:T(8,128)(2,1)} %get-tuple-element.62), channel_id=1, source_target_pairs={{0,4},{1,5},{2,6},{3,7},{4,8},{5,9},{6,10},{7,11},{8,12},{9,13},{1... | collective-permute-start | bytes 1572872 | tf_op jit(solution)/shard_map/ppermute | solution.py:24
  71.8 25.5 %collective-permute-start.15 = (bf16[4,2,64,512]{3,2,1,0:T(8,128)(2,1)}, bf16[4,2,64,512]{3,2,1,0:T(8,128)(2,1)S(1)}, u32[]{:S(2)}, u32[]{:S(2)}) collective-permute-start(bf16[4,2,64,512]{3,2,1,0:T(8,128)(2,1)} %get-tuple-element.63), channel_id=1, source_target_pairs={{0,12},{1,13},{2,14},{3,15},{4,0},{5,1},{6,2},{7,3},{8,4},{9,5},{1... | collective-permute-start | bytes 1572872 | tf_op jit(solution)/shard_map/ppermute | solution.py:24
  74.5 27.8 %collective-permute-start.16 = (bf16[4,2,64,512]{3,2,1,0:T(8,128)(2,1)}, bf16[4,2,64,512]{3,2,1,0:T(8,128)(2,1)S(1)}, u32[]{:S(2)}, u32[]{:S(2)}) collective-permute-start(bf16[4,2,64,512]{3,2,1,0:T(8,128)(2,1)} %get-tuple-element.64), channel_id=1, source_target_pairs={{0,8},{1,9},{2,10},{3,11},{4,12},{5,13},{6,14},{7,15},{8,0},{9,1},... | collective-permute-start | bytes 1572872 | tf_op jit(solution)/shard_map/ppermute | solution.py:24
  91.3 34.4 %collective-permute-start.12 = (bf16[2,64,2048]{2,1,0:T(8,128)(2,1)}, bf16[2,64,2048]{2,1,0:T(8,128)(2,1)}, u32[]{:S(2)}, u32[]{:S(2)}) collective-permute-start(bf16[2,64,2048]{2,1,0:T(8,128)(2,1)} %get-tuple-element.59), channel_id=1, source_target_pairs={{0,2},{1,3},{2,0},{3,1},{4,6},{5,7},{6,4},{7,5},{8,10},{9,11},{10,... | collective-permute-start | bytes 1572872 | tf_op jit(solution)/shard_map/ppermute | solution.py:28
  94.9 40.8 %collective-permute-start.11 = (bf16[2,64,2048]{2,1,0:T(8,128)(2,1)}, bf16[2,64,2048]{2,1,0:T(8,128)(2,1)}, u32[]{:S(2)}, u32[]{:S(2)}) collective-permute-start(bf16[2,64,2048]{2,1,0:T(8,128)(2,1)} %get-tuple-element.58), channel_id=1, source_target_pairs={{0,3},{1,0},{2,1},{3,2},{4,7},{5,4},{6,5},{7,6},{8,11},{9,8},{10,9... | collective-permute-start | bytes 1572872 | tf_op jit(solution)/shard_map/ppermute | solution.py:28
  95.7 41.3 %collective-permute-start.10 = (bf16[2,64,2048]{2,1,0:T(8,128)(2,1)}, bf16[2,64,2048]{2,1,0:T(8,128)(2,1)}, u32[]{:S(2)}, u32[]{:S(2)}) collective-permute-start(bf16[2,64,2048]{2,1,0:T(8,128)(2,1)} %get-tuple-element.57), channel_id=1, source_target_pairs={{0,1},{1,2},{2,3},{3,0},{4,5},{5,6},{6,7},{7,4},{8,9},{9,10},{10,1... | collective-permute-start | bytes 1572872 | tf_op jit(solution)/shard_map/ppermute | solution.py:28
  111.1 29.7 %collective-permute-start.19 = (bf16[2,64,2048]{2,1,0:T(8,128)(2,1)}, bf16[2,64,2048]{2,1,0:T(8,128)(2,1)}, u32[]{:S(2)}, u32[]{:S(2)}) collective-permute-start(bf16[2,64,2048]{2,1,0:T(8,128)(2,1)} %get-tuple-element.68), channel_id=1, source_target_pairs={{0,2},{1,3},{2,0},{3,1},{4,6},{5,7},{6,4},{7,5},{8,10},{9,11},{10,... | collective-permute-start | bytes 1572872 | tf_op jit(solution)/shard_map/ppermute | solution.py:28
  114.6 28.2 %collective-permute-start.18 = (bf16[2,64,2048]{2,1,0:T(8,128)(2,1)}, bf16[2,64,2048]{2,1,0:T(8,128)(2,1)}, u32[]{:S(2)}, u32[]{:S(2)}) collective-permute-start(bf16[2,64,2048]{2,1,0:T(8,128)(2,1)} %get-tuple-element.67), channel_id=1, source_target_pairs={{0,3},{1,0},{2,1},{3,2},{4,7},{5,4},{6,5},{7,6},{8,11},{9,8},{10,9... | collective-permute-start | bytes 1572872 | tf_op jit(solution)/shard_map/ppermute | solution.py:28
  125.8 17.0 %collective-permute-start.17 = (bf16[2,64,2048]{2,1,0:T(8,128)(2,1)S(1)}, bf16[2,64,2048]{2,1,0:T(8,128)(2,1)S(1)}, u32[]{:S(2)}, u32[]{:S(2)}) collective-permute-start(bf16[2,64,2048]{2,1,0:T(8,128)(2,1)S(1)} %copy-done.21), channel_id=1, source_target_pairs={{0,1},{1,2},{2,3},{3,0},{4,5},{5,6},{6,7},{7,4},{8,9},{9,10},{10,1... | collective-permute-start | bytes 1572872 | tf_op jit(solution)/shard_map/ppermute | solution.py:28
  135.7 14.3 %collective-permute-start.26 = (bf16[2,64,2048]{2,1,0:T(8,128)(2,1)S(1)}, bf16[2,64,2048]{2,1,0:T(8,128)(2,1)S(1)}, u32[]{:S(2)}, u32[]{:S(2)}) collective-permute-start(bf16[2,64,2048]{2,1,0:T(8,128)(2,1)S(1)} %copy-done.20), channel_id=1, source_target_pairs={{0,2},{1,3},{2,0},{3,1},{4,6},{5,7},{6,4},{7,5},{8,10},{9,11},{10,... | collective-permute-start | bytes 1572872 | tf_op jit(solution)/shard_map/ppermute | solution.py:28
  137.0 27.8 %collective-permute-start.25 = (bf16[2,64,2048]{2,1,0:T(8,128)(2,1)S(1)}, bf16[2,64,2048]{2,1,0:T(8,128)(2,1)S(1)}, u32[]{:S(2)}, u32[]{:S(2)}) collective-permute-start(bf16[2,64,2048]{2,1,0:T(8,128)(2,1)S(1)} %copy-done.19), channel_id=1, source_target_pairs={{0,3},{1,0},{2,1},{3,2},{4,7},{5,4},{6,5},{7,6},{8,11},{9,8},{10,9... | collective-permute-start | bytes 1572872 | tf_op jit(solution)/shard_map/ppermute | solution.py:28
  140.8 31.7 %collective-permute-start.24 = (bf16[2,64,2048]{2,1,0:T(8,128)(2,1)S(1)}, bf16[2,64,2048]{2,1,0:T(8,128)(2,1)S(1)}, u32[]{:S(2)}, u32[]{:S(2)}) collective-permute-start(bf16[2,64,2048]{2,1,0:T(8,128)(2,1)S(1)} %copy-done.18), channel_id=1, source_target_pairs={{0,1},{1,2},{2,3},{3,0},{4,5},{5,6},{6,7},{7,4},{8,9},{9,10},{10,1... | collective-permute-start | bytes 1572872 | tf_op jit(solution)/shard_map/ppermute | solution.py:28
  142.8 30.6 %collective-permute-start.30 = (bf16[2,64,2048]{2,1,0:T(8,128)(2,1)S(1)}, bf16[2,64,2048]{2,1,0:T(8,128)(2,1)S(1)}, u32[]{:S(2)}, u32[]{:S(2)}) collective-permute-start(bf16[2,64,2048]{2,1,0:T(8,128)(2,1)S(1)} %copy-done.17), channel_id=1, source_target_pairs={{0,2},{1,3},{2,0},{3,1},{4,6},{5,7},{6,4},{7,5},{8,10},{9,11},{10,... | collective-permute-start | bytes 1572872 | tf_op jit(solution)/shard_map/ppermute | solution.py:28
  142.8 42.8 %collective-permute-start.29 = (bf16[2,64,2048]{2,1,0:T(8,128)(2,1)S(1)}, bf16[2,64,2048]{2,1,0:T(8,128)(2,1)S(1)}, u32[]{:S(2)}, u32[]{:S(2)}) collective-permute-start(bf16[2,64,2048]{2,1,0:T(8,128)(2,1)S(1)} %copy-done.16), channel_id=1, source_target_pairs={{0,3},{1,0},{2,1},{3,2},{4,7},{5,4},{6,5},{7,6},{8,11},{9,8},{10,9... | collective-permute-start | bytes 1572872 | tf_op jit(solution)/shard_map/ppermute | solution.py:28
  150.0 36.5 %collective-permute-start.28 = (bf16[2,64,2048]{2,1,0:T(8,128)(2,1)S(1)}, bf16[2,64,2048]{2,1,0:T(8,128)(2,1)S(1)}, u32[]{:S(2)}, u32[]{:S(2)}) collective-permute-start(bf16[2,64,2048]{2,1,0:T(8,128)(2,1)S(1)} %copy-done.15), channel_id=1, source_target_pairs={{0,1},{1,2},{2,3},{3,0},{4,5},{5,6},{6,7},{7,4},{8,9},{9,10},{10,1... | collective-permute-start | bytes 1572872 | tf_op jit(solution)/shard_map/ppermute | solution.py:28
  164.8 22.8 %collective-permute-start.13 = (bf16[64,2048]{1,0:T(8,128)(2,1)S(1)}, bf16[64,2048]{1,0:T(8,128)(2,1)S(1)}, u32[]{:S(2)}, u32[]{:S(2)}) collective-permute-start(bf16[64,2048]{1,0:T(8,128)(2,1)S(1)} %get-tuple-element.89), channel_id=1, source_target_pairs={{0,4},{1,5},{2,6},{3,7},{4,0},{5,1},{6,2},{7,3},{8,12},{9,13},{10,... | collective-permute-start | bytes 786440 | tf_op jit(solution)/shard_map/ppermute | solution.py:32
  172.5 15.2 %collective-permute-start.20 = (bf16[64,2048]{1,0:T(8,128)(2,1)S(1)}, bf16[64,2048]{1,0:T(8,128)(2,1)S(1)}, u32[]{:S(2)}, u32[]{:S(2)}) collective-permute-start(bf16[64,2048]{1,0:T(8,128)(2,1)S(1)} %get-tuple-element.87), channel_id=1, source_target_pairs={{0,4},{1,5},{2,6},{3,7},{4,0},{5,1},{6,2},{7,3},{8,12},{9,13},{10,... | collective-permute-start | bytes 786440 | tf_op jit(solution)/shard_map/ppermute | solution.py:32
  173.5 14.2 %collective-permute-start.27 = (bf16[64,2048]{1,0:T(8,128)(2,1)S(1)}, bf16[64,2048]{1,0:T(8,128)(2,1)S(1)}, u32[]{:S(2)}, u32[]{:S(2)}) collective-permute-start(bf16[64,2048]{1,0:T(8,128)(2,1)S(1)} %get-tuple-element.85), channel_id=1, source_target_pairs={{0,4},{1,5},{2,6},{3,7},{4,0},{5,1},{6,2},{7,3},{8,12},{9,13},{10,... | collective-permute-start | bytes 786440 | tf_op jit(solution)/shard_map/ppermute | solution.py:32
  186.9 6.9 %collective-permute-start.31 = (bf16[64,2048]{1,0:T(8,128)(2,1)S(1)}, bf16[64,2048]{1,0:T(8,128)(2,1)S(1)}, u32[]{:S(2)}, u32[]{:S(2)}) collective-permute-start(bf16[64,2048]{1,0:T(8,128)(2,1)S(1)} %get-tuple-element.83), channel_id=1, source_target_pairs={{0,4},{1,5},{2,6},{3,7},{4,0},{5,1},{6,2},{7,3},{8,12},{9,13},{10,... | collective-permute-start | bytes 786440 | tf_op jit(solution)/shard_map/ppermute | solution.py:32
  (24 other events, 244.6 us)
Sparse Core Ops, SparseCore 0:
  27.4 42.9 all-gather.4
  72.1 40.9 all-gather.6

commit v4 on v3

--- a/solution.py
+++ b/solution.py
@@ -8,16 +8,22 @@
 from jax.sharding import PartitionSpec as P
 
 POLES = 16
+PAD = 8
 LANES = 128
 NX, NCORE, NY, NZ = 4, 2, 4, 4
 STEPS = (1, -1, 2)
 ROW_PARTS = (1, 1)
 COL_PARTS = (1, 1)
 TILES = (((0,), (0,)), ((1,), (0,)), ((0,), (1,)), ((1,), (1,)))
+OFFLOADED = ()
 HBM = pl.BlockSpec(memory_space=pltpu.HBM)
 SMEM = pl.BlockSpec(memory_space=pltpu.SMEM)
 VMEM = pl.BlockSpec(memory_space=pltpu.VMEM)
-LIMIT = pltpu.CompilerParams(vmem_limit_bytes=48 * 1024 * 1024)
+LIMIT = pltpu.CompilerParams(vmem_limit_bytes=60 * 1024 * 1024)
+
+
+def work(us):
+    return pl.CostEstimate(flops=us * 1_150_000_000, bytes_accessed=0, transcendentals=0)
 
 
 def over_y(value, step):
@@ -44,7 +50,9 @@
 def state_kernel(k_ref, v_ref, rate_ref, excl_ref, span_ref, drive, fb, *, T, unroll):
     W = k_ref.shape[-1]
     nO = k_ref.shape[0]
-    drive[...] = (k_ref[...].astype(jnp.float32) * v_ref[...].astype(jnp.float32)).reshape(nO*T, W)
+    PT = T + PAD
+    for o in range(nO):
+        drive[pl.ds(o*PT, T), :] = k_ref[o].astype(jnp.float32) * v_ref[o].astype(jnp.float32)
     rate = rate_ref[...]
     f = jnp.exp(-rate)
     for r in range(POLES):
@@ -59,7 +67,7 @@
         s = [list(x) for x in s]
         for j in range(unroll):
             for p in range(G):
-                u = drive[pl.ds(p*8*T + i*unroll + j, 8, stride=T), :]
+                u = drive[pl.ds(p*8*PT + i*unroll + j, 8, stride=PT), :]
                 for r in range(POLES):
                     s[p][r] = fr[r]*s[p][r] + u
         return tuple(tuple(x) for x in s)
@@ -83,7 +91,7 @@
         spans.append(carry)
     span_ref[...] = jnp.concatenate(spans, axis=0)
 
-def states(k3, v3, rate, unroll=4):
+def states(k3, v3, rate, unroll=16):
     nO,T,C = k3.shape
     W=128
     return pl.pallas_call(
@@ -93,7 +101,9 @@
                   pl.BlockSpec((POLES,W), lambda c:(0,c))],
         out_specs=[pl.BlockSpec((POLES,nO,W), lambda c:(0,0,c)), pl.BlockSpec((POLES,W), lambda c:(0,c))],
         out_shape=[jax.ShapeDtypeStruct((POLES,nO,C), jnp.float32), jax.ShapeDtypeStruct((POLES,C), jnp.float32)],
-        scratch_shapes=[pltpu.VMEM((nO*T,W), jnp.float32), pltpu.VMEM((POLES,8,W), jnp.float32)],
+        scratch_shapes=[pltpu.VMEM((nO*(T+PAD),W), jnp.float32), pltpu.VMEM((POLES,8,W), jnp.float32)],
+        compiler_params=LIMIT,
+        cost_estimate=work(8),
         name="states",
     )(k3, v3, rate)
 
@@ -105,7 +115,9 @@
     state_ref = None if last else rest[4]
     drive, y, fb, rb, mixed = rest[4 if last else 5:]
     nO, T, W = k_ref.shape
-    drive[...] = (k_ref[...].astype(jnp.float32) * v_ref[...].astype(jnp.float32)).reshape(nO * T, W)
+    PT = T + PAD
+    for o in range(nO):
+        drive[pl.ds(o * PT, T), :] = k_ref[o].astype(jnp.float32) * v_ref[o].astype(jnp.float32)
     rate = rate_ref[...]
     f = jnp.exp(-rate)
     for r in range(POLES):
@@ -126,7 +138,7 @@
         s = [list(x) for x in s]
         for j in range(unroll):
             t = i * unroll + j
-            us = [drive[pl.ds(p * 8 * T + t, 8, stride=T), :] for p in range(G)]
+            us = [drive[pl.ds(p * 8 * PT + t, 8, stride=PT), :] for p in range(G)]
             acc = [[rb[POLES] * us[p], None] for p in range(G)]
             for r in range(POLES):
                 rr = rb[r]
@@ -135,7 +147,7 @@
                     m = rr * s[p][r]
                     acc[p][r % 2] = m if acc[p][r % 2] is None else acc[p][r % 2] + m
             for p in range(G):
-                y[pl.ds(p * 8 * T + t, 8, stride=T), :] = acc[p][0] + acc[p][1]
+                y[pl.ds(p * 8 * PT + t, 8, stride=PT), :] = acc[p][0] + acc[p][1]
         return tuple(tuple(x) for x in s)
 
     s = lax.fori_loop(0, T // unroll, body, tuple(tuple(begin(p, r) for r in range(POLES)) for p in range(G)))
@@ -143,7 +155,8 @@
         for p in range(G):
             for r in range(POLES):
                 state_ref[r, pl.ds(p * 8, 8), :] = s[p][r]
-    mixed[...] = (q_ref[...].astype(jnp.float32) * y[...].reshape(nO, T, W)).astype(jnp.bfloat16)
+    for o in range(nO):
+        mixed[o] = (q_ref[o].astype(jnp.float32) * y[pl.ds(o * PT, T), :]).astype(jnp.bfloat16)
     my_y, my_z = pos_ref[0], pos_ref[1]
     for out_ref, step in zip(outs, (0,) + STEPS):
         half = lax.rem(my_y + step + NY, NY) // 2
@@ -172,20 +185,20 @@
         out_shape = out_shape + [jax.ShapeDtypeStruct((POLES, nO, C), jnp.float32)]
         out_specs = out_specs + [st]
     res = pl.pallas_call(
-        functools.partial(conv_kernel, unroll=4, per=T, first=first, last=last),
+        functools.partial(conv_kernel, unroll=16, per=T, first=first, last=last),
         grid=(C // W,),
         in_specs=specs,
         out_specs=out_specs,
         out_shape=out_shape,
         scratch_shapes=[
-            pltpu.VMEM((nO * tc, W), jnp.float32),
-            pltpu.VMEM((nO * tc, W), jnp.float32),
+            pltpu.VMEM((nO * (tc + PAD), W), jnp.float32),
+            pltpu.VMEM((nO * (tc + PAD), W), jnp.float32),
             pltpu.VMEM((POLES, 8, W), jnp.float32),
             pltpu.VMEM((POLES + 1, 8, W), jnp.float32),
             pltpu.VMEM((nO, tc, W), jnp.bfloat16),
         ],
         compiler_params=LIMIT,
-        cost_estimate=pl.CostEstimate(flops=nO * tc * C * POLES * 4, bytes_accessed=nO * tc * C * 10, transcendentals=0),
+        cost_estimate=work(8),
         name="conv",
     )(*ops)
     return res[:4], (None if last else res[4])
@@ -214,7 +227,7 @@
         functools.partial(share_kernel, widths=widths, offsets=offsets, half_cols=half_cols),
         in_specs=[SMEM, HBM],
         out_specs=[VMEM] * n,
-        out_shape=[pltpu.HBM((k, w), weight.dtype) for w in widths for _ in STEPS],
+        out_shape=[jax.ShapeDtypeStruct((k, w), weight.dtype) for w in widths for _ in STEPS],
         scratch_shapes=[pltpu.SemaphoreType.DMA((n,))],
         compiler_params=LIMIT,
         name="weight_shares",
@@ -222,11 +235,12 @@
     return [out[g * len(STEPS):(g + 1) * len(STEPS)] for g in range(len(widths))]
 
 
-def tile_kernel(pos_ref, w_ref, *refs, row_sizes, cols, offsets, half_cols, block):
+def tile_kernel(pos_ref, w_ref, *refs, row_sizes, cols, offsets, half_cols, block, split):
     nr, nc = len(row_sizes), len(cols)
     a_refs, b_refs = refs[:4 * nr], refs[4 * nr:4 * nr + nc]
-    outs = refs[4 * nr + nc:4 * nr + nc + NZ]
-    a_v, b_v, sem_a, sem_b, sem_w = refs[4 * nr + nc + NZ:]
+    n_out = 1 if split else NZ
+    outs = refs[4 * nr + nc:4 * nr + nc + n_out]
+    a_v, b_v, out_v, sem_a, sem_b, sem_w, sem_out = refs[4 * nr + nc + n_out:]
     width = w_ref.shape[0]
     total = sum(row_sizes)
     a_copies = []
@@ -236,9 +250,7 @@
             dst = a_v.at[:, :, pl.ds(start, tc), pl.ds(d * width, width)]
             a_copies.append(pltpu.make_async_copy(a_refs[4 * i + d], dst, sem_a.at[4 * i + d]))
         start += tc
-    for c in a_copies:
-        c.start()
-    waits = []
+    blocks = []
     base = 0
     n = 0
     for g, (size, offset) in enumerate(zip(cols, offsets)):
@@ -253,44 +265,67 @@
                 here.append(pltpu.make_async_copy(
                     b_refs[g].at[s], b_v.at[pl.ds(width, 3 * width), pl.ds(base + s * piece, piece)], sem_b.at[n]))
                 n += 1
-            for c in here:
+            blocks.append(here)
+        base += size
+
+    def begin(nb):
+        if nb < len(blocks):
+            for c in blocks[nb]:
                 c.start()
-            waits.append(here)
-        base += size
+
+    for c in a_copies:
+        c.start()
+    begin(0)
     for c in a_copies:
         c.wait()
+    begin(1)
+    begin(2)
+    out_copies = []
     a = a_v[...].reshape(NZ * 2 * total, 4 * width)
-    for nb, here in enumerate(waits):
+    for nb, here in enumerate(blocks):
         for c in here:
             c.wait()
+        begin(nb + 3)
         at = pl.ds(nb * block, block)
         part = jnp.dot(a, b_v[:, at], preferred_element_type=jnp.float32).astype(jnp.bfloat16)
-        part = part.reshape(NZ, 2, total, block)
+        out_v[:, :, :, at] = part.reshape(NZ, 2, total, block)
         for zr in range(NZ):
-            outs[zr][:, :, at] = part[zr]
-
-
-def tile(pos, weight, a_parts, b_parts, cols, offsets, half_cols):
+            pairs = []
+            for i in range(2):
+                src = out_v.at[zr, lax.rem(pos_ref[0] + 1 + i, 2), :, at]
+                dst = outs[0].at[lax.rem(pos_ref[1] + zr, NZ), i, :, at] if split else outs[zr].at[i, :, at]
+                pairs.append((src, dst))
+            for src, dst in pairs:
+                c = pltpu.make_async_copy(src, dst, sem_out.at[len(out_copies)])
+                c.start()
+                out_copies.append(c)
+    for c in out_copies:
+        c.wait()
+
+
+def tile(pos, weight, a_parts, b_parts, cols, offsets, half_cols, split):
     width = weight.shape[0]
     row_sizes = tuple(a[0].shape[2] for a in a_parts)
     total, n = sum(row_sizes), sum(cols)
     block = 512
     flat = [piece for a in a_parts for piece in a]
+    outs = [pltpu.HBM((NZ, 2, total, n), jnp.bfloat16)] if split else [pltpu.HBM((2, total, n), jnp.bfloat16)] * NZ
     return pl.pallas_call(
-        functools.partial(tile_kernel, row_sizes=row_sizes, cols=cols, offsets=offsets, half_cols=half_cols, block=block),
+        functools.partial(tile_kernel, row_sizes=row_sizes, cols=cols, offsets=offsets, half_cols=half_cols, block=block, split=split),
         in_specs=[SMEM, HBM] + [HBM] * (len(flat) + len(b_parts)),
-        out_specs=[VMEM] * NZ,
-        out_shape=[pltpu.HBM((2, total, n), jnp.bfloat16)] * NZ,
+        out_specs=[HBM] * len(outs),
+        out_shape=outs,
         scratch_shapes=[
             pltpu.VMEM((NZ, 2, total, 4 * width), jnp.bfloat16),
             pltpu.VMEM((4 * width, n), jnp.bfloat16),
+            pltpu.VMEM((NZ, 2, total, n), jnp.bfloat16),
             pltpu.SemaphoreType.DMA((len(flat),)),
             pltpu.SemaphoreType.DMA((NX * NCORE * len(cols),)),
             pltpu.SemaphoreType.DMA((n // block,)),
+            pltpu.SemaphoreType.DMA((n // block * 2 * NZ,)),
         ],
         compiler_params=LIMIT,
-        cost_estimate=pl.CostEstimate(
-            flops=2 * NZ * 2 * total * 4 * width * n, bytes_accessed=4 * width * n * 2 + NZ * 2 * total * n * 4, transcendentals=0),
+        cost_estimate=work(9),
         name="tile",
     )(pos, weight, *flat, *b_parts)
 
@@ -300,13 +335,24 @@
     ins, out, sems = refs[:n], refs[n], refs[n + 1]
     copies = []
     for i, (other, row, rows, col, cols) in enumerate(places):
-        half = lax.rem(pos_ref[0] + other, 2)
-        at = pl.multiple_of(half * half_cols + col, LANES)
+        at = pl.multiple_of(lax.rem(pos_ref[0] + other, 2) * half_cols + col, LANES)
         copies.append(pltpu.make_async_copy(ins[i], out.at[pl.ds(row, rows), pl.ds(at, cols)], sems.at[i]))
     for c in copies:
         c.start()
     for c in copies:
         c.wait()
+
+
+def place(pos, pieces, places, shape, half_cols):
+    return pl.pallas_call(
+        functools.partial(place_kernel, places=tuple(places), half_cols=half_cols),
+        in_specs=[SMEM] + [pl.BlockSpec(memory_space=pl.ANY)] * len(pieces),
+        out_specs=VMEM,
+        out_shape=jax.ShapeDtypeStruct(shape, jnp.bfloat16),
+        scratch_shapes=[pltpu.SemaphoreType.DMA((len(pieces),))],
+        compiler_params=pltpu.CompilerParams(vmem_limit_bytes=32 * 1024 * 1024),
+        name="place",
+    )(pos, *pieces)
 
 
 def local(query_proj, key_proj, value_proj, pole_rate, pole_residue, skip_gain, out_weight):
@@ -328,6 +374,7 @@
     fetched = [[over_y(piece, step) for piece, step in zip(group, STEPS)] for group in shares]
 
     q3, k3, v3 = [x.reshape(owners, per, width) for x in (query_proj, key_proj, value_proj)]
+    k3 = lax.optimization_barrier((k3, shares[0][0]))[0]
     excl, span = states(k3, v3, pole_rate)
 
     def gathered(group, after):
@@ -354,31 +401,33 @@
         mixed.append([sent[0]] + [over_y(piece, step) for piece, step in zip(sent[1:], STEPS)])
         start += tc
 
+    def reduced(part):
+        arrived = [part[0]] + [over_z(part[step % NZ], step) for step in STEPS]
+        return sum(p.astype(jnp.float32) for p in arrived).astype(jnp.bfloat16)
+
     pieces, places = [], []
-    parity = my_y % 2
-    for row_set, col_set in TILES:
+    for k, (row_set, col_set) in enumerate(TILES):
+        split = k in OFFLOADED
+        weight = out_weight
+        if k:
+            weight = lax.optimization_barrier((weight, part[0]))[0]
         part = tile(
-            pos, out_weight, [mixed[i] for i in row_set], [weights[g] for g in col_set],
-            tuple(cols[g] for g in col_set), tuple(offsets[g] for g in col_set), half_cols)
-        arrived = [part[0]] + [over_z(part[step % NZ], step) for step in STEPS]
-        summed = sum(p.astype(jnp.float32) for p in arrived).astype(jnp.bfloat16)
-        keep = lax.dynamic_index_in_dim(summed, parity, 0, keepdims=False)
-        send = lax.dynamic_index_in_dim(summed, 1 - parity, 0, keepdims=False)
+            pos, weight, [mixed[i] for i in row_set], [weights[g] for g in col_set],
+            tuple(cols[g] for g in col_set), tuple(offsets[g] for g in col_set), half_cols, split)
+        if split:
+            flat = part[0].reshape(-1, part[0].shape[-1])
+            groups = [[y * NZ + z for z in range(NZ)] for y in range(NY)]
+            flat = lax.psum_scatter(flat, "chan", scatter_dimension=0, axis_index_groups=groups, tiled=True)
+            send, keep = flat.reshape(part[0].shape[1:])
+        else:
+            send, keep = reduced(part)
         row = sum(tcs[:row_set[0]])
         size = sum(tcs[i] for i in row_set)
         col = offsets[col_set[0]]
         n = sum(cols[g] for g in col_set)
         pieces += [keep, with_partner(send)]
         places += [(0, row, size, col, n), (1, row, size, col, n)]
-    return pl.pallas_call(
-        functools.partial(place_kernel, places=tuple(places), half_cols=half_cols),
-        in_specs=[SMEM] + [HBM] * len(pieces),
-        out_specs=VMEM,
-        out_shape=jax.ShapeDtypeStruct((per, total_cols), jnp.bfloat16),
-        scratch_shapes=[pltpu.SemaphoreType.DMA((len(pieces),))],
-        compiler_params=LIMIT,
-        name="place",
-    )(pos, *pieces)
+    return place(pos, pieces, places, (per, total_cols), half_cols)
 
 
 def solution(mesh):

time: 205 us -> 202 us (0.985)
  waiting for transfers between devices: 54 us -> 66.9 us
  Pallas kernels: 75.3 us -> 65.5 us
  local copies, waits for them, and re-layouts: 4.5 us -> 1.82 us
  other arithmetic: 6.76 us -> 4.49 us
    ppermute x12, waiting for transfers between devices: 11 us -> 22.2 us  [over_y(): lax.ppermute(value, 'chan', [(y * NZ + z, (y + step) % NY * NZ + z) for y...]
    pallas_call x3, Pallas kernels: 21.9 us -> 17.4 us  [the longest x2 15.3 us: conv_chunk(): pl.pallas_call(functools.partial(conv_kernel, unroll=16, per=T, first=fir...]
    ppermute x4, starting transfers between devices: 3.17 us -> 6.18 us  [with_partner(): lax.ppermute(value, 'chan', [(y * NZ + z, (y ^ 1) * NZ + z) for y in rang...]
    pallas_call x1, Pallas kernels: 10.5 us -> 7.63 us  [states(): pl.pallas_call(functools.partial(state_kernel, T=T, unroll=unroll), grid=...]
    unnamed x44 -> x42, local copies, waits for them, and re-layouts: 4.31 us -> 1.67 us
    convert_element_type x4, other arithmetic: 3.94 us -> 1.34 us  [reduced(): return sum((p.astype(jnp.float32) for p in arrived)).astype(jnp.bfloat16)]
    pallas_call x4, Pallas kernels: 39.7 us -> 37.1 us  [tile(): pl.pallas_call(functools.partial(tile_kernel, row_sizes=row_sizes, cols=c...]
    ppermute x12, starting transfers between devices: 19.5 us -> 17.4 us  [over_z(): lax.ppermute(value, 'chan', [(y * NZ + z, y * NZ + (z + step) % NZ) for y...]
  transfers between devices with their start and end apart: 34 -> 34, of which waited for: 12 -> 13; matrix products, arithmetic and copies ran while one was open for 3% -> 2% of each run, Pallas kernels for 35% -> 30%
where the time goes in v4:
time: 202 us; the launch traced here: 201 us
  waiting for transfers between devices  66.9 us (33%)
  Pallas kernels  65.5 us (32%)
  starting transfers between devices  48.8 us (24%)
  between operations  13.8 us (7%)
  other arithmetic  4.49 us (2%)
    ppermute x12, waiting for transfers between devices, over_z(): lax.ppermute(value, 'chan', [(y * NZ + z, y * NZ + (z + step) % NZ) for y...  37.7 us
    pallas_call x4, Pallas kernels, tile(): pl.pallas_call(functools.partial(tile_kernel, row_sizes=row_sizes, cols=c...  37.1 us
    ppermute x12, waiting for transfers between devices, over_y(): lax.ppermute(value, 'chan', [(y * NZ + z, (y + step) % NY * NZ + z) for y...  22.2 us
    ppermute x12, starting transfers between devices, over_z(): lax.ppermute(value, 'chan', [(y * NZ + z, y * NZ + (z + step) % NZ) for y...  17.4 us
    pallas_call x2, Pallas kernels, conv_chunk(): pl.pallas_call(functools.partial(conv_kernel, unroll=16, per=T, first=fir...  15.3 us
    ppermute x12, starting transfers between devices, over_y(): lax.ppermute(value, 'chan', [(y * NZ + z, (y + step) % NY * NZ + z) for y...  15 us
    ppermute x3, starting transfers between devices, from_chip_behind(): return lax.ppermute(value, 'seq', pairs)  8.69 us
    pallas_call x1, Pallas kernels, states(): pl.pallas_call(functools.partial(state_kernel, T=T, unroll=unroll), grid=...  7.63 us
  transfers between devices with their start and end apart: 34, of which 13 were waited for; matrix products, arithmetic and copies ran while one was open for 2% of the time, Pallas kernels for 30%

profile of v4, /device:TPU:1, one launch (start us, length us, event | category | flops | bytes accessed | tf_op | source)
XLA Modules:
  0.0 201.3 jit_solution(12564015838172051100)
XLA Ops:
  7.2 3.4 %weight_shares.1 = (bf16[512,256]{1,0:T(8,128)(2,1)}, bf16[512,256]{1,0:T(8,128)(2,1)}, bf16[512,256]{1,0:T(8,128)(2,1)}, bf16[512,256]{1,0:T(8,128)(2,1)}, bf16...) custom-call(s32[3]{0:T(128)} %pad_add_fusion.pos_ref, bf16[512,8192]{1,0:T(8,128)(2,1)} %w_ref.6), custom_call_target="tpu_custom_call" | custom-call | tf_op jit(solution)/shard_map/weight_shares/pallas_call | solution.py:226
  10.5 2.2 %collective-permute-start.7 = (bf16[512,256]{1,0:T(8,128)(2,1)}, bf16[512,256]{1,0:T(8,128)(2,1)S(1)}, u32[]{:S(2)}, u32[]{:S(2)}) collective-permute-start(bf16[512,256]{1,0:T(8,128)(2,1)} %get-tuple-element.48), channel_id=1, source_target_pairs={{0,4},{1,5},{2,6},{3,7},{4,8},{5,9},{6,10},{7,11},{8,12},{9,13},{1... | collective-permute-start | bytes 786440 | tf_op jit(solution)/shard_map/ppermute | solution.py:30
  12.7 1.5 collective-permute-start.8
  14.3 1.5 collective-permute-start.9
  15.8 7.6 %states.1 = (f32[16,16,512]{2,1,0:T(8,128)}, f32[16,512]{1,0:T(8,128)}) custom-call(bf16[16,128,512]{2,1,0:T(8,128)(2,1)} %bitcast.31, bf16[16,128,512]{2,1,0:T(8,128)(2,1)} %bitcast.34, f32[16,512]{1,0:T(8,128)} %rate_ref.5), custom_call_target="tpu_custom_call" | custom-call | flops 9200000000 | tf_op jit(solution)/shard_map/states/pallas_call | solution.py:97
  23.5 3.5 %collective-permute-done.9 = bf16[512,256]{1,0:T(8,128)(2,1)S(1)} collective-permute-done((bf16[512,256]{1,0:T(8,128)(2,1)}, bf16[512,256]{1,0:T(8,128)(2,1)S(1)}, u32[]{:S(2)}, u32[]{:S(2)}) %collective-permute-start.9) | collective-permute-done | bytes 262176 | tf_op jit(solution)/shard_map/ppermute | solution.py:30
  30.4 4.3 %collective-permute-start.3 = (f32[16,512]{1,0:T(8,128)S(1)}, f32[16,512]{1,0:T(8,128)S(1)}, u32[]{:S(2)}, u32[]{:S(2)}) collective-permute-start(f32[16,512]{1,0:T(8,128)S(1)} %add_select_fusion.1), channel_id=1, source_target_pairs={{0,96},{16,112},{1,97},{17,113},{2,98},{18,114},{3,99},{19,115},{4... | collective-permute-start | bytes 98312 | tf_op jit(solution)/shard_map/ppermute | solution.py:47
  36.0 3.1 %collective-permute-start.2 = (f32[16,512]{1,0:T(8,128)S(1)}, f32[16,512]{1,0:T(8,128)S(1)}, u32[]{:S(2)}, u32[]{:S(2)}) collective-permute-start(f32[16,512]{1,0:T(8,128)S(1)} %add_select_fusion.1), channel_id=1, source_target_pairs={{0,64},{16,80},{32,96},{48,112},{1,65},{17,81},{33,97},{49,113},{2... | collective-permute-start | bytes 98312 | tf_op jit(solution)/shard_map/ppermute | solution.py:47
  40.1 1.8 collective-permute-start.22
  42.7 7.7 %conv.2 = (bf16[4,2,64,512]{3,2,1,0:T(8,128)(2,1)}, bf16[4,2,64,512]{3,2,1,0:T(8,128)(2,1)}, bf16[4,2,64,512]{3,2,1,0:T(8,128)(2,1)}, bf16[4,2,64,512]{3,2,1,0:T(8,128)(2,1)}, f32[16,16,512]{2,1,0:T(8,128)}) custom-call(s32[3]{0:T(128)} %pad_add_fusion.pos_ref, bf16[16,128,512]{2,1,0:T(8,128)(2,1)} %bitcast.29, bf16[16,128,512]{2,1,0:T(8,128)(2,1)} %bitcast.32, ...), custom_call_target="tpu_custom_call" | custom-call | flops 9200000000 | tf_op jit(solution)/shard_map/conv/pallas_call | solution.py:187
  50.5 2.5 %collective-permute-done.23 = bf16[512,256]{1,0:T(8,128)(2,1)S(1)} collective-permute-done((bf16[512,256]{1,0:T(8,128)(2,1)S(1)}, bf16[512,256]{1,0:T(8,128)(2,1)S(1)}, u32[]{:S(2)}, u32[]{:S(2)}) %collective-permute-start.23) | collective-permute-done | bytes 262176 | tf_op jit(solution)/shard_map/ppermute | solution.py:30
  54.7 2.0 collective-permute-start.5
  57.0 7.5 %conv.3 = (bf16[4,2,64,512]{3,2,1,0:T(8,128)(2,1)}, bf16[4,2,64,512]{3,2,1,0:T(8,128)(2,1)}, bf16[4,2,64,512]{3,2,1,0:T(8,128)(2,1)}, bf16[4,2,64,512]{3,2,1,0:T(8,128)(2,1)}) custom-call(s32[3]{0:T(128)} %pad_add_fusion.pos_ref, bf16[16,128,512]{2,1,0:T(8,128)(2,1)} %bitcast.30, bf16[16,128,512]{2,1,0:T(8,128)(2,1)} %bitcast.33, ...), custom_call_target="tpu_custom_call" | custom-call | flops 9200000000 | tf_op jit(solution)/shard_map/conv/pallas_call | solution.py:187
  65.5 1.7 collective-permute-start.15
  68.8 8.7 %collective-permute-done.6.refs_3_ = bf16[4,2,64,512]{3,2,1,0:T(8,128)(2,1)S(1)} collective-permute-done((bf16[4,2,64,512]{3,2,1,0:T(8,128)(2,1)}, bf16[4,2,64,512]{3,2,1,0:T(8,128)(2,1)S(1)}, u32[]{:S(2)}, u32[]{:S(2)}) %collective-permute-start.6) | collective-permute-done | bytes 524320 | tf_op jit(solution)/shard_map/ppermute | solution.py:30
  78.3 9.3 %tile.4 = (bf16[2,64,2048]{2,1,0:T(8,128)(2,1)}, bf16[2,64,2048]{2,1,0:T(8,128)(2,1)}, bf16[2,64,2048]{2,1,0:T(8,128)(2,1)}, bf16[2,64,2048]{2,1,0:T(8,128)(2,1)}) custom-call(s32[3]{0:T(128)} %pad_add_fusion.pos_ref, bf16[512,8192]{1,0:T(8,128)(2,1)} %w_ref.6, bf16[4,2,64,512]{3,2,1,0:T(8,128)(2,1)} %get-tuple-element.52.refs_0_, ...), custom_call_target="tpu_custom_call" | custom-call | flops 10350000128 | tf_op jit(solution)/shard_map/tile/pallas_call | solution.py:313
  87.6 3.7 %collective-permute-start.12 = (bf16[2,64,2048]{2,1,0:T(8,128)(2,1)}, bf16[2,64,2048]{2,1,0:T(8,128)(2,1)S(1)}, u32[]{:S(2)}, u32[]{:S(2)}) collective-permute-start(bf16[2,64,2048]{2,1,0:T(8,128)(2,1)} %get-tuple-element.64), channel_id=1, source_target_pairs={{0,2},{1,3},{2,0},{3,1},{4,6},{5,7},{6,4},{7,5},{8,10},{9,11},{10,... | collective-permute-start | bytes 1572872 | tf_op jit(solution)/shard_map/ppermute | solution.py:34
  93.0 7.0 %collective-permute-done.16.refs_3_ = bf16[4,2,64,512]{3,2,1,0:T(8,128)(2,1)S(1)} collective-permute-done((bf16[4,2,64,512]{3,2,1,0:T(8,128)(2,1)}, bf16[4,2,64,512]{3,2,1,0:T(8,128)(2,1)S(1)}, u32[]{:S(2)}, u32[]{:S(2)}) %collective-permute-start.16) | collective-permute-done | bytes 524320 | tf_op jit(solution)/shard_map/ppermute | solution.py:30
  100.8 9.4 %tile.5 = (bf16[2,64,2048]{2,1,0:T(8,128)(2,1)}, bf16[2,64,2048]{2,1,0:T(8,128)(2,1)}, bf16[2,64,2048]{2,1,0:T(8,128)(2,1)}, bf16[2,64,2048]{2,1,0:T(8,128)(2,1)}) custom-call(s32[3]{0:T(128)} %pad_add_fusion.pos_ref, bf16[512,8192]{1,0:T(8,128)(2,1)} %w_ref.6, bf16[4,2,64,512]{3,2,1,0:T(8,128)(2,1)} %get-tuple-element.67.refs_0_, ...), custom_call_target="tpu_custom_call" | custom-call | flops 10350000128 | tf_op jit(solution)/shard_map/tile/pallas_call | solution.py:313
  110.2 3.5 %collective-permute-start.19 = (bf16[2,64,2048]{2,1,0:T(8,128)(2,1)}, bf16[2,64,2048]{2,1,0:T(8,128)(2,1)S(1)}, u32[]{:S(2)}, u32[]{:S(2)}) collective-permute-start(bf16[2,64,2048]{2,1,0:T(8,128)(2,1)} %get-tuple-element.74), channel_id=1, source_target_pairs={{0,2},{1,3},{2,0},{3,1},{4,6},{5,7},{6,4},{7,5},{8,10},{9,11},{10,... | collective-permute-start | bytes 1572872 | tf_op jit(solution)/shard_map/ppermute | solution.py:34
  114.2 9.2 %tile.6 = (bf16[2,64,2048]{2,1,0:T(8,128)(2,1)}, bf16[2,64,2048]{2,1,0:T(8,128)(2,1)}, bf16[2,64,2048]{2,1,0:T(8,128)(2,1)}, bf16[2,64,2048]{2,1,0:T(8,128)(2,1)}) custom-call(s32[3]{0:T(128)} %pad_add_fusion.pos_ref, bf16[512,8192]{1,0:T(8,128)(2,1)} %w_ref.6, bf16[4,2,64,512]{3,2,1,0:T(8,128)(2,1)} %get-tuple-element.52.refs_0_, ...), custom_call_target="tpu_custom_call" | custom-call | flops 10350000128 | tf_op jit(solution)/shard_map/tile/pallas_call | solution.py:313
  124.5 9.2 %tile.7 = (bf16[2,64,2048]{2,1,0:T(8,128)(2,1)}, bf16[2,64,2048]{2,1,0:T(8,128)(2,1)}, bf16[2,64,2048]{2,1,0:T(8,128)(2,1)}, bf16[2,64,2048]{2,1,0:T(8,128)(2,1)}) custom-call(s32[3]{0:T(128)} %pad_add_fusion.pos_ref, bf16[512,8192]{1,0:T(8,128)(2,1)} %w_ref.6, bf16[4,2,64,512]{3,2,1,0:T(8,128)(2,1)} %get-tuple-element.67.refs_0_, ...), custom_call_target="tpu_custom_call" | custom-call | flops 10350000128 | tf_op jit(solution)/shard_map/tile/pallas_call | solution.py:313
  133.7 2.5 %collective-permute-start.26 = (bf16[2,64,2048]{2,1,0:T(8,128)(2,1)}, bf16[2,64,2048]{2,1,0:T(8,128)(2,1)S(1)}, u32[]{:S(2)}, u32[]{:S(2)}) collective-permute-start(bf16[2,64,2048]{2,1,0:T(8,128)(2,1)} %get-tuple-element.85), channel_id=1, source_target_pairs={{0,2},{1,3},{2,0},{3,1},{4,6},{5,7},{6,4},{7,5},{8,10},{9,11},{10,... | collective-permute-start | bytes 1572872 | tf_op jit(solution)/shard_map/ppermute | solution.py:34
  139.0 2.1 %collective-permute-start.29 = (bf16[2,64,2048]{2,1,0:T(8,128)(2,1)S(1)}, bf16[2,64,2048]{2,1,0:T(8,128)(2,1)S(1)}, u32[]{:S(2)}, u32[]{:S(2)}) collective-permute-start(bf16[2,64,2048]{2,1,0:T(8,128)(2,1)S(1)} %copy-done.8), channel_id=1, source_target_pairs={{0,3},{1,0},{2,1},{3,2},{4,7},{5,4},{6,5},{7,6},{8,11},{9,8},{10,9... | collective-permute-start | bytes 1572872 | tf_op jit(solution)/shard_map/ppermute | solution.py:34
  141.5 5.8 %collective-permute-done.26 = bf16[2,64,2048]{2,1,0:T(8,128)(2,1)S(1)} collective-permute-done((bf16[2,64,2048]{2,1,0:T(8,128)(2,1)}, bf16[2,64,2048]{2,1,0:T(8,128)(2,1)S(1)}, u32[]{:S(2)}, u32[]{:S(2)}) %collective-permute-start.26) | collective-permute-done | bytes 524320 | tf_op jit(solution)/shard_map/ppermute | solution.py:34
  147.4 14.4 %collective-permute-done.25 = bf16[2,64,2048]{2,1,0:T(8,128)(2,1)S(1)} collective-permute-done((bf16[2,64,2048]{2,1,0:T(8,128)(2,1)}, bf16[2,64,2048]{2,1,0:T(8,128)(2,1)S(1)}, u32[]{:S(2)}, u32[]{:S(2)}) %collective-permute-start.25) | collective-permute-done | bytes 524320 | tf_op jit(solution)/shard_map/ppermute | solution.py:34
  161.8 2.5 %collective-permute-start.13 = (bf16[64,2048]{1,0:T(8,128)(2,1)S(1)}, bf16[64,2048]{1,0:T(8,128)(2,1)S(1)}, u32[]{:S(2)}, u32[]{:S(2)}) collective-permute-start(bf16[64,2048]{1,0:T(8,128)(2,1)S(1)} %get-tuple-element.97), channel_id=1, source_target_pairs={{0,4},{1,5},{2,6},{3,7},{4,0},{5,1},{6,2},{7,3},{8,12},{9,13},{10,... | collective-permute-start | bytes 786440 | tf_op jit(solution)/shard_map/ppermute | solution.py:38
  166.9 3.0 %collective-permute-done.30 = bf16[2,64,2048]{2,1,0:T(8,128)(2,1)S(1)} collective-permute-done((bf16[2,64,2048]{2,1,0:T(8,128)(2,1)S(1)}, bf16[2,64,2048]{2,1,0:T(8,128)(2,1)S(1)}, u32[]{:S(2)}, u32[]{:S(2)}) %collective-permute-start.30) | collective-permute-done | bytes 524320 | tf_op jit(solution)/shard_map/ppermute | solution.py:34
  171.3 10.6 %collective-permute-done.29 = bf16[2,64,2048]{2,1,0:T(8,128)(2,1)S(1)} collective-permute-done((bf16[2,64,2048]{2,1,0:T(8,128)(2,1)S(1)}, bf16[2,64,2048]{2,1,0:T(8,128)(2,1)S(1)}, u32[]{:S(2)}, u32[]{:S(2)}) %collective-permute-start.29) | collective-permute-done | bytes 524320 | tf_op jit(solution)/shard_map/ppermute | solution.py:34
  181.8 2.7 %collective-permute-done.28 = bf16[2,64,2048]{2,1,0:T(8,128)(2,1)S(1)} collective-permute-done((bf16[2,64,2048]{2,1,0:T(8,128)(2,1)S(1)}, bf16[2,64,2048]{2,1,0:T(8,128)(2,1)S(1)}, u32[]{:S(2)}, u32[]{:S(2)}) %collective-permute-start.28) | collective-permute-done | bytes 524320 | tf_op jit(solution)/shard_map/ppermute | solution.py:34
  186.2 6.2 %collective-permute-done.31.refs_7_ = bf16[64,2048]{1,0:T(8,128)(2,1)S(1)} collective-permute-done((bf16[64,2048]{1,0:T(8,128)(2,1)S(1)}, bf16[64,2048]{1,0:T(8,128)(2,1)S(1)}, u32[]{:S(2)}, u32[]{:S(2)}) %collective-permute-start.31) | collective-permute-done | bytes 262176 | tf_op jit(solution)/shard_map/ppermute | solution.py:38
  192.4 2.1 %place.1 = bf16[128,8192]{1,0:T(8,128)(2,1)} custom-call(s32[3]{0:T(128)S(1)} %copy-done, bf16[64,2048]{1,0:T(8,128)(2,1)S(1)} %get-tuple-element.98.refs_0_, bf16[64,2048]{1,0:T(8,128)(2,1)S(1)} %collective-permute-done.13.refs_1_, bf16[64,2048]{1,0:T(8,128)(2,1)S(1)} %get-tuple-element.96.refs_2_, bf16[64,2048]{1,0:T(8,128)(2,1)S(1)} %collective-permute-done.20.refs_3_, ...), custom_call_target="tpu_custom_call" | custom-call | tf_op jit(solution)/shard_map/place/pallas_call | solution.py:347
  (102 shorter events, 25.1 us)
Async XLA Ops:
  6.5 71.0 %all-gather.5.cloned.1.call-start = ((), (), s32[]{:S(2)}) async-start(), calls=%async_computation | async-start | bytes 7077888 | tf_op jit(solution)/shard_map/all_gather | solution.py:382
  10.5 12.9 %collective-permute-start.7 = (bf16[512,256]{1,0:T(8,128)(2,1)}, bf16[512,256]{1,0:T(8,128)(2,1)S(1)}, u32[]{:S(2)}, u32[]{:S(2)}) collective-permute-start(bf16[512,256]{1,0:T(8,128)(2,1)} %get-tuple-element.48), channel_id=1, source_target_pairs={{0,4},{1,5},{2,6},{3,7},{4,8},{5,9},{6,10},{7,11},{8,12},{9,13},{1... | collective-permute-start | bytes 786440 | tf_op jit(solution)/shard_map/ppermute | solution.py:30
  12.7 10.7 %collective-permute-start.8 = (bf16[512,256]{1,0:T(8,128)(2,1)}, bf16[512,256]{1,0:T(8,128)(2,1)S(1)}, u32[]{:S(2)}, u32[]{:S(2)}) collective-permute-start(bf16[512,256]{1,0:T(8,128)(2,1)} %get-tuple-element.56), channel_id=1, source_target_pairs={{0,12},{1,13},{2,14},{3,15},{4,0},{5,1},{6,2},{7,3},{8,4},{9,5},{1... | collective-permute-start | bytes 786440 | tf_op jit(solution)/shard_map/ppermute | solution.py:30
  14.3 12.8 %collective-permute-start.9 = (bf16[512,256]{1,0:T(8,128)(2,1)}, bf16[512,256]{1,0:T(8,128)(2,1)S(1)}, u32[]{:S(2)}, u32[]{:S(2)}) collective-permute-start(bf16[512,256]{1,0:T(8,128)(2,1)} %get-tuple-element.57), channel_id=1, source_target_pairs={{0,8},{1,9},{2,10},{3,11},{4,12},{5,13},{6,14},{7,15},{8,0},{9,1},... | collective-permute-start | bytes 786440 | tf_op jit(solution)/shard_map/ppermute | solution.py:30
  28.0 86.2 %all-gather.7.cloned.1.call-start = ((), (), s32[]{:S(2)}) async-start(), calls=%async_computation.1 | async-start | bytes 7077888 | tf_op jit(solution)/shard_map/all_gather | solution.py:382
  30.4 11.5 %collective-permute-start.3 = (f32[16,512]{1,0:T(8,128)S(1)}, f32[16,512]{1,0:T(8,128)S(1)}, u32[]{:S(2)}, u32[]{:S(2)}) collective-permute-start(f32[16,512]{1,0:T(8,128)S(1)} %add_select_fusion.1), channel_id=1, source_target_pairs={{0,96},{16,112},{1,97},{17,113},{2,98},{18,114},{3,99},{19,115},{4... | collective-permute-start | bytes 98312 | tf_op jit(solution)/shard_map/ppermute | solution.py:47
  34.7 7.3 %collective-permute-start.1 = (f32[16,512]{1,0:T(8,128)S(1)}, f32[16,512]{1,0:T(8,128)S(1)}, u32[]{:S(2)}, u32[]{:S(2)}) collective-permute-start(f32[16,512]{1,0:T(8,128)S(1)} %add_select_fusion.1), channel_id=1, source_target_pairs={{0,32},{16,48},{32,64},{48,80},{64,96},{80,112},{1,33},{17,49},{33... | collective-permute-start | bytes 98312 | tf_op jit(solution)/shard_map/ppermute | solution.py:47
  39.1 11.3 %collective-permute-start.21 = (bf16[512,256]{1,0:T(8,128)(2,1)S(1)}, bf16[512,256]{1,0:T(8,128)(2,1)S(1)}, u32[]{:S(2)}, u32[]{:S(2)}) collective-permute-start(bf16[512,256]{1,0:T(8,128)(2,1)S(1)} %copy-done.20), channel_id=1, source_target_pairs={{0,4},{1,5},{2,6},{3,7},{4,8},{5,9},{6,10},{7,11},{8,12},{9,13},{1... | collective-permute-start | bytes 786440 | tf_op jit(solution)/shard_map/ppermute | solution.py:30
  40.1 10.4 %collective-permute-start.22 = (bf16[512,256]{1,0:T(8,128)(2,1)S(1)}, bf16[512,256]{1,0:T(8,128)(2,1)S(1)}, u32[]{:S(2)}, u32[]{:S(2)}) collective-permute-start(bf16[512,256]{1,0:T(8,128)(2,1)S(1)} %copy-done.19), channel_id=1, source_target_pairs={{0,12},{1,13},{2,14},{3,15},{4,0},{5,1},{6,2},{7,3},{8,4},{9,5},{1... | collective-permute-start | bytes 786440 | tf_op jit(solution)/shard_map/ppermute | solution.py:30
  41.9 11.1 %collective-permute-start.23 = (bf16[512,256]{1,0:T(8,128)(2,1)S(1)}, bf16[512,256]{1,0:T(8,128)(2,1)S(1)}, u32[]{:S(2)}, u32[]{:S(2)}) collective-permute-start(bf16[512,256]{1,0:T(8,128)(2,1)S(1)} %copy-done.18), channel_id=1, source_target_pairs={{0,8},{1,9},{2,10},{3,11},{4,12},{5,13},{6,14},{7,15},{8,0},{9,1},... | collective-permute-start | bytes 786440 | tf_op jit(solution)/shard_map/ppermute | solution.py:30
  54.0 13.7 %collective-permute-start.4 = (bf16[4,2,64,512]{3,2,1,0:T(8,128)(2,1)S(1)}, bf16[4,2,64,512]{3,2,1,0:T(8,128)(2,1)S(1)}, u32[]{:S(2)}, u32[]{:S(2)}) collective-permute-start(bf16[4,2,64,512]{3,2,1,0:T(8,128)(2,1)S(1)} %copy-done.17), channel_id=1, source_target_pairs={{0,4},{1,5},{2,6},{3,7},{4,8},{5,9},{6,10},{7,11},{8,12},{9,13},{1... | collective-permute-start | bytes 1572872 | tf_op jit(solution)/shard_map/ppermute | solution.py:30
  54.7 14.0 %collective-permute-start.5 = (bf16[4,2,64,512]{3,2,1,0:T(8,128)(2,1)}, bf16[4,2,64,512]{3,2,1,0:T(8,128)(2,1)S(1)}, u32[]{:S(2)}, u32[]{:S(2)}) collective-permute-start(bf16[4,2,64,512]{3,2,1,0:T(8,128)(2,1)} %get-tuple-element.54), channel_id=1, source_target_pairs={{0,12},{1,13},{2,14},{3,15},{4,0},{5,1},{6,2},{7,3},{8,4},{9,5},{1... | collective-permute-start | bytes 1572872 | tf_op jit(solution)/shard_map/ppermute | solution.py:30
  56.7 20.7 %collective-permute-start.6 = (bf16[4,2,64,512]{3,2,1,0:T(8,128)(2,1)}, bf16[4,2,64,512]{3,2,1,0:T(8,128)(2,1)S(1)}, u32[]{:S(2)}, u32[]{:S(2)}) collective-permute-start(bf16[4,2,64,512]{3,2,1,0:T(8,128)(2,1)} %get-tuple-element.55), channel_id=1, source_target_pairs={{0,8},{1,9},{2,10},{3,11},{4,12},{5,13},{6,14},{7,15},{8,0},{9,1},... | collective-permute-start | bytes 1572872 | tf_op jit(solution)/shard_map/ppermute | solution.py:30
  64.5 27.2 %collective-permute-start.14 = (bf16[4,2,64,512]{3,2,1,0:T(8,128)(2,1)}, bf16[4,2,64,512]{3,2,1,0:T(8,128)(2,1)S(1)}, u32[]{:S(2)}, u32[]{:S(2)}) collective-permute-start(bf16[4,2,64,512]{3,2,1,0:T(8,128)(2,1)} %get-tuple-element.68), channel_id=1, source_target_pairs={{0,4},{1,5},{2,6},{3,7},{4,8},{5,9},{6,10},{7,11},{8,12},{9,13},{1... | collective-permute-start | bytes 1572872 | tf_op jit(solution)/shard_map/ppermute | solution.py:30
  65.5 27.5 %collective-permute-start.15 = (bf16[4,2,64,512]{3,2,1,0:T(8,128)(2,1)}, bf16[4,2,64,512]{3,2,1,0:T(8,128)(2,1)S(1)}, u32[]{:S(2)}, u32[]{:S(2)}) collective-permute-start(bf16[4,2,64,512]{3,2,1,0:T(8,128)(2,1)} %get-tuple-element.69), channel_id=1, source_target_pairs={{0,12},{1,13},{2,14},{3,15},{4,0},{5,1},{6,2},{7,3},{8,4},{9,5},{1... | collective-permute-start | bytes 1572872 | tf_op jit(solution)/shard_map/ppermute | solution.py:30
  67.7 32.3 %collective-permute-start.16 = (bf16[4,2,64,512]{3,2,1,0:T(8,128)(2,1)}, bf16[4,2,64,512]{3,2,1,0:T(8,128)(2,1)S(1)}, u32[]{:S(2)}, u32[]{:S(2)}) collective-permute-start(bf16[4,2,64,512]{3,2,1,0:T(8,128)(2,1)} %get-tuple-element.70), channel_id=1, source_target_pairs={{0,8},{1,9},{2,10},{3,11},{4,12},{5,13},{6,14},{7,15},{8,0},{9,1},... | collective-permute-start | bytes 1572872 | tf_op jit(solution)/shard_map/ppermute | solution.py:30
  87.6 35.8 %collective-permute-start.12 = (bf16[2,64,2048]{2,1,0:T(8,128)(2,1)}, bf16[2,64,2048]{2,1,0:T(8,128)(2,1)S(1)}, u32[]{:S(2)}, u32[]{:S(2)}) collective-permute-start(bf16[2,64,2048]{2,1,0:T(8,128)(2,1)} %get-tuple-element.64), channel_id=1, source_target_pairs={{0,2},{1,3},{2,0},{3,1},{4,6},{5,7},{6,4},{7,5},{8,10},{9,11},{10,... | collective-permute-start | bytes 1572872 | tf_op jit(solution)/shard_map/ppermute | solution.py:34
  91.4 42.4 %collective-permute-start.11 = (bf16[2,64,2048]{2,1,0:T(8,128)(2,1)}, bf16[2,64,2048]{2,1,0:T(8,128)(2,1)S(1)}, u32[]{:S(2)}, u32[]{:S(2)}) collective-permute-start(bf16[2,64,2048]{2,1,0:T(8,128)(2,1)} %get-tuple-element.63), channel_id=1, source_target_pairs={{0,3},{1,0},{2,1},{3,2},{4,7},{5,4},{6,5},{7,6},{8,11},{9,8},{10,9... | collective-permute-start | bytes 1572872 | tf_op jit(solution)/shard_map/ppermute | solution.py:34
  91.7 44.6 %collective-permute-start.10 = (bf16[2,64,2048]{2,1,0:T(8,128)(2,1)}, bf16[2,64,2048]{2,1,0:T(8,128)(2,1)S(1)}, u32[]{:S(2)}, u32[]{:S(2)}) collective-permute-start(bf16[2,64,2048]{2,1,0:T(8,128)(2,1)} %get-tuple-element.62), channel_id=1, source_target_pairs={{0,1},{1,2},{2,3},{3,0},{4,5},{5,6},{6,7},{7,4},{8,9},{9,10},{10,1... | collective-permute-start | bytes 1572872 | tf_op jit(solution)/shard_map/ppermute | solution.py:34
  110.2 27.5 %collective-permute-start.19 = (bf16[2,64,2048]{2,1,0:T(8,128)(2,1)}, bf16[2,64,2048]{2,1,0:T(8,128)(2,1)S(1)}, u32[]{:S(2)}, u32[]{:S(2)}) collective-permute-start(bf16[2,64,2048]{2,1,0:T(8,128)(2,1)} %get-tuple-element.74), channel_id=1, source_target_pairs={{0,2},{1,3},{2,0},{3,1},{4,6},{5,7},{6,4},{7,5},{8,10},{9,11},{10,... | collective-permute-start | bytes 1572872 | tf_op jit(solution)/shard_map/ppermute | solution.py:34
  113.7 24.5 %collective-permute-start.18 = (bf16[2,64,2048]{2,1,0:T(8,128)(2,1)}, bf16[2,64,2048]{2,1,0:T(8,128)(2,1)S(1)}, u32[]{:S(2)}, u32[]{:S(2)}) collective-permute-start(bf16[2,64,2048]{2,1,0:T(8,128)(2,1)} %get-tuple-element.73), channel_id=1, source_target_pairs={{0,3},{1,0},{2,1},{3,2},{4,7},{5,4},{6,5},{7,6},{8,11},{9,8},{10,9... | collective-permute-start | bytes 1572872 | tf_op jit(solution)/shard_map/ppermute | solution.py:34
  123.4 15.6 %collective-permute-start.17 = (bf16[2,64,2048]{2,1,0:T(8,128)(2,1)}, bf16[2,64,2048]{2,1,0:T(8,128)(2,1)S(1)}, u32[]{:S(2)}, u32[]{:S(2)}) collective-permute-start(bf16[2,64,2048]{2,1,0:T(8,128)(2,1)} %get-tuple-element.72), channel_id=1, source_target_pairs={{0,1},{1,2},{2,3},{3,0},{4,5},{5,6},{6,7},{7,4},{8,9},{9,10},{10,1... | collective-permute-start | bytes 1572872 | tf_op jit(solution)/shard_map/ppermute | solution.py:34
  133.7 13.6 %collective-permute-start.26 = (bf16[2,64,2048]{2,1,0:T(8,128)(2,1)}, bf16[2,64,2048]{2,1,0:T(8,128)(2,1)S(1)}, u32[]{:S(2)}, u32[]{:S(2)}) collective-permute-start(bf16[2,64,2048]{2,1,0:T(8,128)(2,1)} %get-tuple-element.85), channel_id=1, source_target_pairs={{0,2},{1,3},{2,0},{3,1},{4,6},{5,7},{6,4},{7,5},{8,10},{9,11},{10,... | collective-permute-start | bytes 1572872 | tf_op jit(solution)/shard_map/ppermute | solution.py:34
  136.3 25.5 %collective-permute-start.25 = (bf16[2,64,2048]{2,1,0:T(8,128)(2,1)}, bf16[2,64,2048]{2,1,0:T(8,128)(2,1)S(1)}, u32[]{:S(2)}, u32[]{:S(2)}) collective-permute-start(bf16[2,64,2048]{2,1,0:T(8,128)(2,1)} %get-tuple-element.84), channel_id=1, source_target_pairs={{0,3},{1,0},{2,1},{3,2},{4,7},{5,4},{6,5},{7,6},{8,11},{9,8},{10,9... | collective-permute-start | bytes 1572872 | tf_op jit(solution)/shard_map/ppermute | solution.py:34
  137.7 27.7 %collective-permute-start.24 = (bf16[2,64,2048]{2,1,0:T(8,128)(2,1)S(1)}, bf16[2,64,2048]{2,1,0:T(8,128)(2,1)S(1)}, u32[]{:S(2)}, u32[]{:S(2)}) collective-permute-start(bf16[2,64,2048]{2,1,0:T(8,128)(2,1)S(1)} %copy-done.10), channel_id=1, source_target_pairs={{0,1},{1,2},{2,3},{3,0},{4,5},{5,6},{6,7},{7,4},{8,9},{9,10},{10,1... | collective-permute-start | bytes 1572872 | tf_op jit(solution)/shard_map/ppermute | solution.py:34
  138.2 31.7 %collective-permute-start.30 = (bf16[2,64,2048]{2,1,0:T(8,128)(2,1)S(1)}, bf16[2,64,2048]{2,1,0:T(8,128)(2,1)S(1)}, u32[]{:S(2)}, u32[]{:S(2)}) collective-permute-start(bf16[2,64,2048]{2,1,0:T(8,128)(2,1)S(1)} %copy-done.9), channel_id=1, source_target_pairs={{0,2},{1,3},{2,0},{3,1},{4,6},{5,7},{6,4},{7,5},{8,10},{9,11},{10,... | collective-permute-start | bytes 1572872 | tf_op jit(solution)/shard_map/ppermute | solution.py:34
  139.0 42.8 %collective-permute-start.29 = (bf16[2,64,2048]{2,1,0:T(8,128)(2,1)S(1)}, bf16[2,64,2048]{2,1,0:T(8,128)(2,1)S(1)}, u32[]{:S(2)}, u32[]{:S(2)}) collective-permute-start(bf16[2,64,2048]{2,1,0:T(8,128)(2,1)S(1)} %copy-done.8), channel_id=1, source_target_pairs={{0,3},{1,0},{2,1},{3,2},{4,7},{5,4},{6,5},{7,6},{8,11},{9,8},{10,9... | collective-permute-start | bytes 1572872 | tf_op jit(solution)/shard_map/ppermute | solution.py:34
  147.4 37.1 %collective-permute-start.28 = (bf16[2,64,2048]{2,1,0:T(8,128)(2,1)S(1)}, bf16[2,64,2048]{2,1,0:T(8,128)(2,1)S(1)}, u32[]{:S(2)}, u32[]{:S(2)}) collective-permute-start(bf16[2,64,2048]{2,1,0:T(8,128)(2,1)S(1)} %copy-done.7), channel_id=1, source_target_pairs={{0,1},{1,2},{2,3},{3,0},{4,5},{5,6},{6,7},{7,4},{8,9},{9,10},{10,1... | collective-permute-start | bytes 1572872 | tf_op jit(solution)/shard_map/ppermute | solution.py:34
  161.8 24.4 %collective-permute-start.13 = (bf16[64,2048]{1,0:T(8,128)(2,1)S(1)}, bf16[64,2048]{1,0:T(8,128)(2,1)S(1)}, u32[]{:S(2)}, u32[]{:S(2)}) collective-permute-start(bf16[64,2048]{1,0:T(8,128)(2,1)S(1)} %get-tuple-element.97), channel_id=1, source_target_pairs={{0,4},{1,5},{2,6},{3,7},{4,0},{5,1},{6,2},{7,3},{8,12},{9,13},{10,... | collective-permute-start | bytes 786440 | tf_op jit(solution)/shard_map/ppermute | solution.py:38
  165.5 20.7 %collective-permute-start.20 = (bf16[64,2048]{1,0:T(8,128)(2,1)S(1)}, bf16[64,2048]{1,0:T(8,128)(2,1)S(1)}, u32[]{:S(2)}, u32[]{:S(2)}) collective-permute-start(bf16[64,2048]{1,0:T(8,128)(2,1)S(1)} %get-tuple-element.95), channel_id=1, source_target_pairs={{0,4},{1,5},{2,6},{3,7},{4,0},{5,1},{6,2},{7,3},{8,12},{9,13},{10,... | collective-permute-start | bytes 786440 | tf_op jit(solution)/shard_map/ppermute | solution.py:38
  169.9 16.3 %collective-permute-start.27 = (bf16[64,2048]{1,0:T(8,128)(2,1)S(1)}, bf16[64,2048]{1,0:T(8,128)(2,1)S(1)}, u32[]{:S(2)}, u32[]{:S(2)}) collective-permute-start(bf16[64,2048]{1,0:T(8,128)(2,1)S(1)} %get-tuple-element.93), channel_id=1, source_target_pairs={{0,4},{1,5},{2,6},{3,7},{4,0},{5,1},{6,2},{7,3},{8,12},{9,13},{10,... | collective-permute-start | bytes 786440 | tf_op jit(solution)/shard_map/ppermute | solution.py:38
  184.9 7.5 %collective-permute-start.31 = (bf16[64,2048]{1,0:T(8,128)(2,1)S(1)}, bf16[64,2048]{1,0:T(8,128)(2,1)S(1)}, u32[]{:S(2)}, u32[]{:S(2)}) collective-permute-start(bf16[64,2048]{1,0:T(8,128)(2,1)S(1)} %get-tuple-element.91), channel_id=1, source_target_pairs={{0,4},{1,5},{2,6},{3,7},{4,0},{5,1},{6,2},{7,3},{8,12},{9,13},{10,... | collective-permute-start | bytes 786440 | tf_op jit(solution)/shard_map/ppermute | solution.py:38
  (23 other events, 202.7 us)
Sparse Core Ops, SparseCore 0:
  28.1 42.9 all-gather.4
  72.8 40.9 all-gather.6

commit v5 on v4

--- a/solution.py
+++ b/solution.py
@@ -12,9 +12,9 @@
 LANES = 128
 NX, NCORE, NY, NZ = 4, 2, 4, 4
 STEPS = (1, -1, 2)
-ROW_PARTS = (1, 1)
+ROW_PARTS = (1, 1, 2)
 COL_PARTS = (1, 1)
-TILES = (((0,), (0,)), ((1,), (0,)), ((0,), (1,)), ((1,), (1,)))
+TILES = (((0, 1), (0,)), ((2,), (0,)), ((0, 1), (1,)), ((2,), (1,)))
 OFFLOADED = ()
 HBM = pl.BlockSpec(memory_space=pltpu.HBM)
 SMEM = pl.BlockSpec(memory_space=pltpu.SMEM)
@@ -91,7 +91,7 @@
         spans.append(carry)
     span_ref[...] = jnp.concatenate(spans, axis=0)
 
-def states(k3, v3, rate, unroll=16):
+def states(k3, v3, rate, unroll=32):
     nO,T,C = k3.shape
     W=128
     return pl.pallas_call(
@@ -185,7 +185,7 @@
         out_shape = out_shape + [jax.ShapeDtypeStruct((POLES, nO, C), jnp.float32)]
         out_specs = out_specs + [st]
     res = pl.pallas_call(
-        functools.partial(conv_kernel, unroll=16, per=T, first=first, last=last),
+        functools.partial(conv_kernel, unroll=32, per=T, first=first, last=last),
         grid=(C // W,),
         in_specs=specs,
         out_specs=out_specs,
@@ -381,7 +381,7 @@
         _, *pieces = lax.optimization_barrier((after, *group))
         return lax.all_gather(jnp.concatenate(pieces, axis=0), "seq", axis=0)
 
-    weights = [gathered(fetched[0], span)]
+
     across = jnp.exp(-pole_rate * rows)
     across2 = jnp.exp(-pole_rate * (2.0 * rows))
     across4 = jnp.exp(-pole_rate * (4.0 * rows))
@@ -390,14 +390,16 @@
     behind = from_chip_behind(chip, 1) + across2 * from_chip_behind(chip, 2) + across4 * from_chip_behind(chip, 3)
     incoming = jnp.where(core == 0, behind, across * behind + theirs)
 
+    weights = [gathered(fetched[0], chip)]
+
     mixed = []
     state, start = excl, 0
     for i, tc in enumerate(tcs):
         sent, state = conv_chunk(
             pos, q3, k3, v3, pole_rate, pole_residue, skip_gain, state, incoming if i == 0 else None,
             start // tc, tc, i == len(tcs) - 1)
-        if i + 1 < len(fetched):
-            weights.append(gathered(fetched[i + 1], sent[0]))
+        if i == 1:
+            weights.append(gathered(fetched[1], sent[0]))
         mixed.append([sent[0]] + [over_y(piece, step) for piece, step in zip(sent[1:], STEPS)])
         start += tc
 

time: 202 us -> 202 us (level)
  waiting for transfers between devices: 66.9 us -> 60.3 us
  starting transfers between devices: 48.8 us -> 52.2 us
  Pallas kernels: 65.5 us -> 67.9 us
    ppermute x12 -> x15, waiting for transfers between devices: 22.2 us -> 10.8 us  [over_y(): lax.ppermute(value, 'chan', [(y * NZ + z, (y + step) % NY * NZ + z) for y...]
    ppermute x12 -> x15, starting transfers between devices: 15 us -> 19.3 us  [over_y(): lax.ppermute(value, 'chan', [(y * NZ + z, (y + step) % NY * NZ + z) for y...]
    pallas_call x2 -> x3, Pallas kernels: 15.3 us -> 18.3 us  [conv_chunk(): pl.pallas_call(functools.partial(conv_kernel, unroll=32, per=T, first=fir...]
    all_gather x2, waiting for transfers between devices: 0.01 us -> 2.36 us  [gathered(): return lax.all_gather(jnp.concatenate(pieces, axis=0), 'seq', axis=0)]
    ppermute x12, waiting for transfers between devices: 37.7 us -> 39.8 us  [over_z(): lax.ppermute(value, 'chan', [(y * NZ + z, y * NZ + (z + step) % NZ) for y...]
  transfers between devices with their start and end apart: 34 -> 37, of which waited for: 13 -> 13; matrix products, arithmetic and copies ran while one was open for 2% -> 2% of each run, Pallas kernels for 30% -> 31%
where the time goes in v5:
time: 202 us; the launch traced here: 201 us
  Pallas kernels  67.9 us (34%)
  waiting for transfers between devices  60.3 us (30%)
  starting transfers between devices  52.2 us (26%)
  between operations  13.9 us (7%)
  other arithmetic  5.29 us (3%)
    ppermute x12, waiting for transfers between devices, over_z(): lax.ppermute(value, 'chan', [(y * NZ + z, y * NZ + (z + step) % NZ) for y...  39.8 us
    pallas_call x4, Pallas kernels, tile(): pl.pallas_call(functools.partial(tile_kernel, row_sizes=row_sizes, cols=c...  36.7 us
    ppermute x15, starting transfers between devices, over_y(): lax.ppermute(value, 'chan', [(y * NZ + z, (y + step) % NY * NZ + z) for y...  19.3 us
    pallas_call x3, Pallas kernels, conv_chunk(): pl.pallas_call(functools.partial(conv_kernel, unroll=32, per=T, first=fir...  18.3 us
    ppermute x12, starting transfers between devices, over_z(): lax.ppermute(value, 'chan', [(y * NZ + z, y * NZ + (z + step) % NZ) for y...  18.1 us
    ppermute x15, waiting for transfers between devices, over_y(): lax.ppermute(value, 'chan', [(y * NZ + z, (y + step) % NY * NZ + z) for y...  10.8 us
    ppermute x3, starting transfers between devices, from_chip_behind(): return lax.ppermute(value, 'seq', pairs)  8.59 us
    pallas_call x1, Pallas kernels, states(): pl.pallas_call(functools.partial(state_kernel, T=T, unroll=unroll), grid=...  7.47 us
  transfers between devices with their start and end apart: 37, of which 13 were waited for; matrix products, arithmetic and copies ran while one was open for 2% of the time, Pallas kernels for 31%

profile of v5, /device:TPU:1, one launch (start us, length us, event | category | flops | bytes accessed | tf_op | source)
XLA Modules:
  0.0 201.3 jit_solution(7028088233640058135)
XLA Ops:
  7.2 3.3 %weight_shares.1 = (bf16[512,256]{1,0:T(8,128)(2,1)}, bf16[512,256]{1,0:T(8,128)(2,1)}, bf16[512,256]{1,0:T(8,128)(2,1)}, bf16[512,256]{1,0:T(8,128)(2,1)}, bf16...) custom-call(s32[3]{0:T(128)} %pad_add_fusion.pos_ref, bf16[512,8192]{1,0:T(8,128)(2,1)} %w_ref.6), custom_call_target="tpu_custom_call" | custom-call | tf_op jit(solution)/shard_map/weight_shares/pallas_call | solution.py:226
  10.6 2.2 %collective-permute-start.10 = (bf16[512,256]{1,0:T(8,128)(2,1)}, bf16[512,256]{1,0:T(8,128)(2,1)S(1)}, u32[]{:S(2)}, u32[]{:S(2)}) collective-permute-start(bf16[512,256]{1,0:T(8,128)(2,1)} %get-tuple-element.53), channel_id=1, source_target_pairs={{0,4},{1,5},{2,6},{3,7},{4,8},{5,9},{6,10},{7,11},{8,12},{9,13},{1... | collective-permute-start | bytes 786440 | tf_op jit(solution)/shard_map/ppermute | solution.py:30
  15.8 7.5 %states.1 = (f32[16,16,512]{2,1,0:T(8,128)}, f32[16,512]{1,0:T(8,128)}) custom-call(bf16[16,128,512]{2,1,0:T(8,128)(2,1)} %bitcast.32, bf16[16,128,512]{2,1,0:T(8,128)(2,1)} %bitcast.36, f32[16,512]{1,0:T(8,128)} %rate_ref.7), custom_call_target="tpu_custom_call" | custom-call | flops 9200000000 | tf_op jit(solution)/shard_map/states/pallas_call | solution.py:97
  23.3 1.7 collective-permute-start
  28.1 4.2 %collective-permute-start.3 = (f32[16,512]{1,0:T(8,128)S(1)}, f32[16,512]{1,0:T(8,128)S(1)}, u32[]{:S(2)}, u32[]{:S(2)}) collective-permute-start(f32[16,512]{1,0:T(8,128)S(1)} %add_select_fusion.1), channel_id=1, source_target_pairs={{0,96},{16,112},{1,97},{17,113},{2,98},{18,114},{3,99},{19,115},{4... | collective-permute-start | bytes 98312 | tf_op jit(solution)/shard_map/ppermute | solution.py:47
  33.6 3.1 %collective-permute-start.2 = (f32[16,512]{1,0:T(8,128)S(1)}, f32[16,512]{1,0:T(8,128)S(1)}, u32[]{:S(2)}, u32[]{:S(2)}) collective-permute-start(f32[16,512]{1,0:T(8,128)S(1)} %add_select_fusion.1), channel_id=1, source_target_pairs={{0,64},{16,80},{32,96},{48,112},{1,65},{17,81},{33,97},{49,113},{2... | collective-permute-start | bytes 98312 | tf_op jit(solution)/shard_map/ppermute | solution.py:47
  37.3 2.1 %collective-permute-start.25 = (bf16[512,256]{1,0:T(8,128)(2,1)S(1)}, bf16[512,256]{1,0:T(8,128)(2,1)S(1)}, u32[]{:S(2)}, u32[]{:S(2)}) collective-permute-start(bf16[512,256]{1,0:T(8,128)(2,1)S(1)} %copy-done.14), channel_id=1, source_target_pairs={{0,12},{1,13},{2,14},{3,15},{4,0},{5,1},{6,2},{7,3},{8,4},{9,5},{1... | collective-permute-start | bytes 786440 | tf_op jit(solution)/shard_map/ppermute | solution.py:30
  40.1 5.4 %conv.3 = (bf16[4,2,32,512]{3,2,1,0:T(8,128)(2,1)}, bf16[4,2,32,512]{3,2,1,0:T(8,128)(2,1)}, bf16[4,2,32,512]{3,2,1,0:T(8,128)(2,1)}, bf16[4,2,32,512]{3,2,1,0:T(8,128)(2,1)}, f32[16,16,512]{2,1,0:T(8,128)}) custom-call(s32[3]{0:T(128)} %pad_add_fusion.pos_ref, bf16[16,128,512]{2,1,0:T(8,128)(2,1)} %bitcast.29, bf16[16,128,512]{2,1,0:T(8,128)(2,1)} %bitcast.33, ...), custom_call_target="tpu_custom_call" | custom-call | flops 9200000000 | tf_op jit(solution)/shard_map/conv/pallas_call | solution.py:187
  45.5 5.4 %conv.4 = (bf16[4,2,32,512]{3,2,1,0:T(8,128)(2,1)}, bf16[4,2,32,512]{3,2,1,0:T(8,128)(2,1)}, bf16[4,2,32,512]{3,2,1,0:T(8,128)(2,1)}, bf16[4,2,32,512]{3,2,1,0:T(8,128)(2,1)}, f32[16,16,512]{2,1,0:T(8,128)}) custom-call(s32[3]{0:T(128)} %pad_add_fusion.pos_ref, bf16[16,128,512]{2,1,0:T(8,128)(2,1)} %bitcast.30, bf16[16,128,512]{2,1,0:T(8,128)(2,1)} %bitcast.34, ...), custom_call_target="tpu_custom_call" | custom-call | flops 9200000000 | tf_op jit(solution)/shard_map/conv/pallas_call | solution.py:187
  52.7 2.0 %collective-permute-start.5 = (bf16[4,2,32,512]{3,2,1,0:T(8,128)(2,1)S(1)}, bf16[4,2,32,512]{3,2,1,0:T(8,128)(2,1)S(1)}, u32[]{:S(2)}, u32[]{:S(2)}) collective-permute-start(bf16[4,2,32,512]{3,2,1,0:T(8,128)(2,1)S(1)} %copy-done.25), channel_id=1, source_target_pairs={{0,12},{1,13},{2,14},{3,15},{4,0},{5,1},{6,2},{7,3},{8,4},{9,5},{1... | collective-permute-start | bytes 786440 | tf_op jit(solution)/shard_map/ppermute | solution.py:30
  56.4 2.7 %collective-permute-start.8 = (bf16[4,2,32,512]{3,2,1,0:T(8,128)(2,1)}, bf16[4,2,32,512]{3,2,1,0:T(8,128)(2,1)S(1)}, u32[]{:S(2)}, u32[]{:S(2)}) collective-permute-start(bf16[4,2,32,512]{3,2,1,0:T(8,128)(2,1)} %get-tuple-element.64), channel_id=1, source_target_pairs={{0,12},{1,13},{2,14},{3,15},{4,0},{5,1},{6,2},{7,3},{8,4},{9,5},{1... | collective-permute-start | bytes 786440 | tf_op jit(solution)/shard_map/ppermute | solution.py:30
  60.6 7.5 %conv.5 = (bf16[4,2,64,512]{3,2,1,0:T(8,128)(2,1)}, bf16[4,2,64,512]{3,2,1,0:T(8,128)(2,1)}, bf16[4,2,64,512]{3,2,1,0:T(8,128)(2,1)}, bf16[4,2,64,512]{3,2,1,0:T(8,128)(2,1)}) custom-call(s32[3]{0:T(128)} %pad_add_fusion.pos_ref, bf16[16,128,512]{2,1,0:T(8,128)(2,1)} %bitcast.31, bf16[16,128,512]{2,1,0:T(8,128)(2,1)} %bitcast.35, ...), custom_call_target="tpu_custom_call" | custom-call | flops 9200000000 | tf_op jit(solution)/shard_map/conv/pallas_call | solution.py:187
  68.2 2.6 %collective-permute-start.18 = (bf16[4,2,64,512]{3,2,1,0:T(8,128)(2,1)}, bf16[4,2,64,512]{3,2,1,0:T(8,128)(2,1)S(1)}, u32[]{:S(2)}, u32[]{:S(2)}) collective-permute-start(bf16[4,2,64,512]{3,2,1,0:T(8,128)(2,1)} %get-tuple-element.79), channel_id=1, source_target_pairs={{0,12},{1,13},{2,14},{3,15},{4,0},{5,1},{6,2},{7,3},{8,4},{9,5},{1... | collective-permute-start | bytes 1572872 | tf_op jit(solution)/shard_map/ppermute | solution.py:30
  71.5 3.3 %collective-permute-done.9.refs_7_ = bf16[4,2,32,512]{3,2,1,0:T(8,128)(2,1)S(1)} collective-permute-done((bf16[4,2,32,512]{3,2,1,0:T(8,128)(2,1)S(1)}, bf16[4,2,32,512]{3,2,1,0:T(8,128)(2,1)S(1)}, u32[]{:S(2)}, u32[]{:S(2)}) %collective-permute-start.9) | collective-permute-done | bytes 262176 | tf_op jit(solution)/shard_map/ppermute | solution.py:30
  75.5 9.1 %tile.4 = (bf16[2,64,2048]{2,1,0:T(8,128)(2,1)}, bf16[2,64,2048]{2,1,0:T(8,128)(2,1)}, bf16[2,64,2048]{2,1,0:T(8,128)(2,1)}, bf16[2,64,2048]{2,1,0:T(8,128)(2,1)}) custom-call(s32[3]{0:T(128)} %pad_add_fusion.pos_ref, bf16[512,8192]{1,0:T(8,128)(2,1)} %w_ref.6, bf16[4,2,32,512]{3,2,1,0:T(8,128)(2,1)} %get-tuple-element.57.refs_0_, ...), custom_call_target="tpu_custom_call" | custom-call | flops 10350000128 | tf_op jit(solution)/shard_map/tile/pallas_call | solution.py:313
  84.7 4.0 %collective-permute-start.15 = (bf16[2,64,2048]{2,1,0:T(8,128)(2,1)}, bf16[2,64,2048]{2,1,0:T(8,128)(2,1)S(1)}, u32[]{:S(2)}, u32[]{:S(2)}) collective-permute-start(bf16[2,64,2048]{2,1,0:T(8,128)(2,1)} %get-tuple-element.74), channel_id=1, source_target_pairs={{0,2},{1,3},{2,0},{3,1},{4,6},{5,7},{6,4},{7,5},{8,10},{9,11},{10,... | collective-permute-start | bytes 1572872 | tf_op jit(solution)/shard_map/ppermute | solution.py:34
  90.2 6.7 %collective-permute-done.19.refs_3_ = bf16[4,2,64,512]{3,2,1,0:T(8,128)(2,1)S(1)} collective-permute-done((bf16[4,2,64,512]{3,2,1,0:T(8,128)(2,1)}, bf16[4,2,64,512]{3,2,1,0:T(8,128)(2,1)S(1)}, u32[]{:S(2)}, u32[]{:S(2)}) %collective-permute-start.19) | collective-permute-done | bytes 524320 | tf_op jit(solution)/shard_map/ppermute | solution.py:30
  97.7 9.2 %tile.5 = (bf16[2,64,2048]{2,1,0:T(8,128)(2,1)}, bf16[2,64,2048]{2,1,0:T(8,128)(2,1)}, bf16[2,64,2048]{2,1,0:T(8,128)(2,1)}, bf16[2,64,2048]{2,1,0:T(8,128)(2,1)}) custom-call(s32[3]{0:T(128)} %pad_add_fusion.pos_ref, bf16[512,8192]{1,0:T(8,128)(2,1)} %w_ref.6, bf16[4,2,64,512]{3,2,1,0:T(8,128)(2,1)} %get-tuple-element.77.refs_0_, ...), custom_call_target="tpu_custom_call" | custom-call | flops 10350000128 | tf_op jit(solution)/shard_map/tile/pallas_call | solution.py:313
  106.9 4.1 %collective-permute-start.22 = (bf16[2,64,2048]{2,1,0:T(8,128)(2,1)}, bf16[2,64,2048]{2,1,0:T(8,128)(2,1)S(1)}, u32[]{:S(2)}, u32[]{:S(2)}) collective-permute-start(bf16[2,64,2048]{2,1,0:T(8,128)(2,1)} %get-tuple-element.84), channel_id=1, source_target_pairs={{0,2},{1,3},{2,0},{3,1},{4,6},{5,7},{6,4},{7,5},{8,10},{9,11},{10,... | collective-permute-start | bytes 1572872 | tf_op jit(solution)/shard_map/ppermute | solution.py:34
  111.5 2.4 %all-gather.7.cloned.1.call-done = bf16[12288,256]{1,0:T(8,128)(2,1)} async-done(((bf16[1536,256]{1,0:T(8,128)(2,1)}), bf16[12288,256]{1,0:T(8,128)(2,1)}) %all-gather.7.cloned.1.call-update) | async-done | bytes 6291472 | tf_op jit(solution)/shard_map/all_gather | solution.py:382
  113.8 9.2 %tile.6 = (bf16[2,64,2048]{2,1,0:T(8,128)(2,1)}, bf16[2,64,2048]{2,1,0:T(8,128)(2,1)}, bf16[2,64,2048]{2,1,0:T(8,128)(2,1)}, bf16[2,64,2048]{2,1,0:T(8,128)(2,1)}) custom-call(s32[3]{0:T(128)} %pad_add_fusion.pos_ref, bf16[512,8192]{1,0:T(8,128)(2,1)} %w_ref.6, bf16[4,2,32,512]{3,2,1,0:T(8,128)(2,1)} %get-tuple-element.57.refs_0_, ...), custom_call_target="tpu_custom_call" | custom-call | flops 10350000128 | tf_op jit(solution)/shard_map/tile/pallas_call | solution.py:313
  124.4 9.2 %tile.7 = (bf16[2,64,2048]{2,1,0:T(8,128)(2,1)}, bf16[2,64,2048]{2,1,0:T(8,128)(2,1)}, bf16[2,64,2048]{2,1,0:T(8,128)(2,1)}, bf16[2,64,2048]{2,1,0:T(8,128)(2,1)}) custom-call(s32[3]{0:T(128)} %pad_add_fusion.pos_ref, bf16[512,8192]{1,0:T(8,128)(2,1)} %w_ref.6, bf16[4,2,64,512]{3,2,1,0:T(8,128)(2,1)} %get-tuple-element.77.refs_0_, ...), custom_call_target="tpu_custom_call" | custom-call | flops 10350000128 | tf_op jit(solution)/shard_map/tile/pallas_call | solution.py:313
  133.7 2.7 %collective-permute-start.29 = (bf16[2,64,2048]{2,1,0:T(8,128)(2,1)}, bf16[2,64,2048]{2,1,0:T(8,128)(2,1)S(1)}, u32[]{:S(2)}, u32[]{:S(2)}) collective-permute-start(bf16[2,64,2048]{2,1,0:T(8,128)(2,1)} %get-tuple-element.95), channel_id=1, source_target_pairs={{0,2},{1,3},{2,0},{3,1},{4,6},{5,7},{6,4},{7,5},{8,10},{9,11},{10,... | collective-permute-start | bytes 1572872 | tf_op jit(solution)/shard_map/ppermute | solution.py:34
  141.2 6.1 %collective-permute-done.29 = bf16[2,64,2048]{2,1,0:T(8,128)(2,1)S(1)} collective-permute-done((bf16[2,64,2048]{2,1,0:T(8,128)(2,1)}, bf16[2,64,2048]{2,1,0:T(8,128)(2,1)S(1)}, u32[]{:S(2)}, u32[]{:S(2)}) %collective-permute-start.29) | collective-permute-done | bytes 524320 | tf_op jit(solution)/shard_map/ppermute | solution.py:34
  147.3 16.4 %collective-permute-done.28 = bf16[2,64,2048]{2,1,0:T(8,128)(2,1)S(1)} collective-permute-done((bf16[2,64,2048]{2,1,0:T(8,128)(2,1)}, bf16[2,64,2048]{2,1,0:T(8,128)(2,1)S(1)}, u32[]{:S(2)}, u32[]{:S(2)}) %collective-permute-start.28) | collective-permute-done | bytes 524320 | tf_op jit(solution)/shard_map/ppermute | solution.py:34
  163.7 1.8 collective-permute-done.27
  165.9 3.9 %collective-permute-done.33 = bf16[2,64,2048]{2,1,0:T(8,128)(2,1)S(1)} collective-permute-done((bf16[2,64,2048]{2,1,0:T(8,128)(2,1)S(1)}, bf16[2,64,2048]{2,1,0:T(8,128)(2,1)S(1)}, u32[]{:S(2)}, u32[]{:S(2)}) %collective-permute-start.33) | collective-permute-done | bytes 524320 | tf_op jit(solution)/shard_map/ppermute | solution.py:34
  169.8 3.1 %collective-permute-start.30 = (bf16[64,2048]{1,0:T(8,128)(2,1)S(1)}, bf16[64,2048]{1,0:T(8,128)(2,1)S(1)}, u32[]{:S(2)}, u32[]{:S(2)}) collective-permute-start(bf16[64,2048]{1,0:T(8,128)(2,1)S(1)} %get-tuple-element.103), channel_id=1, source_target_pairs={{0,4},{1,5},{2,6},{3,7},{4,0},{5,1},{6,2},{7,3},{8,12},{9,13},{10,... | collective-permute-start | bytes 786440 | tf_op jit(solution)/shard_map/ppermute | solution.py:38
  172.9 8.3 %collective-permute-done.32 = bf16[2,64,2048]{2,1,0:T(8,128)(2,1)S(1)} collective-permute-done((bf16[2,64,2048]{2,1,0:T(8,128)(2,1)S(1)}, bf16[2,64,2048]{2,1,0:T(8,128)(2,1)S(1)}, u32[]{:S(2)}, u32[]{:S(2)}) %collective-permute-start.32) | collective-permute-done | bytes 524320 | tf_op jit(solution)/shard_map/ppermute | solution.py:34
  181.1 3.4 %collective-permute-done.31 = bf16[2,64,2048]{2,1,0:T(8,128)(2,1)S(1)} collective-permute-done((bf16[2,64,2048]{2,1,0:T(8,128)(2,1)S(1)}, bf16[2,64,2048]{2,1,0:T(8,128)(2,1)S(1)}, u32[]{:S(2)}, u32[]{:S(2)}) %collective-permute-start.31) | collective-permute-done | bytes 524320 | tf_op jit(solution)/shard_map/ppermute | solution.py:34
  186.2 6.2 %collective-permute-done.34.refs_7_ = bf16[64,2048]{1,0:T(8,128)(2,1)S(1)} collective-permute-done((bf16[64,2048]{1,0:T(8,128)(2,1)S(1)}, bf16[64,2048]{1,0:T(8,128)(2,1)S(1)}, u32[]{:S(2)}, u32[]{:S(2)}) %collective-permute-start.34) | collective-permute-done | bytes 262176 | tf_op jit(solution)/shard_map/ppermute | solution.py:38
  192.3 2.1 %place.1 = bf16[128,8192]{1,0:T(8,128)(2,1)} custom-call(s32[3]{0:T(128)S(1)} %copy-done, bf16[64,2048]{1,0:T(8,128)(2,1)S(1)} %get-tuple-element.108.refs_0_, bf16[64,2048]{1,0:T(8,128)(2,1)S(1)} %collective-permute-done.16.refs_1_, bf16[64,2048]{1,0:T(8,128)(2,1)S(1)} %get-tuple-element.106.refs_2_, bf16[64,2048]{1,0:T(8,128)(2,1)S(1)} %collective-permute-done.23.refs_3_, ...), custom_call_target="tpu_custom_call" | custom-call | tf_op jit(solution)/shard_map/place/pallas_call | solution.py:347
  (121 shorter events, 26.7 us)
Async XLA Ops:
  6.5 68.3 %all-gather.5.cloned.1.call-start = ((), (), s32[]{:S(2)}) async-start(), calls=%async_computation | async-start | bytes 7077888 | tf_op jit(solution)/shard_map/all_gather | solution.py:382
  10.6 16.3 %collective-permute-start.10 = (bf16[512,256]{1,0:T(8,128)(2,1)}, bf16[512,256]{1,0:T(8,128)(2,1)S(1)}, u32[]{:S(2)}, u32[]{:S(2)}) collective-permute-start(bf16[512,256]{1,0:T(8,128)(2,1)} %get-tuple-element.53), channel_id=1, source_target_pairs={{0,4},{1,5},{2,6},{3,7},{4,8},{5,9},{6,10},{7,11},{8,12},{9,13},{1... | collective-permute-start | bytes 786440 | tf_op jit(solution)/shard_map/ppermute | solution.py:30
  12.8 14.1 %collective-permute-start.11 = (bf16[512,256]{1,0:T(8,128)(2,1)}, bf16[512,256]{1,0:T(8,128)(2,1)S(1)}, u32[]{:S(2)}, u32[]{:S(2)}) collective-permute-start(bf16[512,256]{1,0:T(8,128)(2,1)} %get-tuple-element.66), channel_id=1, source_target_pairs={{0,12},{1,13},{2,14},{3,15},{4,0},{5,1},{6,2},{7,3},{8,4},{9,5},{1... | collective-permute-start | bytes 786440 | tf_op jit(solution)/shard_map/ppermute | solution.py:30
  14.3 12.8 %collective-permute-start.12 = (bf16[512,256]{1,0:T(8,128)(2,1)}, bf16[512,256]{1,0:T(8,128)(2,1)S(1)}, u32[]{:S(2)}, u32[]{:S(2)}) collective-permute-start(bf16[512,256]{1,0:T(8,128)(2,1)} %get-tuple-element.67), channel_id=1, source_target_pairs={{0,8},{1,9},{2,10},{3,11},{4,12},{5,13},{6,14},{7,15},{8,0},{9,1},... | collective-permute-start | bytes 786440 | tf_op jit(solution)/shard_map/ppermute | solution.py:30
  28.0 85.8 %all-gather.7.cloned.1.call-start = ((), (), s32[]{:S(2)}) async-start(), calls=%async_computation.1 | async-start | bytes 7077888 | tf_op jit(solution)/shard_map/all_gather | solution.py:382
  28.1 11.4 %collective-permute-start.3 = (f32[16,512]{1,0:T(8,128)S(1)}, f32[16,512]{1,0:T(8,128)S(1)}, u32[]{:S(2)}, u32[]{:S(2)}) collective-permute-start(f32[16,512]{1,0:T(8,128)S(1)} %add_select_fusion.1), channel_id=1, source_target_pairs={{0,96},{16,112},{1,97},{17,113},{2,98},{18,114},{3,99},{19,115},{4... | collective-permute-start | bytes 98312 | tf_op jit(solution)/shard_map/ppermute | solution.py:47
  36.7 14.3 %collective-permute-start.24 = (bf16[512,256]{1,0:T(8,128)(2,1)S(1)}, bf16[512,256]{1,0:T(8,128)(2,1)S(1)}, u32[]{:S(2)}, u32[]{:S(2)}) collective-permute-start(bf16[512,256]{1,0:T(8,128)(2,1)S(1)} %copy-done.15), channel_id=1, source_target_pairs={{0,4},{1,5},{2,6},{3,7},{4,8},{5,9},{6,10},{7,11},{8,12},{9,13},{1... | collective-permute-start | bytes 786440 | tf_op jit(solution)/shard_map/ppermute | solution.py:30
  37.3 13.7 %collective-permute-start.25 = (bf16[512,256]{1,0:T(8,128)(2,1)S(1)}, bf16[512,256]{1,0:T(8,128)(2,1)S(1)}, u32[]{:S(2)}, u32[]{:S(2)}) collective-permute-start(bf16[512,256]{1,0:T(8,128)(2,1)S(1)} %copy-done.14), channel_id=1, source_target_pairs={{0,12},{1,13},{2,14},{3,15},{4,0},{5,1},{6,2},{7,3},{8,4},{9,5},{1... | collective-permute-start | bytes 786440 | tf_op jit(solution)/shard_map/ppermute | solution.py:30
  39.4 11.5 %collective-permute-start.26 = (bf16[512,256]{1,0:T(8,128)(2,1)S(1)}, bf16[512,256]{1,0:T(8,128)(2,1)S(1)}, u32[]{:S(2)}, u32[]{:S(2)}) collective-permute-start(bf16[512,256]{1,0:T(8,128)(2,1)S(1)} %copy-done.13), channel_id=1, source_target_pairs={{0,8},{1,9},{2,10},{3,11},{4,12},{5,13},{6,14},{7,15},{8,0},{9,1},... | collective-permute-start | bytes 786440 | tf_op jit(solution)/shard_map/ppermute | solution.py:30
  52.7 15.4 %collective-permute-start.5 = (bf16[4,2,32,512]{3,2,1,0:T(8,128)(2,1)S(1)}, bf16[4,2,32,512]{3,2,1,0:T(8,128)(2,1)S(1)}, u32[]{:S(2)}, u32[]{:S(2)}) collective-permute-start(bf16[4,2,32,512]{3,2,1,0:T(8,128)(2,1)S(1)} %copy-done.25), channel_id=1, source_target_pairs={{0,12},{1,13},{2,14},{3,15},{4,0},{5,1},{6,2},{7,3},{8,4},{9,5},{1... | collective-permute-start | bytes 786440 | tf_op jit(solution)/shard_map/ppermute | solution.py:30
  54.7 13.4 %collective-permute-start.6 = (bf16[4,2,32,512]{3,2,1,0:T(8,128)(2,1)S(1)}, bf16[4,2,32,512]{3,2,1,0:T(8,128)(2,1)S(1)}, u32[]{:S(2)}, u32[]{:S(2)}) collective-permute-start(bf16[4,2,32,512]{3,2,1,0:T(8,128)(2,1)S(1)} %copy-done.24), channel_id=1, source_target_pairs={{0,8},{1,9},{2,10},{3,11},{4,12},{5,13},{6,14},{7,15},{8,0},{9,1},... | collective-permute-start | bytes 786440 | tf_op jit(solution)/shard_map/ppermute | solution.py:30
  56.4 15.1 %collective-permute-start.7 = (bf16[4,2,32,512]{3,2,1,0:T(8,128)(2,1)S(1)}, bf16[4,2,32,512]{3,2,1,0:T(8,128)(2,1)S(1)}, u32[]{:S(2)}, u32[]{:S(2)}) collective-permute-start(bf16[4,2,32,512]{3,2,1,0:T(8,128)(2,1)S(1)} %copy-done.23), channel_id=1, source_target_pairs={{0,4},{1,5},{2,6},{3,7},{4,8},{5,9},{6,10},{7,11},{8,12},{9,13},{1... | collective-permute-start | bytes 786440 | tf_op jit(solution)/shard_map/ppermute | solution.py:30
  56.4 15.1 %collective-permute-start.8 = (bf16[4,2,32,512]{3,2,1,0:T(8,128)(2,1)}, bf16[4,2,32,512]{3,2,1,0:T(8,128)(2,1)S(1)}, u32[]{:S(2)}, u32[]{:S(2)}) collective-permute-start(bf16[4,2,32,512]{3,2,1,0:T(8,128)(2,1)} %get-tuple-element.64), channel_id=1, source_target_pairs={{0,12},{1,13},{2,14},{3,15},{4,0},{5,1},{6,2},{7,3},{8,4},{9,5},{1... | collective-permute-start | bytes 786440 | tf_op jit(solution)/shard_map/ppermute | solution.py:30
  59.1 15.7 %collective-permute-start.9 = (bf16[4,2,32,512]{3,2,1,0:T(8,128)(2,1)S(1)}, bf16[4,2,32,512]{3,2,1,0:T(8,128)(2,1)S(1)}, u32[]{:S(2)}, u32[]{:S(2)}) collective-permute-start(bf16[4,2,32,512]{3,2,1,0:T(8,128)(2,1)S(1)} %copy-done.22), channel_id=1, source_target_pairs={{0,8},{1,9},{2,10},{3,11},{4,12},{5,13},{6,14},{7,15},{8,0},{9,1},... | collective-permute-start | bytes 786440 | tf_op jit(solution)/shard_map/ppermute | solution.py:30
  68.1 21.2 %collective-permute-start.17 = (bf16[4,2,64,512]{3,2,1,0:T(8,128)(2,1)}, bf16[4,2,64,512]{3,2,1,0:T(8,128)(2,1)S(1)}, u32[]{:S(2)}, u32[]{:S(2)}) collective-permute-start(bf16[4,2,64,512]{3,2,1,0:T(8,128)(2,1)} %get-tuple-element.78), channel_id=1, source_target_pairs={{0,4},{1,5},{2,6},{3,7},{4,8},{5,9},{6,10},{7,11},{8,12},{9,13},{1... | collective-permute-start | bytes 1572872 | tf_op jit(solution)/shard_map/ppermute | solution.py:30
  68.2 22.0 %collective-permute-start.18 = (bf16[4,2,64,512]{3,2,1,0:T(8,128)(2,1)}, bf16[4,2,64,512]{3,2,1,0:T(8,128)(2,1)S(1)}, u32[]{:S(2)}, u32[]{:S(2)}) collective-permute-start(bf16[4,2,64,512]{3,2,1,0:T(8,128)(2,1)} %get-tuple-element.79), channel_id=1, source_target_pairs={{0,12},{1,13},{2,14},{3,15},{4,0},{5,1},{6,2},{7,3},{8,4},{9,5},{1... | collective-permute-start | bytes 1572872 | tf_op jit(solution)/shard_map/ppermute | solution.py:30
  71.5 25.3 %collective-permute-start.19 = (bf16[4,2,64,512]{3,2,1,0:T(8,128)(2,1)}, bf16[4,2,64,512]{3,2,1,0:T(8,128)(2,1)S(1)}, u32[]{:S(2)}, u32[]{:S(2)}) collective-permute-start(bf16[4,2,64,512]{3,2,1,0:T(8,128)(2,1)} %get-tuple-element.80), channel_id=1, source_target_pairs={{0,8},{1,9},{2,10},{3,11},{4,12},{5,13},{6,14},{7,15},{8,0},{9,1},... | collective-permute-start | bytes 1572872 | tf_op jit(solution)/shard_map/ppermute | solution.py:30
  84.7 38.4 %collective-permute-start.15 = (bf16[2,64,2048]{2,1,0:T(8,128)(2,1)}, bf16[2,64,2048]{2,1,0:T(8,128)(2,1)S(1)}, u32[]{:S(2)}, u32[]{:S(2)}) collective-permute-start(bf16[2,64,2048]{2,1,0:T(8,128)(2,1)} %get-tuple-element.74), channel_id=1, source_target_pairs={{0,2},{1,3},{2,0},{3,1},{4,6},{5,7},{6,4},{7,5},{8,10},{9,11},{10,... | collective-permute-start | bytes 1572872 | tf_op jit(solution)/shard_map/ppermute | solution.py:34
  88.7 45.0 %collective-permute-start.14 = (bf16[2,64,2048]{2,1,0:T(8,128)(2,1)}, bf16[2,64,2048]{2,1,0:T(8,128)(2,1)S(1)}, u32[]{:S(2)}, u32[]{:S(2)}) collective-permute-start(bf16[2,64,2048]{2,1,0:T(8,128)(2,1)} %get-tuple-element.73), channel_id=1, source_target_pairs={{0,3},{1,0},{2,1},{3,2},{4,7},{5,4},{6,5},{7,6},{8,11},{9,8},{10,9... | collective-permute-start | bytes 1572872 | tf_op jit(solution)/shard_map/ppermute | solution.py:34
  89.3 47.0 %collective-permute-start.13 = (bf16[2,64,2048]{2,1,0:T(8,128)(2,1)}, bf16[2,64,2048]{2,1,0:T(8,128)(2,1)S(1)}, u32[]{:S(2)}, u32[]{:S(2)}) collective-permute-start(bf16[2,64,2048]{2,1,0:T(8,128)(2,1)} %get-tuple-element.72), channel_id=1, source_target_pairs={{0,1},{1,2},{2,3},{3,0},{4,5},{5,6},{6,7},{7,4},{8,9},{9,10},{10,1... | collective-permute-start | bytes 1572872 | tf_op jit(solution)/shard_map/ppermute | solution.py:34
  106.9 30.9 %collective-permute-start.22 = (bf16[2,64,2048]{2,1,0:T(8,128)(2,1)}, bf16[2,64,2048]{2,1,0:T(8,128)(2,1)S(1)}, u32[]{:S(2)}, u32[]{:S(2)}) collective-permute-start(bf16[2,64,2048]{2,1,0:T(8,128)(2,1)} %get-tuple-element.84), channel_id=1, source_target_pairs={{0,2},{1,3},{2,0},{3,1},{4,6},{5,7},{6,4},{7,5},{8,10},{9,11},{10,... | collective-permute-start | bytes 1572872 | tf_op jit(solution)/shard_map/ppermute | solution.py:34
  110.9 27.3 %collective-permute-start.21 = (bf16[2,64,2048]{2,1,0:T(8,128)(2,1)}, bf16[2,64,2048]{2,1,0:T(8,128)(2,1)S(1)}, u32[]{:S(2)}, u32[]{:S(2)}) collective-permute-start(bf16[2,64,2048]{2,1,0:T(8,128)(2,1)} %get-tuple-element.83), channel_id=1, source_target_pairs={{0,3},{1,0},{2,1},{3,2},{4,7},{5,4},{6,5},{7,6},{8,11},{9,8},{10,9... | collective-permute-start | bytes 1572872 | tf_op jit(solution)/shard_map/ppermute | solution.py:34
  123.0 16.0 %collective-permute-start.20 = (bf16[2,64,2048]{2,1,0:T(8,128)(2,1)}, bf16[2,64,2048]{2,1,0:T(8,128)(2,1)S(1)}, u32[]{:S(2)}, u32[]{:S(2)}) collective-permute-start(bf16[2,64,2048]{2,1,0:T(8,128)(2,1)} %get-tuple-element.82), channel_id=1, source_target_pairs={{0,1},{1,2},{2,3},{3,0},{4,5},{5,6},{6,7},{7,4},{8,9},{9,10},{10,1... | collective-permute-start | bytes 1572872 | tf_op jit(solution)/shard_map/ppermute | solution.py:34
  133.7 13.6 %collective-permute-start.29 = (bf16[2,64,2048]{2,1,0:T(8,128)(2,1)}, bf16[2,64,2048]{2,1,0:T(8,128)(2,1)S(1)}, u32[]{:S(2)}, u32[]{:S(2)}) collective-permute-start(bf16[2,64,2048]{2,1,0:T(8,128)(2,1)} %get-tuple-element.95), channel_id=1, source_target_pairs={{0,2},{1,3},{2,0},{3,1},{4,6},{5,7},{6,4},{7,5},{8,10},{9,11},{10,... | collective-permute-start | bytes 1572872 | tf_op jit(solution)/shard_map/ppermute | solution.py:34
  136.3 27.4 %collective-permute-start.28 = (bf16[2,64,2048]{2,1,0:T(8,128)(2,1)}, bf16[2,64,2048]{2,1,0:T(8,128)(2,1)S(1)}, u32[]{:S(2)}, u32[]{:S(2)}) collective-permute-start(bf16[2,64,2048]{2,1,0:T(8,128)(2,1)} %get-tuple-element.94), channel_id=1, source_target_pairs={{0,3},{1,0},{2,1},{3,2},{4,7},{5,4},{6,5},{7,6},{8,11},{9,8},{10,9... | collective-permute-start | bytes 1572872 | tf_op jit(solution)/shard_map/ppermute | solution.py:34
  137.8 27.7 %collective-permute-start.27 = (bf16[2,64,2048]{2,1,0:T(8,128)(2,1)S(1)}, bf16[2,64,2048]{2,1,0:T(8,128)(2,1)S(1)}, u32[]{:S(2)}, u32[]{:S(2)}) collective-permute-start(bf16[2,64,2048]{2,1,0:T(8,128)(2,1)S(1)} %copy-done.9), channel_id=1, source_target_pairs={{0,1},{1,2},{2,3},{3,0},{4,5},{5,6},{6,7},{7,4},{8,9},{9,10},{10,1... | collective-permute-start | bytes 1572872 | tf_op jit(solution)/shard_map/ppermute | solution.py:34
  138.2 31.6 %collective-permute-start.33 = (bf16[2,64,2048]{2,1,0:T(8,128)(2,1)S(1)}, bf16[2,64,2048]{2,1,0:T(8,128)(2,1)S(1)}, u32[]{:S(2)}, u32[]{:S(2)}) collective-permute-start(bf16[2,64,2048]{2,1,0:T(8,128)(2,1)S(1)} %copy-done.10), channel_id=1, source_target_pairs={{0,2},{1,3},{2,0},{3,1},{4,6},{5,7},{6,4},{7,5},{8,10},{9,11},{10,... | collective-permute-start | bytes 1572872 | tf_op jit(solution)/shard_map/ppermute | solution.py:34
  139.1 42.1 %collective-permute-start.32 = (bf16[2,64,2048]{2,1,0:T(8,128)(2,1)S(1)}, bf16[2,64,2048]{2,1,0:T(8,128)(2,1)S(1)}, u32[]{:S(2)}, u32[]{:S(2)}) collective-permute-start(bf16[2,64,2048]{2,1,0:T(8,128)(2,1)S(1)} %copy-done.7), channel_id=1, source_target_pairs={{0,3},{1,0},{2,1},{3,2},{4,7},{5,4},{6,5},{7,6},{8,11},{9,8},{10,9... | collective-permute-start | bytes 1572872 | tf_op jit(solution)/shard_map/ppermute | solution.py:34
  147.3 37.2 %collective-permute-start.31 = (bf16[2,64,2048]{2,1,0:T(8,128)(2,1)S(1)}, bf16[2,64,2048]{2,1,0:T(8,128)(2,1)S(1)}, u32[]{:S(2)}, u32[]{:S(2)}) collective-permute-start(bf16[2,64,2048]{2,1,0:T(8,128)(2,1)S(1)} %copy-done.6), channel_id=1, source_target_pairs={{0,1},{1,2},{2,3},{3,0},{4,5},{5,6},{6,7},{7,4},{8,9},{9,10},{10,1... | collective-permute-start | bytes 1572872 | tf_op jit(solution)/shard_map/ppermute | solution.py:34
  163.7 22.4 %collective-permute-start.16 = (bf16[64,2048]{1,0:T(8,128)(2,1)S(1)}, bf16[64,2048]{1,0:T(8,128)(2,1)S(1)}, u32[]{:S(2)}, u32[]{:S(2)}) collective-permute-start(bf16[64,2048]{1,0:T(8,128)(2,1)S(1)} %get-tuple-element.107), channel_id=1, source_target_pairs={{0,4},{1,5},{2,6},{3,7},{4,0},{5,1},{6,2},{7,3},{8,12},{9,13},{10,... | collective-permute-start | bytes 786440 | tf_op jit(solution)/shard_map/ppermute | solution.py:38
  165.5 20.7 %collective-permute-start.23 = (bf16[64,2048]{1,0:T(8,128)(2,1)S(1)}, bf16[64,2048]{1,0:T(8,128)(2,1)S(1)}, u32[]{:S(2)}, u32[]{:S(2)}) collective-permute-start(bf16[64,2048]{1,0:T(8,128)(2,1)S(1)} %get-tuple-element.105), channel_id=1, source_target_pairs={{0,4},{1,5},{2,6},{3,7},{4,0},{5,1},{6,2},{7,3},{8,12},{9,13},{10,... | collective-permute-start | bytes 786440 | tf_op jit(solution)/shard_map/ppermute | solution.py:38
  169.8 16.4 %collective-permute-start.30 = (bf16[64,2048]{1,0:T(8,128)(2,1)S(1)}, bf16[64,2048]{1,0:T(8,128)(2,1)S(1)}, u32[]{:S(2)}, u32[]{:S(2)}) collective-permute-start(bf16[64,2048]{1,0:T(8,128)(2,1)S(1)} %get-tuple-element.103), channel_id=1, source_target_pairs={{0,4},{1,5},{2,6},{3,7},{4,0},{5,1},{6,2},{7,3},{8,12},{9,13},{10,... | collective-permute-start | bytes 786440 | tf_op jit(solution)/shard_map/ppermute | solution.py:38
  (32 other events, 242.4 us)
Sparse Core Ops, SparseCore 0:
  28.1 42.9 all-gather.4
  72.8 40.9 all-gather.6
